TPU v7x, 128 devices: a whole 4x4x4 slice. The times are simulated.
128 devices in a mesh: img: 16 (over y, x_lo, core), ifg: 8 (over x_hi, z).
Axes of the slice: x: 4 (x_hi: 2, x_lo: 2; x = x_hi * 2 + x_lo), y: 4, z: 4, core: 2. Of those that a mesh axis runs over, the one named last changes fastest.
Arguments:
- phases: bfloat16 [1024, 8, 16384], P('ifg', None, 'img'), may hold values from -15 to 15
- coherence: bfloat16 [1024, 8, 16384], P('ifg', None, 'img'), may hold values from 0.099609375 to 1
- kernel_taps: float32 [3, 5], replicated, may hold values from 0.2 to 1
- inverse: bfloat16 [256, 1024], replicated, may hold values from -0.1875 to 0.1875
- date_pairs: int32 [1024, 2], replicated, may hold values from 0 to 255, as said below
- triplets: int32 [512, 3], replicated, may hold values from 0 to 1023
Outputs:
- displacement: bfloat16 [256, 8, 16384], P(None, None, ('img', 'ifg'))
- closure: bfloat16 [512, 8, 16384], P(None, None, ('img', 'ifg'))
Inputs may be any that keep to these rules, and one draw needn't show every extreme that they name: `date_pairs`: each row holds the earlier date of an interferogram, then a strictly later one.
All inputs are finite; a program needn't handle non-finite values.
Results may differ from a plain program's by a relative error of at most 0.0055.
Values may be sent and summed in bfloat16 or wider, within the bound.
No kernel may reach another device: no remote copies, remote signals or barrier semaphores. Data moves between devices by JAX's collectives and lax.ppermute only.
A program may use at most 64 MiB of HBM per device.

v0:
```python
import jax
import jax.numpy as jnp
from jax import lax
from jax.sharding import PartitionSpec as P


def with_halo(array, sides, width):
    for axis, dim in sides:
        size, length = (lax.axis_size(axis), array.shape[dim])
        up = [(i, (i + 1) % size) for i in range(size - 1)]
        down = [(j, i) for i, j in up]
        last = lax.slice_in_dim(array, length - width, length, axis=dim)
        first = lax.slice_in_dim(array, 0, width, axis=dim)
        before = lax.ppermute(last, axis, up)
        after = lax.ppermute(first, axis, down)
        array = jnp.concatenate([before, array, after], axis=dim)
    return array


def smooth(stacked, kernel_taps):
    values = stacked[0].astype(jnp.float32)
    weights = stacked[1].astype(jnp.float32)
    row_count = values.shape[1]
    col_count = values.shape[2] - kernel_taps.shape[1] + 1
    product = jnp.pad(values * weights, ((0, 0), (1, 1), (0, 0)))
    padded_weights = jnp.pad(weights, ((0, 0), (1, 1), (0, 0)))
    numerator = jnp.zeros((values.shape[0], row_count, col_count), jnp.float32)
    denominator = jnp.zeros((values.shape[0], row_count, col_count), jnp.float32)
    for row_shift in range(kernel_taps.shape[0]):
        for col_shift in range(kernel_taps.shape[1]):
            factor = kernel_taps[row_shift, col_shift]
            numerator = (
                numerator
                + factor
                * product[:, row_shift : row_shift + row_count, col_shift : col_shift + col_count]
            )
            denominator = (
                denominator
                + factor
                * padded_weights[
                    :, row_shift : row_shift + row_count, col_shift : col_shift + col_count
                ]
            )
    return (numerator / denominator).astype(jnp.bfloat16)


def invert_block(block, inverse, date_pairs, triplets):
    count_ifg, rows_here, width_here = block.shape
    flattened = block.reshape(count_ifg, rows_here * width_here)
    displacement = jnp.dot(inverse, flattened, preferred_element_type=jnp.float32).astype(
        jnp.bfloat16
    )
    later = jnp.take(displacement, date_pairs[:, 1], axis=0).astype(jnp.float32)
    earlier = jnp.take(displacement, date_pairs[:, 0], axis=0).astype(jnp.float32)
    misfit = flattened.astype(jnp.float32) - (later - earlier)
    closure = (
        jnp.take(misfit, triplets[:, 0], axis=0)
        + jnp.take(misfit, triplets[:, 1], axis=0)
        - jnp.take(misfit, triplets[:, 2], axis=0)
    )
    return (
        displacement.reshape(-1, rows_here, width_here),
        closure.astype(jnp.bfloat16).reshape(-1, rows_here, width_here),
    )


def per_device(phases, coherence, kernel_taps, inverse, date_pairs, triplets):
    radius = (kernel_taps.shape[1] - 1) // 2
    stacked = jnp.stack([phases, coherence])
    regrouped = lax.all_to_all(stacked, "ifg", split_axis=3, concat_axis=1, tiled=True)
    padded = with_halo(regrouped, ((("img", "ifg"), 3),), radius)
    filtered = smooth(padded, kernel_taps)
    displacement, closure = invert_block(filtered, inverse, date_pairs, triplets)
    return (displacement, closure)


def solution(mesh):
    return jax.shard_map(
        per_device,
        mesh=mesh,
        in_specs=(P("ifg", None, "img"), P("ifg", None, "img"), P(), P(), P(), P()),
        out_specs=(P(None, None, ("img", "ifg")), P(None, None, ("img", "ifg"))),
        check_vma=False,
    )
```

profile of v0, /device:TPU:1, one launch (start us, length us, event | category | flops | bytes accessed | tf_op | source)
XLA Modules:
  0.0 202.3 jit_solution(96826869824282997)
XLA Ops:
  0.6 0.0 copy-start
  0.6 4.6 %pad_maximum_fusion.1 = bf16[2,128,8,1024]{3,2,1,0:T(8,128)(2,1)} fusion(bf16[1,128,8,1024]{3,2,1,0:T(8,128)(2,1)} %bitcast.60, bf16[1,128,8,1024]{3,2,1,0:T(8,128)(2,1)} %bitcast.61), kind=kLoop, calls=%fused_computation.86 | loop fusion | flops 2097152 | bytes 8388608 | tf_op jit(solution)/shard_map/stack | solution.py:69
  5.3 7.3 %copy.19 = bf16[2,128,8,1024]{1,2,0,3:T(8,128)(2,1)} copy(bf16[2,128,8,1024]{3,2,1,0:T(8,128)(2,1)} %pad_maximum_fusion.1) | data formatting | bytes 8388608 | tf_op jit(solution)/shard_map/stack | solution.py:69
  12.6 0.0 copy-start.3
  12.6 8.5 %all-to-all-start = ((bf16[2,128,8,1024]{1,2,0,3:T(8,128)(2,1)}), bf16[2,128,8,1024]{1,2,0,3:T(8,128)(2,1)}, u32[]{:S(2)}, u32[]{:S(2)}) async-start(bf16[2,128,8,1024]{1,2,0,3:T(8,128)(2,1)} %copy.19), calls=%async_computation | async-start | bytes 8388608 | tf_op jit(solution)/shard_map/all_to_all | solution.py:70
  21.0 0.0 copy-done.3
  21.1 0.0 copy-done.1
  21.1 0.7 fusion.64
  21.9 0.0 copy-done.2
  21.9 47.8 %all-to-all-done = bf16[2,128,8,1024]{1,2,0,3:T(8,128)(2,1)} async-done(((bf16[2,128,8,1024]{1,2,0,3:T(8,128)(2,1)}), bf16[2,128,8,1024]{1,2,0,3:T(8,128)(2,1)}, u32[]{:S(2)}, u32[]{:S(2)}) %all-to-all-start) | async-done | bytes 4194336 | tf_op jit(solution)/shard_map/all_to_all | solution.py:70
  69.8 3.4 %copy.35 = bf16[2,8,128,8,128]{2,3,1,4,0:T(8,128)(2,1)S(1)} copy(bf16[2,8,128,8,128]{2,3,0,4,1:T(8,128)(2,1)} %bitcast.4) | data formatting | bytes 8388608 | tf_op jit(solution)/shard_map/all_to_all | solution.py:70
  73.2 6.2 %collective-permute-start.1 = (bf16[2,1024,8,2]{1,2,3,0:T(8,128)(2,1)S(1)}, bf16[2,1024,8,2]{1,2,3,0:T(8,128)(2,1)S(1)}, u32[]{:S(2)}, u32[]{:S(2)}) collective-permute-start(bf16[2,1024,8,2]{1,2,3,0:T(8,128)(2,1)S(1)} %get-tuple-element.11), channel_id=1, source_target_pairs={{1,0},{2,1},{3,2},{4,3},{5,4},{6,5},{7,6},{8,7},{9,8},{10,9},{11,1... | collective-permute-start | bytes 196616 | tf_op jit(solution)/shard_map/ppermute | solution.py:15
  79.4 2.1 %collective-permute-start = (bf16[2,1024,8,2]{1,2,3,0:T(8,128)(2,1)S(1)}, bf16[2,1024,8,2]{1,2,3,0:T(8,128)(2,1)S(1)}, u32[]{:S(2)}, u32[]{:S(2)}) collective-permute-start(bf16[2,1024,8,2]{1,2,3,0:T(8,128)(2,1)S(1)} %get-tuple-element.10), channel_id=1, source_target_pairs={{0,1},{1,2},{2,3},{3,4},{4,5},{5,6},{6,7},{7,8},{8,9},{9,10},{10,1... | collective-permute-start | bytes 196616 | tf_op jit(solution)/shard_map/ppermute | solution.py:14
  81.5 0.0 collective-permute-done.1
  81.5 7.2 %collective-permute-done = bf16[2,1024,8,2]{1,2,3,0:T(8,128)(2,1)S(1)} collective-permute-done((bf16[2,1024,8,2]{1,2,3,0:T(8,128)(2,1)S(1)}, bf16[2,1024,8,2]{1,2,3,0:T(8,128)(2,1)S(1)}, u32[]{:S(2)}, u32[]{:S(2)}) %collective-permute-start) | collective-permute-done | bytes 65568 | tf_op jit(solution)/shard_map/ppermute | solution.py:14
  88.7 0.6 pad_maximum_fusion
  89.3 2.5 %fusion.50 = f32[1024,8,132]{0,1,2:T(8,128)} fusion(bf16[2,1024,8,132]{1,2,3,0:T(8,128)(2,1)S(1)} %pad_maximum_fusion), kind=kLoop, calls=%fused_computation.91 | loop fusion | flops 1081344 | bytes 6488064 | tf_op jit(solution)/shard_map/convert_element_type | solution.py:22
  91.7 3.0 %convert_multiply_fusion = f32[1024,8,132]{0,1,2:T(8,128)} fusion(bf16[2,1024,8,132]{1,2,3,0:T(8,128)(2,1)S(1)} %pad_maximum_fusion), kind=kLoop, calls=%fused_computation.26 | loop fusion | flops 3244032 | bytes 8650752 | tf_op jit(solution)/shard_map/mul | solution.py:25
  94.7 66.3 %fusion.49 = bf16[1024,8,128]{0,1,2:T(8,128)(2,1)S(1)} fusion(f32[1024,8,132]{0,1,2:T(8,128)} %fusion.50, f32[1024,8,132]{0,1,2:T(8,128)} %convert_multiply_fusion, f32[]{:T(128)} %bitcast.21, f32[]{:T(128)} %bitcast.20, f32[]{:T(128)} %bitcast.19, f32[]{:T(128)} %bitcast.18, f32[]{:T(128)} %bitcast.17, f32[]{:T(128)} %bitcast.16, f32[]{:T(128)} %bitcast.15, ...), kind=kLoop, calls=%fused_computation.89 | loop fusion | flops 62914560 | bytes 52698624 | tf_op jit(solution)/shard_map/convert_element_type | solution.py:44
  161.1 3.2 %copy.21 = bf16[1024,8,128]{2,1,0:T(8,128)(2,1)} copy(bf16[1024,8,128]{0,1,2:T(8,128)(2,1)S(1)} %fusion.49) | data formatting | bytes 4194304 | tf_op jit(solution)/shard_map/convert_element_type | solution.py:44
  164.3 0.0 copy-done
  164.3 2.4 %fusion.55 = bf16[1024,256]{1,0:T(8,128)(2,1)S(1)} fusion(bf16[256,1024]{1,0:T(8,128)(2,1)S(1)} %copy-done, bf16[128,8,8,128]{3,2,1,0:T(8,128)(2,1)} %bitcast.56), kind=kOutput, calls=%fused_computation.99 | convolution fusion | flops 537133056 | bytes 3145728 | tf_op jit(solution)/shard_map/dot_general | solution.py:50
  166.7 1.1 copy.24
  167.8 0.2 copy.22
  168.0 4.1 %gather_fusion.1 = bf16[1024,1024]{1,0:T(8,128)(2,1)S(1)} fusion(bf16[256,1024]{1,0:T(8,128)(2,1)S(1)} %copy.22, s32[1024]{0:T(1024)S(1)} %fusion.60), kind=kCustom, calls=%fused_computation.2.clone | custom fusion | bytes 4198400 | tf_op jit(solution)/shard_map/jit(_take)/gather | solution.py:54
  172.1 5.3 %gather_fusion = bf16[1024,1024]{1,0:T(8,128)(2,1)} fusion(bf16[256,1024]{1,0:T(8,128)(2,1)S(1)} %copy.22, s32[1024]{0:T(1024)S(1)} %fusion.59), kind=kCustom, calls=%fused_computation.clone | custom fusion | bytes 4198400 | tf_op jit(solution)/shard_map/jit(_take)/gather | solution.py:53
  177.4 4.2 %subtract_subtract_fusion = f32[1024,1024]{1,0:T(8,128)} fusion(bf16[1024,1024]{1,0:T(8,128)(2,1)S(1)} %gather_fusion.1, bf16[1024,1024]{1,0:T(8,128)(2,1)} %gather_fusion, pred[1024]{0:T(1024)(128)(4,1)S(1)} %get-tuple-element.32, pred[1024]{0:T(1024)(128)(4,1)S(1)} %get-tuple-element.33, bf16[128,8,8,128]{3,2,1,0:T(8,128)(2,1)} %bitcast.57), kind=kLoop, calls=%fused_computation.88 | loop fusion | flops 7340032 | bytes 10487808 | tf_op jit(solution)/shard_map/sub | solution.py:55
  181.6 5.0 %gather_fusion.4 = f32[512,1024]{1,0:T(8,128)S(1)} fusion(f32[1024,1024]{1,0:T(8,128)} %subtract_subtract_fusion, s32[1024]{0:T(1024)S(1)} %pad_clamp_fusion), kind=kCustom, calls=%fused_computation.4.clone | custom fusion | bytes 4196352 | tf_op jit(solution)/shard_map/jit(_take)/gather | solution.py:59
  186.6 5.8 %gather_fusion.3 = f32[512,1024]{1,0:T(8,128)} fusion(f32[1024,1024]{1,0:T(8,128)} %subtract_subtract_fusion, s32[1024]{0:T(1024)S(1)} %pad_clamp_fusion.1), kind=kCustom, calls=%fused_computation.3.clone | custom fusion | bytes 4196352 | tf_op jit(solution)/shard_map/jit(_take)/gather | solution.py:58
  192.4 5.8 %gather_fusion.2 = f32[512,1024]{1,0:T(8,128)} fusion(f32[1024,1024]{1,0:T(8,128)} %subtract_subtract_fusion, s32[1024]{0:T(1024)S(1)} %pad_clamp_fusion.2), kind=kCustom, calls=%fused_computation.1.clone | custom fusion | bytes 4196352 | tf_op jit(solution)/shard_map/jit(_take)/gather | solution.py:57
  198.2 2.8 %fusion.58 = bf16[64,8,8,128]{3,1,2,0:T(8,128)(2,1)S(1)} fusion(f32[512,1024]{1,0:T(8,128)S(1)} %gather_fusion.4, f32[512,1024]{1,0:T(8,128)} %gather_fusion.3, f32[512,1024]{1,0:T(8,128)} %gather_fusion.2, pred[512]{0:T(512)(128)(4,1)S(1)} %get-tuple-element.34, pred[512]{0:T(512)(128)(4,1)S(1)} %get-tuple-element.35, pred[512]{0:T(512)(128)(4,1)S(1)} %compare_and_fusion.4), kind=kLoop, calls=%fused_computation.100 | loop fusion | flops 3145728 | bytes 7341568
  201.0 1.3 copy.26
  (16 shorter events, 0.1 us)
Async XLA Ops:
  0.6 163.7 %copy-start = (bf16[256,1024]{1,0:T(8,128)(2,1)S(1)}, bf16[256,1024]{1,0:T(8,128)(2,1)}, u32[]{:S(2)}) copy-start(bf16[256,1024]{1,0:T(8,128)(2,1)} %param.13) | copy-start | bytes 1572868
  12.6 8.5 %copy-start.3 = (s32[512,3]{0,1:T(4,128)S(1)}, s32[512,3]{0,1:T(4,128)}, u32[]{:S(2)}) copy-start(s32[512,3]{0,1:T(4,128)} %param.15) | copy-start | bytes 18436
  12.6 8.5 %copy-start.1 = (f32[3,5]{1,0:T(4,128)S(1)}, f32[3,5]{1,0:T(4,128)}, u32[]{:S(2)}) copy-start(f32[3,5]{1,0:T(4,128)} %param.12) | copy-start | bytes 184
  12.6 9.3 %copy-start.2 = (s32[1024,2]{0,1:T(2,128)S(1)}, s32[1024,2]{0,1:T(2,128)}, u32[]{:S(2)}) copy-start(s32[1024,2]{0,1:T(2,128)} %param.14) | copy-start | bytes 24580
  12.6 57.2 %all-to-all-start = ((bf16[2,128,8,1024]{1,2,0,3:T(8,128)(2,1)}), bf16[2,128,8,1024]{1,2,0,3:T(8,128)(2,1)}, u32[]{:S(2)}, u32[]{:S(2)}) async-start(bf16[2,128,8,1024]{1,2,0,3:T(8,128)(2,1)} %copy.19), calls=%async_computation | async-start | bytes 8388608 | tf_op jit(solution)/shard_map/all_to_all | solution.py:70
  73.2 8.4 %collective-permute-start.1 = (bf16[2,1024,8,2]{1,2,3,0:T(8,128)(2,1)S(1)}, bf16[2,1024,8,2]{1,2,3,0:T(8,128)(2,1)S(1)}, u32[]{:S(2)}, u32[]{:S(2)}) collective-permute-start(bf16[2,1024,8,2]{1,2,3,0:T(8,128)(2,1)S(1)} %get-tuple-element.11), channel_id=1, source_target_pairs={{1,0},{2,1},{3,2},{4,3},{5,4},{6,5},{7,6},{8,7},{9,8},{10,9},{11,1... | collective-permute-start | bytes 196616 | tf_op jit(solution)/shard_map/ppermute | solution.py:15
  79.4 9.3 %collective-permute-start = (bf16[2,1024,8,2]{1,2,3,0:T(8,128)(2,1)S(1)}, bf16[2,1024,8,2]{1,2,3,0:T(8,128)(2,1)S(1)}, u32[]{:S(2)}, u32[]{:S(2)}) collective-permute-start(bf16[2,1024,8,2]{1,2,3,0:T(8,128)(2,1)S(1)} %get-tuple-element.10), channel_id=1, source_target_pairs={{0,1},{1,2},{2,3},{3,4},{4,5},{5,6},{6,7},{7,8},{8,9},{9,10},{10,1... | collective-permute-start | bytes 196616 | tf_op jit(solution)/shard_map/ppermute | solution.py:14
where the time goes:
time: 203 us; the launch traced here: 202 us
  other arithmetic  84.1 us (41%)
  waiting for transfers between devices  55 us (27%)
  local copies, waits for them, and re-layouts  43.2 us (21%)
  starting transfers between devices  16.8 us (8%)
  matrix products  2.38 us (1%)
    convert_element_type x1, other arithmetic, smooth(): return (numerator / denominator).astype(jnp.bfloat16)  66.3 us
    all_to_all x1, waiting for transfers between devices, per_device(): lax.all_to_all(stacked, 'ifg', split_axis=3, concat_axis=1, tiled=True)  47.8 us
    all_to_all x1, starting transfers between devices, per_device(): lax.all_to_all(stacked, 'ifg', split_axis=3, concat_axis=1, tiled=True)  8.46 us
    another operation x1, local copies, waits for them, and re-layouts, per_device(): stacked = jnp.stack([phases, coherence])  7.28 us
    ppermute x1, waiting for transfers between devices, with_halo(): before = lax.ppermute(last, axis, up)  7.17 us
    ppermute x1, starting transfers between devices, with_halo(): after = lax.ppermute(first, axis, down)  6.22 us
    gather x1, local copies, waits for them, and re-layouts, invert_block(): jnp.take(misfit, triplets[:, 0], axis=0)  5.82 us
    gather x1, local copies, waits for them, and re-layouts, invert_block(): jnp.take(misfit, triplets[:, 1], axis=0)  5.82 us
  transfers between devices with their start and end apart: 3, of which 2 were waited for; matrix products, arithmetic and copies ran while one was open for 0% of the time, Pallas kernels for 0%

commit v1 on v0

v1 whole, which is shorter than its diff:
```python
import functools

import jax
import jax.numpy as jnp
from jax import lax
from jax.experimental import pallas as pl
from jax.experimental.pallas import tpu as pltpu
from jax.sharding import PartitionSpec as P

LANES = 128
F32 = jnp.float32
BF16 = jnp.bfloat16
VMEM = pl.BlockSpec(memory_space=pltpu.VMEM)
SMEM = pl.BlockSpec(memory_space=pltpu.SMEM)
ANY = pl.BlockSpec(memory_space=pl.ANY)
ORDER = (4, 2, 5, 7, 6, 1, 3)
EARLY = (0, 4, 2, 5, 7, 1)
LATE = (6, 3)


def cost(flops, nbytes):
    return pl.CostEstimate(flops=int(flops), bytes_accessed=int(nbytes), transcendentals=0)


def params(mib=48):
    return pltpu.CompilerParams(vmem_limit_bytes=mib * 1024 * 1024)


def pack_kernel(first_phase, last_phase, first_coh, last_coh, left_out, right_out):
    lane = lax.broadcasted_iota(jnp.int32, (4, 8, LANES), 2)
    to_left = jnp.zeros((4, 8, LANES), F32)
    to_right = jnp.zeros((4, 8, LANES), F32)
    for k in range(32):
        a = first_phase[:, k].astype(F32)
        b = first_coh[:, k].astype(F32)
        both = jnp.where(lane < 2, a, pltpu.roll(b, 2, 2))
        here = (lane >> 2) == k
        to_left = jnp.where(here, pltpu.roll(both, 4 * k, 2) if k else both, to_left)
        a = last_phase[:, k].astype(F32)
        b = last_coh[:, k].astype(F32)
        both = jnp.where(lane >= 126, b, pltpu.roll(a, 126, 2))
        shift = (4 * k + 4) % LANES
        to_right = jnp.where(here, pltpu.roll(both, shift, 2) if shift else both, to_right)
    left_out[...] = to_left.astype(BF16)
    right_out[...] = to_right.astype(BF16)


def pack_edges(phases, coherence):
    count, rows, width = phases.shape
    shape = (4, count // 4, rows, width)
    first = pl.BlockSpec((4, count // 4, rows, LANES), lambda i: (0, 0, 0, 0))
    last = pl.BlockSpec((4, count // 4, rows, LANES), lambda i: (0, 0, 0, width // LANES - 1))
    small = jax.ShapeDtypeStruct((4, rows, LANES), BF16)
    phase4 = phases.reshape(shape)
    coh4 = coherence.reshape(shape)
    return pl.pallas_call(
        pack_kernel,
        grid=(1,),
        in_specs=[first, last, first, last],
        out_specs=[pl.BlockSpec((4, rows, LANES), lambda i: (0, 0, 0))] * 2,
        out_shape=[small, small],
        compiler_params=params(),
        cost_estimate=cost(3e8, 2e6),
        name="pack_edges",
    )(phase4, phase4, coh4, coh4)


def filter_kernel(step, me_ref, taps_ref, phase_ref, coh_ref, left_ref, right_ref, out_ref, scratch):
    block = me_ref[0] ^ step
    count = phase_ref.shape[0]
    blocks = phase_ref.shape[2] // LANES
    taps = [[taps_ref[a, b] for b in range(5)] for a in range(3)]
    group = 2
    lane = lax.broadcasted_iota(jnp.int32, (group, 8, LANES), 2)
    row = lax.broadcasted_iota(jnp.int32, (group, 8, LANES), 1)

    def column(index):
        return pl.ds(pl.multiple_of(index * LANES, LANES), LANES)

    def one(i, left_edge, right_edge):
        at = pl.ds(i * group, group)
        centre = column(block)
        phase = phase_ref[at, :, centre].astype(F32)
        coh = coh_ref[at, :, centre].astype(F32)
        if left_edge or right_edge:
            packed = []
            ref = left_ref if left_edge else right_ref
            for j in range(group):
                which = i * group + j
                g = which // 32
                k = which % 32
                vector = ref[pl.ds(g, 1)].astype(F32)
                packed.append(pltpu.roll(vector, (LANES - 4 * k) % LANES, 2))
            packed = jnp.concatenate(packed, axis=0)
        if left_edge:
            phase_before = pltpu.roll(packed, 126, 2)
            coh_before = pltpu.roll(packed, 124, 2)
        else:
            phase_before = phase_ref[at, :, column(jnp.maximum(block - 1, 0))].astype(F32)
            coh_before = coh_ref[at, :, column(jnp.maximum(block - 1, 0))].astype(F32)
        if right_edge:
            phase_after = packed
            coh_after = pltpu.roll(packed, 126, 2)
        else:
            phase_after = phase_ref[at, :, column(jnp.minimum(block + 1, blocks - 1))].astype(F32)
            coh_after = coh_ref[at, :, column(jnp.minimum(block + 1, blocks - 1))].astype(F32)

        def shifted(before, here, after, offset):
            if offset == 0:
                return here
            if offset < 0:
                return pltpu.roll(jnp.where(lane >= LANES + offset, before, here), -offset, 2)
            return pltpu.roll(jnp.where(lane < offset, after, here), LANES - offset, 2)

        num = [None] * 3
        den = [None] * 3
        for b in range(5):
            weight = shifted(coh_before, coh, coh_after, b - 2)
            value = shifted(phase_before, phase, phase_after, b - 2) * weight
            for a in range(3):
                n = value * taps[a][b]
                d = weight * taps[a][b]
                num[a] = n if num[a] is None else num[a] + n
                den[a] = d if den[a] is None else den[a] + d

        def vertical(parts):
            down = jnp.where(row == 0, 0.0, pltpu.roll(parts[0], 1, 1))
            up = jnp.where(row == 7, 0.0, pltpu.roll(parts[2], 7, 1))
            return parts[1] + down + up

        bottom = vertical(den)
        inverse = pl.reciprocal(bottom, approx=True)
        inverse = inverse * (2.0 - bottom * inverse)
        inverse = inverse * (2.0 - bottom * inverse)
        result = vertical(num) * inverse
        scratch[pl.ds(pl.multiple_of(i * group * 8, group * 8), group * 8), :] = result.reshape(group * 8, LANES)

    def run(left_edge, right_edge):
        def body(i, carry):
            one(i, left_edge, right_edge)
            return carry

        lax.fori_loop(0, count // group, body, 0, unroll=2)

    @pl.when(block == 0)
    def _():
        run(True, False)

    @pl.when(block == blocks - 1)
    def _():
        run(False, True)

    @pl.when((block > 0) & (block < blocks - 1))
    def _():
        run(False, False)

    for r in range(8):
        out_ref[:, r * LANES : (r + 1) * LANES] = scratch[pl.ds(r, count, stride=8), :].astype(BF16)


def filter_block(step, me, taps, phases, coherence, left, right):
    count, rows, _ = phases.shape
    return pl.pallas_call(
        functools.partial(filter_kernel, step),
        in_specs=[SMEM, SMEM, VMEM, VMEM, VMEM, VMEM],
        out_specs=VMEM,
        out_shape=jax.ShapeDtypeStruct((count, rows * LANES), BF16),
        scratch_shapes=[pltpu.VMEM((count * rows, LANES), F32)],
        compiler_params=params(),
        cost_estimate=cost(1.5e9, 1e6),
        name="filter",
    )(me, taps, phases, coherence, left, right)


def network_kernel(pairs_ref, triplets_ref, member_ref, dates_ref, first):
    count = pairs_ref.shape[1]
    triplet_count = triplets_ref.shape[1]
    date_count = dates_ref.shape[1]
    pairs = jnp.concatenate([pairs_ref[...], jnp.zeros((6, count), jnp.int32)], axis=0).T
    triplets = jnp.concatenate([triplets_ref[...], jnp.zeros((5, triplet_count), jnp.int32)], axis=0).T
    for at in range(0, count, LANES):
        column = lax.broadcasted_iota(jnp.int32, (LANES, date_count), 1)
        block = pairs[at : at + LANES]
        value = jnp.where(column == block[:, 1:2], 1.0, 0.0) - jnp.where(column == block[:, 0:1], 1.0, 0.0)
        first[at : at + LANES, :] = value.astype(BF16)
    for at in range(0, triplet_count, LANES):
        column = lax.broadcasted_iota(jnp.int32, (LANES, count), 1)
        block = triplets[at : at + LANES]
        value = (
            jnp.where(column == block[:, 0:1], 1.0, 0.0)
            + jnp.where(column == block[:, 1:2], 1.0, 0.0)
            - jnp.where(column == block[:, 2:3], 1.0, 0.0)
        )
        member_ref[at : at + LANES, :] = value.astype(BF16)
    dates_ref[...] = jnp.dot(member_ref[...], first[...], preferred_element_type=F32).astype(BF16)


def network(date_pairs, triplets, dates):
    count = date_pairs.shape[0]
    triplet_count = triplets.shape[0]
    return pl.pallas_call(
        network_kernel,
        in_specs=[VMEM, VMEM],
        out_specs=[VMEM, VMEM],
        out_shape=[
            jax.ShapeDtypeStruct((triplet_count, count), BF16),
            jax.ShapeDtypeStruct((triplet_count, dates), BF16),
        ],
        scratch_shapes=[pltpu.VMEM((count, dates), BF16)],
        compiler_params=params(),
        cost_estimate=cost(2e9, 1e6),
        name="network",
    )(date_pairs.T, triplets.T)


def piece(me, step, matrix_ref, rows, share):
    source = pl.multiple_of((me ^ step) * share, share)
    return matrix_ref[rows, pl.ds(source, share)]


def early_kernel(steps, me_ref, inverse_ref, member_ref, *refs):
    pieces, total_ref = refs[:-1], refs[-1]
    me = me_ref[0]
    share = pieces[0].shape[0]
    dates = inverse_ref.shape[0]
    for at in range(0, total_ref.shape[0], dates):
        matrix_ref, rows = (inverse_ref, pl.ds(0, dates)) if at == 0 else (member_ref, pl.ds(at - dates, dates))
        total = None
        for j in range(0, len(steps), 2):
            left = jnp.concatenate([piece(me, s, matrix_ref, rows, share) for s in steps[j : j + 2]], axis=1)
            right = jnp.concatenate([p[...] for p in pieces[j : j + 2]], axis=0)
            part = jnp.dot(left, right, preferred_element_type=F32)
            total = part if total is None else total + part
        total_ref[pl.ds(at, dates), :] = total


def early_sum(steps, me, inverse, member, pieces):
    rows = inverse.shape[0] + member.shape[0]
    width = pieces[0].shape[1]
    return pl.pallas_call(
        functools.partial(early_kernel, steps),
        in_specs=[SMEM] + [VMEM] * (2 + len(pieces)),
        out_specs=VMEM,
        out_shape=jax.ShapeDtypeStruct((rows, width), F32),
        compiler_params=params(),
        cost_estimate=cost(2e9, 1e6),
        name="early_sum",
    )(me, inverse, member, *pieces)


def late_kernel(steps, me_ref, inverse_ref, member_ref, dates_ref, total_ref, *refs):
    count = len(steps)
    pieces = refs[:count]
    disp_hbm, closure_hbm, disp, closure, rounded, spread, sems = refs[count:]
    me = me_ref[0]
    share = pieces[0].shape[0]
    dates = inverse_ref.shape[0]
    rows = disp.shape[1]
    right = jnp.concatenate([p[...] for p in pieces], axis=0)
    chunk = 128

    def times(matrix_ref, at):
        left = jnp.concatenate([piece(me, s, matrix_ref, pl.ds(at, chunk), share) for s in steps], axis=1)
        return jnp.dot(left, right, preferred_element_type=F32)

    def regroup(slot, value, out, at):
        for r in range(rows):
            spread[slot, pl.ds(r, chunk, stride=rows), :] = value[:, r * LANES : (r + 1) * LANES]
        out[pl.ds(at, chunk)] = spread[slot].reshape(chunk, rows, LANES).astype(BF16)

    copies = []

    def send(out, hbm, at):
        copy = pltpu.make_async_copy(out.at[pl.ds(at, chunk)], hbm.at[pl.ds(at, chunk)], sems.at[len(copies)])
        copy.start()
        copies.append(copy)

    for at in range(0, dates, chunk):
        value = (total_ref[pl.ds(at, chunk), :] + times(inverse_ref, at)).astype(BF16)
        rounded[pl.ds(at, chunk), :] = value
        regroup(len(copies) % 2, value.astype(F32), disp, at)
        send(disp, disp_hbm, at)
    for at in range(0, closure.shape[0], chunk):
        value = total_ref[pl.ds(dates + at, chunk), :] + times(member_ref, at)
        value = value - jnp.dot(dates_ref[pl.ds(at, chunk), :], rounded[...], preferred_element_type=F32)
        regroup(len(copies) % 2, value, closure, at)
        send(closure, closure_hbm, at)
    for copy in copies:
        copy.wait()


def late_sum(steps, me, inverse, member, dates_matrix, total, pieces, rows):
    dates = inverse.shape[0]
    triplet_count = member.shape[0]
    width = pieces[0].shape[1]
    outs = [(dates, rows, LANES), (triplet_count, rows, LANES)]
    return pl.pallas_call(
        functools.partial(late_kernel, steps),
        in_specs=[SMEM] + [VMEM] * (4 + len(pieces)),
        out_specs=[ANY, ANY],
        out_shape=[jax.ShapeDtypeStruct(shape, BF16) for shape in outs],
        scratch_shapes=[
            pltpu.VMEM(outs[0], BF16),
            pltpu.VMEM(outs[1], BF16),
            pltpu.VMEM((dates, width), BF16),
            pltpu.VMEM((2, 128 * rows, LANES), F32),
            pltpu.SemaphoreType.DMA(((dates + triplet_count) // 128,)),
        ],
        compiler_params=params(),
        cost_estimate=cost(3e9, 2e6),
        name="late_sum",
    )(me, inverse, member, dates_matrix, total, *pieces)


def per_device(phases, coherence, kernel_taps, inverse, date_pairs, triplets):
    rows = phases.shape[1]
    size = lax.axis_size("img")
    peers = lax.axis_size("ifg")
    me = lax.axis_index("ifg").astype(jnp.int32).reshape(1)
    to_left, to_right = pack_edges(phases, coherence)
    left = lax.ppermute(to_right, "img", [(i, i + 1) for i in range(size - 1)])
    right = lax.ppermute(to_left, "img", [(i + 1, i) for i in range(size - 1)])
    member, dates_matrix = network(date_pairs, triplets, inverse.shape[0])
    pieces = {}
    for step in ORDER:
        block = filter_block(step, me, kernel_taps, phases, coherence, left, right)
        pieces[step] = lax.ppermute(block, "ifg", [(i, i ^ step) for i in range(peers)])
    pieces[0] = filter_block(0, me, kernel_taps, phases, coherence, left, right)
    total = early_sum(EARLY, me, inverse, member, [pieces[s] for s in EARLY])
    return tuple(late_sum(LATE, me, inverse, member, dates_matrix, total, [pieces[s] for s in LATE], rows))


def solution(mesh):
    return jax.shard_map(
        per_device,
        mesh=mesh,
        in_specs=(P("ifg", None, "img"), P("ifg", None, "img"), P(), P(), P(), P()),
        out_specs=(P(None, None, ("img", "ifg")), P(None, None, ("img", "ifg"))),
        check_vma=False,
    )
```

time: 203 us -> 101 us (0.50)
  the two profiles are of different devices: /device:TPU:1 before, /device:TPU:10 now
where the time goes in v1:
time: 101 us; the launch traced here: 100 us
  Pallas kernels  56.7 us (56%)
  starting transfers between devices  35.9 us (36%)
  local copies, waits for them, and re-layouts  6.68 us (7%)
    pallas_call x8, Pallas kernels, filter_block(): pl.pallas_call(functools.partial(filter_kernel, step), in_specs=[SMEM, SM...  46.9 us
    ppermute x7, starting transfers between devices, per_device(): lax.ppermute(block, 'ifg', [(i, i ^ step) for i in range(peers)])  30.4 us
    unnamed x18, local copies, waits for them, and re-layouts  6.68 us
    ppermute x1, starting transfers between devices, per_device(): right = lax.ppermute(to_left, 'img', [(i + 1, i) for i in range(size - 1)])  3.64 us
    pallas_call x1, Pallas kernels, early_sum(): pl.pallas_call(functools.partial(early_kernel, steps), in_specs=[SMEM] +...  3.09 us
    pallas_call x1, Pallas kernels, pack_edges(): pl.pallas_call(pack_kernel, grid=(1,), in_specs=[first, last, first, last...  2.94 us
    pallas_call x1, Pallas kernels, late_sum(): pl.pallas_call(functools.partial(late_kernel, steps), in_specs=[SMEM] + [...  2.19 us
  transfers between devices with their start and end apart: 9, of which 0 were waited for; matrix products, arithmetic and copies ran while one was open for 0% of the time, Pallas kernels for 47%

profile of v1, /device:TPU:10, one launch (start us, length us, event | category | flops | bytes accessed | tf_op | source)
XLA Modules:
  0.0 100.2 jit_solution(7017288896778918541)
XLA Ops:
  0.6 0.0 copy-start
  0.6 1.6 %copy-done = bf16[128,8,1024]{2,1,0:T(8,128)(2,1)S(1)} copy-done((bf16[128,8,1024]{2,1,0:T(8,128)(2,1)S(1)}, bf16[128,8,1024]{2,1,0:T(8,128)(2,1)}, u32[]{:S(2)}) %copy-start) | copy-done | bytes 2097176
  2.2 1.6 %copy-done.2 = bf16[128,8,1024]{2,1,0:T(8,128)(2,1)S(1)} copy-done((bf16[128,8,1024]{2,1,0:T(8,128)(2,1)S(1)}, bf16[128,8,1024]{2,1,0:T(8,128)(2,1)}, u32[]{:S(2)}) %copy-start.2) | copy-done | bytes 2097176
  3.8 2.9 %pack_edges.1 = (bf16[4,8,128]{2,1,0:T(8,128)(2,1)S(1)}, bf16[4,8,128]{2,1,0:T(8,128)(2,1)S(1)}) custom-call(bf16[4,32,8,1024]{3,2,1,0:T(8,128)(2,1)S(1)} %bitcast.5, bf16[4,32,8,1024]{3,2,1,0:T(8,128)(2,1)S(1)} %bitcast.6, bf16[4,32,8,1024]{3,2,1,0:T(8,128)(2,1)S(1)} %bitcast.7, bf16[4,32,8,1024]{3,2,1,0:T(8,128)(2,1)S(1)} %bitcast.8), custom_call_target="tpu_custom_call" | custom-call | flops 300000000 | bytes 2000000 | tf_op jit(solution)/shard_map/pack_edges/pallas_call | solution.py:56
  6.8 1.9 %collective-permute-start = (bf16[4,8,128]{2,1,0:T(8,128)(2,1)S(1)}, bf16[4,8,128]{2,1,0:T(8,128)(2,1)S(1)}, u32[]{:S(2)}, u32[]{:S(2)}) collective-permute-start(bf16[4,8,128]{2,1,0:T(8,128)(2,1)S(1)} %get-tuple-element.8), channel_id=1, source_target_pairs={{0,8},{8,16},{16,24},{24,32},{32,40},{40,48},{48,56},{56,64},{64,7... | collective-permute-start | bytes 24584 | tf_op jit(solution)/shard_map/ppermute | solution.py:321
  8.7 3.6 %collective-permute-start.1 = (bf16[4,8,128]{2,1,0:T(8,128)(2,1)S(1)}, bf16[4,8,128]{2,1,0:T(8,128)(2,1)S(1)}, u32[]{:S(2)}, u32[]{:S(2)}) collective-permute-start(bf16[4,8,128]{2,1,0:T(8,128)(2,1)S(1)} %get-tuple-element.9), channel_id=1, source_target_pairs={{8,0},{16,8},{24,16},{32,24},{40,32},{48,40},{56,48},{64,56},{72,6... | collective-permute-start | bytes 24584 | tf_op jit(solution)/shard_map/ppermute | solution.py:322
  12.4 0.0 copy-start.1
  12.4 0.0 copy-start.7
  12.4 1.7 %network.1 = (bf16[512,1024]{1,0:T(8,128)(2,1)S(1)}, bf16[512,256]{1,0:T(8,128)(2,1)S(1)}) custom-call(s32[2,1024]{1,0:T(2,128)S(1)} %bitcast.9, s32[3,512]{1,0:T(4,128)S(1)} %bitcast.10), custom_call_target="tpu_custom_call" | custom-call | flops 2000000000 | bytes 1000000 | tf_op jit(solution)/shard_map/network/pallas_call | solution.py:201
  14.1 0.0 copy-start.3
  14.1 1.6 %copy-done.3 = bf16[128,8,1024]{2,1,0:T(8,128)(2,1)S(1)} copy-done((bf16[128,8,1024]{2,1,0:T(8,128)(2,1)S(1)}, bf16[128,8,1024]{2,1,0:T(8,128)(2,1)}, u32[]{:S(2)}) %copy-start.3) | copy-done | bytes 2097176
  15.7 4.6 %filter.9 = bf16[128,1024]{1,0:T(8,128)(2,1)S(1)} custom-call(s32[1]{0:T(128)} %bitcast.me_ref, f32[3,5]{1,0:T(4,128)S(1)} %copy-done.7, bf16[128,8,1024]{2,1,0:T(8,128)(2,1)S(1)} %copy-done.1, bf16[128,8,1024]{2,1,0:T(8,128)(2,1)S(1)} %copy-done.3, bf16[4,8,128]{2,1,0:T(8,128)(2,1)S(1)} %collective-permute-done.left_ref, ...), custom_call_target="tpu_custom_call" | custom-call | flops 1500000000 | bytes 1000000 | tf_op jit(solution)/shard_map/filter/pallas_call | solution.py:163
  20.3 7.3 %collective-permute-start.2 = (bf16[128,1024]{1,0:T(8,128)(2,1)S(1)}, bf16[128,1024]{1,0:T(8,128)(2,1)S(1)}, u32[]{:S(2)}, u32[]{:S(2)}) collective-permute-start(bf16[128,1024]{1,0:T(8,128)(2,1)S(1)} %filter.9), channel_id=1, source_target_pairs={{0,4},{1,5},{2,6},{3,7},{4,0},{5,1},{6,2},{7,3},{8,12},{9,13},{10,... | collective-permute-start | bytes 786440 | tf_op jit(solution)/shard_map/ppermute | solution.py:327
  27.6 4.6 %filter.10 = bf16[128,1024]{1,0:T(8,128)(2,1)S(1)} custom-call(s32[1]{0:T(128)} %bitcast.me_ref, f32[3,5]{1,0:T(4,128)S(1)} %copy-done.7, bf16[128,8,1024]{2,1,0:T(8,128)(2,1)S(1)} %copy-done.1, bf16[128,8,1024]{2,1,0:T(8,128)(2,1)S(1)} %copy-done.3, bf16[4,8,128]{2,1,0:T(8,128)(2,1)S(1)} %collective-permute-done.left_ref, ...), custom_call_target="tpu_custom_call" | custom-call | flops 1500000000 | bytes 1000000 | tf_op jit(solution)/shard_map/filter/pallas_call | solution.py:163
  32.3 4.0 %collective-permute-start.3 = (bf16[128,1024]{1,0:T(8,128)(2,1)S(1)}, bf16[128,1024]{1,0:T(8,128)(2,1)S(1)}, u32[]{:S(2)}, u32[]{:S(2)}) collective-permute-start(bf16[128,1024]{1,0:T(8,128)(2,1)S(1)} %filter.10), channel_id=1, source_target_pairs={{0,2},{1,3},{2,0},{3,1},{4,6},{5,7},{6,4},{7,5},{8,10},{9,11},{10,... | collective-permute-start | bytes 786440 | tf_op jit(solution)/shard_map/ppermute | solution.py:327
  36.2 4.6 %filter.11 = bf16[128,1024]{1,0:T(8,128)(2,1)S(1)} custom-call(s32[1]{0:T(128)} %bitcast.me_ref, f32[3,5]{1,0:T(4,128)S(1)} %copy-done.7, bf16[128,8,1024]{2,1,0:T(8,128)(2,1)S(1)} %copy-done.1, bf16[128,8,1024]{2,1,0:T(8,128)(2,1)S(1)} %copy-done.3, bf16[4,8,128]{2,1,0:T(8,128)(2,1)S(1)} %collective-permute-done.left_ref, ...), custom_call_target="tpu_custom_call" | custom-call | flops 1500000000 | bytes 1000000 | tf_op jit(solution)/shard_map/filter/pallas_call | solution.py:163
  40.9 6.7 %collective-permute-start.4 = (bf16[128,1024]{1,0:T(8,128)(2,1)S(1)}, bf16[128,1024]{1,0:T(8,128)(2,1)S(1)}, u32[]{:S(2)}, u32[]{:S(2)}) collective-permute-start(bf16[128,1024]{1,0:T(8,128)(2,1)S(1)} %filter.11), channel_id=1, source_target_pairs={{0,5},{1,4},{2,7},{3,6},{4,1},{5,0},{6,3},{7,2},{8,13},{9,12},{10,... | collective-permute-start | bytes 786440 | tf_op jit(solution)/shard_map/ppermute | solution.py:327
  47.5 9.4 %filter.12 = bf16[128,1024]{1,0:T(8,128)(2,1)S(1)} custom-call(s32[1]{0:T(128)} %bitcast.me_ref, f32[3,5]{1,0:T(4,128)S(1)} %copy-done.7, bf16[128,8,1024]{2,1,0:T(8,128)(2,1)S(1)} %copy-done.1, bf16[128,8,1024]{2,1,0:T(8,128)(2,1)S(1)} %copy-done.3, bf16[4,8,128]{2,1,0:T(8,128)(2,1)S(1)} %collective-permute-done.left_ref, ...), custom_call_target="tpu_custom_call" | custom-call | flops 1500000000 | bytes 1000000 | tf_op jit(solution)/shard_map/filter/pallas_call | solution.py:163
  56.9 1.6 %collective-permute-start.5 = (bf16[128,1024]{1,0:T(8,128)(2,1)S(1)}, bf16[128,1024]{1,0:T(8,128)(2,1)S(1)}, u32[]{:S(2)}, u32[]{:S(2)}) collective-permute-start(bf16[128,1024]{1,0:T(8,128)(2,1)S(1)} %filter.12), channel_id=1, source_target_pairs={{0,7},{1,6},{2,5},{3,4},{4,3},{5,2},{6,1},{7,0},{8,15},{9,14},{10,... | collective-permute-start | bytes 786440 | tf_op jit(solution)/shard_map/ppermute | solution.py:327
  58.5 4.6 %filter.13 = bf16[128,1024]{1,0:T(8,128)(2,1)S(1)} custom-call(s32[1]{0:T(128)} %bitcast.me_ref, f32[3,5]{1,0:T(4,128)S(1)} %copy-done.7, bf16[128,8,1024]{2,1,0:T(8,128)(2,1)S(1)} %copy-done.1, bf16[128,8,1024]{2,1,0:T(8,128)(2,1)S(1)} %copy-done.3, bf16[4,8,128]{2,1,0:T(8,128)(2,1)S(1)} %collective-permute-done.left_ref, ...), custom_call_target="tpu_custom_call" | custom-call | flops 1500000000 | bytes 1000000 | tf_op jit(solution)/shard_map/filter/pallas_call | solution.py:163
  63.1 0.1 collective-permute-start.6
  63.2 4.6 %filter.15 = bf16[128,1024]{1,0:T(8,128)(2,1)S(1)} custom-call(s32[1]{0:T(128)} %bitcast.me_ref, f32[3,5]{1,0:T(4,128)S(1)} %copy-done.7, bf16[128,8,1024]{2,1,0:T(8,128)(2,1)S(1)} %copy-done.1, bf16[128,8,1024]{2,1,0:T(8,128)(2,1)S(1)} %copy-done.3, bf16[4,8,128]{2,1,0:T(8,128)(2,1)S(1)} %collective-permute-done.left_ref, ...), custom_call_target="tpu_custom_call" | custom-call | flops 1500000000 | bytes 1000000 | tf_op jit(solution)/shard_map/filter/pallas_call | solution.py:163
  67.8 4.6 %filter.14 = bf16[128,1024]{1,0:T(8,128)(2,1)S(1)} custom-call(s32[1]{0:T(128)} %bitcast.me_ref, f32[3,5]{1,0:T(4,128)S(1)} %copy-done.7, bf16[128,8,1024]{2,1,0:T(8,128)(2,1)S(1)} %copy-done.1, bf16[128,8,1024]{2,1,0:T(8,128)(2,1)S(1)} %copy-done.3, bf16[4,8,128]{2,1,0:T(8,128)(2,1)S(1)} %collective-permute-done.left_ref, ...), custom_call_target="tpu_custom_call" | custom-call | flops 1500000000 | bytes 1000000 | tf_op jit(solution)/shard_map/filter/pallas_call | solution.py:163
  72.5 0.0 copy-start.4
  72.5 10.8 %collective-permute-start.7 = (bf16[128,1024]{1,0:T(8,128)(2,1)S(1)}, bf16[128,1024]{1,0:T(8,128)(2,1)S(1)}, u32[]{:S(2)}, u32[]{:S(2)}) collective-permute-start(bf16[128,1024]{1,0:T(8,128)(2,1)S(1)} %filter.14), channel_id=1, source_target_pairs={{0,6},{1,7},{2,4},{3,5},{4,2},{5,3},{6,0},{7,1},{8,14},{9,15},{10,... | collective-permute-start | bytes 786440 | tf_op jit(solution)/shard_map/ppermute | solution.py:327
  83.3 9.7 %filter.8.refs_0_ = bf16[128,1024]{1,0:T(8,128)(2,1)S(1)} custom-call(s32[1]{0:T(128)} %bitcast.me_ref, f32[3,5]{1,0:T(4,128)S(1)} %copy-done.7, bf16[128,8,1024]{2,1,0:T(8,128)(2,1)S(1)} %copy-done.1, bf16[128,8,1024]{2,1,0:T(8,128)(2,1)S(1)} %copy-done.3, bf16[4,8,128]{2,1,0:T(8,128)(2,1)S(1)} %collective-permute-done.left_ref, ...), custom_call_target="tpu_custom_call" | custom-call | flops 1500000000 | bytes 1000000 | tf_op jit(solution)/shard_map/filter/pallas_call | solution.py:163
  93.0 0.0 collective-permute-done.4.refs_3_
  93.0 0.0 collective-permute-done.5.refs_4_
  93.1 3.1 %early_sum.1.total_ref = f32[768,1024]{1,0:T(8,128)} custom-call(s32[1]{0:T(128)} %bitcast.me_ref, bf16[256,1024]{1,0:T(8,128)(2,1)S(1)} %copy-done.4, bf16[512,1024]{1,0:T(8,128)(2,1)S(1)} %get-tuple-element.6.member_ref, bf16[128,1024]{1,0:T(8,128)(2,1)S(1)} %filter.8.refs_0_, bf16[128,1024]{1,0:T(8,128)(2,1)S(1)} %collective-permute-done.2.refs_1_, ...), custom_call_target="tpu_custom_call" | custom-call | flops 2000000000 | bytes 1000000 | tf_op jit(solution)/shard_map/early_sum/pallas_call | solution.py:240
  96.2 0.0 collective-permute-done.7.refs_0_
  96.2 1.9 %copy-done.8 = f32[768,1024]{1,0:T(8,128)S(1)} copy-done((f32[768,1024]{1,0:T(8,128)S(1)}, f32[768,1024]{1,0:T(8,128)}, u32[]{:S(2)}) %copy-start.8) | copy-done | bytes 3145752
  98.1 2.2 %late_sum.1 = (bf16[256,8,128]{2,1,0:T(8,128)(2,1)}, bf16[512,8,128]{2,1,0:T(8,128)(2,1)}) custom-call(s32[1]{0:T(128)} %bitcast.me_ref, bf16[256,1024]{1,0:T(8,128)(2,1)S(1)} %copy-done.4, bf16[512,1024]{1,0:T(8,128)(2,1)S(1)} %get-tuple-element.6.member_ref, bf16[512,256]{1,0:T(8,128)(2,1)S(1)} %get-tuple-element.7.dates_ref, f32[768,1024]{1,0:T(8,128)S(1)} %copy-done.8, ...), custom_call_target="tpu_custom_call" | custom-call | flops 3000000000 | bytes 2000000 | tf_op jit(solution)/shard_map/late_sum/pallas_call | solution.py:297
  (16 shorter events, 0.0 us)
Async XLA Ops:
  0.6 1.6 %copy-start = (bf16[128,8,1024]{2,1,0:T(8,128)(2,1)S(1)}, bf16[128,8,1024]{2,1,0:T(8,128)(2,1)}, u32[]{:S(2)}) copy-start(bf16[128,8,1024]{2,1,0:T(8,128)(2,1)} %phase_ref.15) | copy-start | bytes 6291460
  2.2 1.6 %copy-start.2 = (bf16[128,8,1024]{2,1,0:T(8,128)(2,1)S(1)}, bf16[128,8,1024]{2,1,0:T(8,128)(2,1)}, u32[]{:S(2)}) copy-start(bf16[128,8,1024]{2,1,0:T(8,128)(2,1)} %coh_ref.15) | copy-start | bytes 6291460
  3.8 8.5 %copy-start.5 = (s32[1024,2]{0,1:T(2,128)S(1)}, s32[1024,2]{0,1:T(2,128)}, u32[]{:S(2)}) copy-start(s32[1024,2]{0,1:T(2,128)} %param.10) | copy-start | bytes 24580
  3.8 8.5 %copy-start.6 = (s32[512,3]{0,1:T(4,128)S(1)}, s32[512,3]{0,1:T(4,128)}, u32[]{:S(2)}) copy-start(s32[512,3]{0,1:T(4,128)} %param.11) | copy-start | bytes 18436
  6.8 7.3 %collective-permute-start = (bf16[4,8,128]{2,1,0:T(8,128)(2,1)S(1)}, bf16[4,8,128]{2,1,0:T(8,128)(2,1)S(1)}, u32[]{:S(2)}, u32[]{:S(2)}) collective-permute-start(bf16[4,8,128]{2,1,0:T(8,128)(2,1)S(1)} %get-tuple-element.8), channel_id=1, source_target_pairs={{0,8},{8,16},{16,24},{24,32},{32,40},{40,48},{48,56},{56,64},{64,7... | collective-permute-start | bytes 24584 | tf_op jit(solution)/shard_map/ppermute | solution.py:321
  8.7 5.4 %collective-permute-start.1 = (bf16[4,8,128]{2,1,0:T(8,128)(2,1)S(1)}, bf16[4,8,128]{2,1,0:T(8,128)(2,1)S(1)}, u32[]{:S(2)}, u32[]{:S(2)}) collective-permute-start(bf16[4,8,128]{2,1,0:T(8,128)(2,1)S(1)} %get-tuple-element.9), channel_id=1, source_target_pairs={{8,0},{16,8},{24,16},{32,24},{40,32},{48,40},{56,48},{64,56},{72,6... | collective-permute-start | bytes 24584 | tf_op jit(solution)/shard_map/ppermute | solution.py:322
  12.4 1.7 %copy-start.1 = (bf16[128,8,1024]{2,1,0:T(8,128)(2,1)S(1)}, bf16[128,8,1024]{2,1,0:T(8,128)(2,1)}, u32[]{:S(2)}) copy-start(bf16[128,8,1024]{2,1,0:T(8,128)(2,1)} %phase_ref.15) | copy-start | bytes 6291460
  12.4 1.7 %copy-start.7 = (f32[3,5]{1,0:T(4,128)S(1)}, f32[3,5]{1,0:T(4,128)}, u32[]{:S(2)}) copy-start(f32[3,5]{1,0:T(4,128)} %taps_ref.15) | copy-start | bytes 184
  14.1 1.6 %copy-start.3 = (bf16[128,8,1024]{2,1,0:T(8,128)(2,1)S(1)}, bf16[128,8,1024]{2,1,0:T(8,128)(2,1)}, u32[]{:S(2)}) copy-start(bf16[128,8,1024]{2,1,0:T(8,128)(2,1)} %coh_ref.15) | copy-start | bytes 6291460
  20.3 52.2 %collective-permute-start.2 = (bf16[128,1024]{1,0:T(8,128)(2,1)S(1)}, bf16[128,1024]{1,0:T(8,128)(2,1)S(1)}, u32[]{:S(2)}, u32[]{:S(2)}) collective-permute-start(bf16[128,1024]{1,0:T(8,128)(2,1)S(1)} %filter.9), channel_id=1, source_target_pairs={{0,4},{1,5},{2,6},{3,7},{4,0},{5,1},{6,2},{7,3},{8,12},{9,13},{10,... | collective-permute-start | bytes 786440 | tf_op jit(solution)/shard_map/ppermute | solution.py:327
  32.3 51.0 %collective-permute-start.3 = (bf16[128,1024]{1,0:T(8,128)(2,1)S(1)}, bf16[128,1024]{1,0:T(8,128)(2,1)S(1)}, u32[]{:S(2)}, u32[]{:S(2)}) collective-permute-start(bf16[128,1024]{1,0:T(8,128)(2,1)S(1)} %filter.10), channel_id=1, source_target_pairs={{0,2},{1,3},{2,0},{3,1},{4,6},{5,7},{6,4},{7,5},{8,10},{9,11},{10,... | collective-permute-start | bytes 786440 | tf_op jit(solution)/shard_map/ppermute | solution.py:327
  40.9 52.2 %collective-permute-start.4 = (bf16[128,1024]{1,0:T(8,128)(2,1)S(1)}, bf16[128,1024]{1,0:T(8,128)(2,1)S(1)}, u32[]{:S(2)}, u32[]{:S(2)}) collective-permute-start(bf16[128,1024]{1,0:T(8,128)(2,1)S(1)} %filter.11), channel_id=1, source_target_pairs={{0,5},{1,4},{2,7},{3,6},{4,1},{5,0},{6,3},{7,2},{8,13},{9,12},{10,... | collective-permute-start | bytes 786440 | tf_op jit(solution)/shard_map/ppermute | solution.py:327
  56.9 36.1 %collective-permute-start.5 = (bf16[128,1024]{1,0:T(8,128)(2,1)S(1)}, bf16[128,1024]{1,0:T(8,128)(2,1)S(1)}, u32[]{:S(2)}, u32[]{:S(2)}) collective-permute-start(bf16[128,1024]{1,0:T(8,128)(2,1)S(1)} %filter.12), channel_id=1, source_target_pairs={{0,7},{1,6},{2,5},{3,4},{4,3},{5,2},{6,1},{7,0},{8,15},{9,14},{10,... | collective-permute-start | bytes 786440 | tf_op jit(solution)/shard_map/ppermute | solution.py:327
  63.1 29.9 %collective-permute-start.6 = (bf16[128,1024]{1,0:T(8,128)(2,1)S(1)}, bf16[128,1024]{1,0:T(8,128)(2,1)S(1)}, u32[]{:S(2)}, u32[]{:S(2)}) collective-permute-start(bf16[128,1024]{1,0:T(8,128)(2,1)S(1)} %filter.13), channel_id=1, source_target_pairs={{0,1},{1,0},{2,3},{3,2},{4,5},{5,4},{6,7},{7,6},{8,9},{9,8},{10,11... | collective-permute-start | bytes 786440 | tf_op jit(solution)/shard_map/ppermute | solution.py:327
  72.5 20.6 %copy-start.4 = (bf16[256,1024]{1,0:T(8,128)(2,1)S(1)}, bf16[256,1024]{1,0:T(8,128)(2,1)}, u32[]{:S(2)}) copy-start(bf16[256,1024]{1,0:T(8,128)(2,1)} %inverse_ref.3) | copy-start | bytes 1572868
  72.5 23.7 %collective-permute-start.7 = (bf16[128,1024]{1,0:T(8,128)(2,1)S(1)}, bf16[128,1024]{1,0:T(8,128)(2,1)S(1)}, u32[]{:S(2)}, u32[]{:S(2)}) collective-permute-start(bf16[128,1024]{1,0:T(8,128)(2,1)S(1)} %filter.14), channel_id=1, source_target_pairs={{0,6},{1,7},{2,4},{3,5},{4,2},{5,3},{6,0},{7,1},{8,14},{9,15},{10,... | collective-permute-start | bytes 786440 | tf_op jit(solution)/shard_map/ppermute | solution.py:327
  83.3 12.9 %collective-permute-start.8 = (bf16[128,1024]{1,0:T(8,128)(2,1)S(1)}, bf16[128,1024]{1,0:T(8,128)(2,1)S(1)}, u32[]{:S(2)}, u32[]{:S(2)}) collective-permute-start(bf16[128,1024]{1,0:T(8,128)(2,1)S(1)} %filter.15), channel_id=1, source_target_pairs={{0,3},{1,2},{2,1},{3,0},{4,7},{5,6},{6,5},{7,4},{8,11},{9,10},{10,... | collective-permute-start | bytes 786440 | tf_op jit(solution)/shard_map/ppermute | solution.py:327
  96.2 1.9 %copy-start.8 = (f32[768,1024]{1,0:T(8,128)S(1)}, f32[768,1024]{1,0:T(8,128)}, u32[]{:S(2)}) copy-start(f32[768,1024]{1,0:T(8,128)} %early_sum.1.total_ref) | copy-start | bytes 9437188

commit v2 on v1

--- a/solution.py
+++ b/solution.py
@@ -12,7 +12,8 @@
 BF16 = jnp.bfloat16
 VMEM = pl.BlockSpec(memory_space=pltpu.VMEM)
 SMEM = pl.BlockSpec(memory_space=pltpu.SMEM)
-ANY = pl.BlockSpec(memory_space=pl.ANY)
+HBM = pl.BlockSpec(memory_space=pltpu.HBM)
+SIZE = 1024
 ORDER = (4, 2, 5, 7, 6, 1, 3)
 EARLY = (0, 4, 2, 5, 7, 1)
 LATE = (6, 3)
@@ -22,154 +23,140 @@
     return pl.CostEstimate(flops=int(flops), bytes_accessed=int(nbytes), transcendentals=0)
 
 
-def params(mib=48):
+def params(mib=16):
     return pltpu.CompilerParams(vmem_limit_bytes=mib * 1024 * 1024)
 
 
-def pack_kernel(first_phase, last_phase, first_coh, last_coh, left_out, right_out):
+def pack_kernel(phase_hbm, coh_hbm, left_out, right_out, edges, sems):
+    width = phase_hbm.shape[2]
+    copies = []
+    for j, hbm in enumerate((phase_hbm, coh_hbm)):
+        for side, at in ((0, 0), (1, width - LANES)):
+            copies.append(pltpu.make_async_copy(hbm.at[:, :, pl.ds(at, LANES)], edges.at[j, side], sems.at[2 * j + side]))
+    for copy in copies:
+        copy.start()
+    lane = lax.broadcasted_iota(jnp.int32, (8, LANES), 1)
+    for j in range(2):
+        for side, out in ((0, left_out), (1, right_out)):
+            copies[2 * j + side].wait()
+            for g in range(4):
+                packed = jnp.zeros((8, LANES), F32)
+                for k in range(32):
+                    value = edges[j, side, 32 * g + k].astype(F32)
+                    value = pltpu.roll(value, 4 * k, 1) if k else value
+                    first = 4 * k if side == 0 else (4 * k - 2) % LANES
+                    packed = jnp.where((lane == first) | (lane == first + 1), value, packed)
+                out[j, g] = packed.astype(BF16)
+
+
+def pack_edges(phases, coherence):
+    count, rows, _ = phases.shape
+    small = jax.ShapeDtypeStruct((2, count // 32, rows, LANES), BF16)
+    return pl.pallas_call(
+        pack_kernel,
+        in_specs=[HBM, HBM],
+        out_specs=[VMEM, VMEM],
+        out_shape=[small, small],
+        scratch_shapes=[pltpu.VMEM((2, 2, count, rows, LANES), BF16), pltpu.SemaphoreType.DMA((4,))],
+        compiler_params=params(60),
+        cost_estimate=cost(3e8, 1e6),
+        name="pack_edges",
+    )(phases, coherence)
+
+
+def bands_kernel(taps_ref, high_ref, low_ref):
+    place = lax.broadcasted_iota(jnp.int32, (2 * LANES, LANES), 0)
+    place = jnp.where(place >= LANES + 64, place - 2 * LANES, place)
+    tap = place - lax.broadcasted_iota(jnp.int32, (2 * LANES, LANES), 1) + 2
+    for a in range(3):
+        band = jnp.zeros((2 * LANES, LANES), F32)
+        for b in range(5):
+            band = jnp.where(tap == b, taps_ref[a, b], band)
+        high = band.astype(BF16)
+        high_ref[:, a * LANES : (a + 1) * LANES] = high
+        low_ref[:, a * LANES : (a + 1) * LANES] = (band - high.astype(F32)).astype(BF16)
+
+def bands(taps):
+    shape = jax.ShapeDtypeStruct((2 * LANES, 3 * LANES), BF16)
+    return pl.pallas_call(bands_kernel, in_specs=[SMEM], out_specs=[VMEM, VMEM], out_shape=[shape, shape],
+        compiler_params=params(), cost_estimate=cost(3e8, 1e5), name="bands")(taps)
+
+
+def expand_kernel(left_ref, right_ref, phase_out, coh_out):
     lane = lax.broadcasted_iota(jnp.int32, (4, 8, LANES), 2)
-    to_left = jnp.zeros((4, 8, LANES), F32)
-    to_right = jnp.zeros((4, 8, LANES), F32)
-    for k in range(32):
-        a = first_phase[:, k].astype(F32)
-        b = first_coh[:, k].astype(F32)
-        both = jnp.where(lane < 2, a, pltpu.roll(b, 2, 2))
-        here = (lane >> 2) == k
-        to_left = jnp.where(here, pltpu.roll(both, 4 * k, 2) if k else both, to_left)
-        a = last_phase[:, k].astype(F32)
-        b = last_coh[:, k].astype(F32)
-        both = jnp.where(lane >= 126, b, pltpu.roll(a, 126, 2))
-        shift = (4 * k + 4) % LANES
-        to_right = jnp.where(here, pltpu.roll(both, shift, 2) if shift else both, to_right)
-    left_out[...] = to_left.astype(BF16)
-    right_out[...] = to_right.astype(BF16)
-
-
-def pack_edges(phases, coherence):
-    count, rows, width = phases.shape
-    shape = (4, count // 4, rows, width)
-    first = pl.BlockSpec((4, count // 4, rows, LANES), lambda i: (0, 0, 0, 0))
-    last = pl.BlockSpec((4, count // 4, rows, LANES), lambda i: (0, 0, 0, width // LANES - 1))
-    small = jax.ShapeDtypeStruct((4, rows, LANES), BF16)
-    phase4 = phases.reshape(shape)
-    coh4 = coherence.reshape(shape)
-    return pl.pallas_call(
-        pack_kernel,
-        grid=(1,),
-        in_specs=[first, last, first, last],
-        out_specs=[pl.BlockSpec((4, rows, LANES), lambda i: (0, 0, 0))] * 2,
-        out_shape=[small, small],
-        compiler_params=params(),
-        cost_estimate=cost(3e8, 2e6),
-        name="pack_edges",
-    )(phase4, phase4, coh4, coh4)
-
-
-def filter_kernel(step, me_ref, taps_ref, phase_ref, coh_ref, left_ref, right_ref, out_ref, scratch):
+    from_left = (lane & 3) >= 2
+    for j, out in ((0, phase_out), (1, coh_out)):
+        both = jnp.where(from_left, left_ref[j].astype(F32), right_ref[j].astype(F32))
+        for k in range(32):
+            out[:, k] = (pltpu.roll(both, (LANES - 4 * k) % LANES, 2) if k else both).astype(BF16)
+
+def expand(left, right):
+    shape = jax.ShapeDtypeStruct((4, 32, 8, LANES), BF16)
+    out = pl.pallas_call(expand_kernel, in_specs=[VMEM, VMEM], out_specs=[VMEM, VMEM], out_shape=[shape, shape],
+        compiler_params=params(), cost_estimate=cost(5e8, 1e5), name="expand")(left, right)
+    return [o.reshape(128, 8, LANES) for o in out]
+
+
+def filter_kernel(step, m, me_ref, high_ref, low_ref, phase_ref, coh_ref, phase_edge_ref, coh_edge_ref, out_ref, scratch):
     block = me_ref[0] ^ step
     count = phase_ref.shape[0]
     blocks = phase_ref.shape[2] // LANES
-    taps = [[taps_ref[a, b] for b in range(5)] for a in range(3)]
-    group = 2
-    lane = lax.broadcasted_iota(jnp.int32, (group, 8, LANES), 2)
+    group = m // 8
+    lane = lax.broadcasted_iota(jnp.int32, (1, 1, LANES), 2)
+    left_here = jnp.where(block == 0, LANES, 64)
+    right_here = jnp.where(block == blocks - 1, 0, 64)
+    use_left = lane >= left_here
+    use_right = lane < right_here
     row = lax.broadcasted_iota(jnp.int32, (group, 8, LANES), 1)
 
     def column(index):
         return pl.ds(pl.multiple_of(index * LANES, LANES), LANES)
-
-    def one(i, left_edge, right_edge):
+    here, before, after = column(block), column(jnp.maximum(block - 1, 0)), column(jnp.minimum(block + 1, blocks - 1))
+
+    def body(i, carry):
         at = pl.ds(i * group, group)
-        centre = column(block)
-        phase = phase_ref[at, :, centre].astype(F32)
-        coh = coh_ref[at, :, centre].astype(F32)
-        if left_edge or right_edge:
-            packed = []
-            ref = left_ref if left_edge else right_ref
-            for j in range(group):
-                which = i * group + j
-                g = which // 32
-                k = which % 32
-                vector = ref[pl.ds(g, 1)].astype(F32)
-                packed.append(pltpu.roll(vector, (LANES - 4 * k) % LANES, 2))
-            packed = jnp.concatenate(packed, axis=0)
-        if left_edge:
-            phase_before = pltpu.roll(packed, 126, 2)
-            coh_before = pltpu.roll(packed, 124, 2)
-        else:
-            phase_before = phase_ref[at, :, column(jnp.maximum(block - 1, 0))].astype(F32)
-            coh_before = coh_ref[at, :, column(jnp.maximum(block - 1, 0))].astype(F32)
-        if right_edge:
-            phase_after = packed
-            coh_after = pltpu.roll(packed, 126, 2)
-        else:
-            phase_after = phase_ref[at, :, column(jnp.minimum(block + 1, blocks - 1))].astype(F32)
-            coh_after = coh_ref[at, :, column(jnp.minimum(block + 1, blocks - 1))].astype(F32)
-
-        def shifted(before, here, after, offset):
-            if offset == 0:
-                return here
-            if offset < 0:
-                return pltpu.roll(jnp.where(lane >= LANES + offset, before, here), -offset, 2)
-            return pltpu.roll(jnp.where(lane < offset, after, here), LANES - offset, 2)
-
-        num = [None] * 3
-        den = [None] * 3
-        for b in range(5):
-            weight = shifted(coh_before, coh, coh_after, b - 2)
-            value = shifted(phase_before, phase, phase_after, b - 2) * weight
-            for a in range(3):
-                n = value * taps[a][b]
-                d = weight * taps[a][b]
-                num[a] = n if num[a] is None else num[a] + n
-                den[a] = d if den[a] is None else den[a] + d
-
+        def edge(ref, edge_ref):
+            return jnp.where(use_left, ref[at, :, before], jnp.where(use_right, ref[at, :, after], edge_ref[at]))
+        def flat(x):
+            return x.reshape(m, LANES)
+        phase = jnp.concatenate([flat(phase_ref[at, :, here]), flat(edge(phase_ref, phase_edge_ref))], axis=1)
+        coh = jnp.concatenate([flat(coh_ref[at, :, here]), flat(edge(coh_ref, coh_edge_ref))], axis=1)
+        product = phase.astype(F32) * coh.astype(F32)
+        major = product.astype(BF16)
+        minor = (product - major.astype(F32)).astype(BF16)
+        high, low = high_ref[...], low_ref[...]
+        den = jnp.dot(jnp.concatenate([coh, coh], axis=1), jnp.concatenate([high, low], axis=0), preferred_element_type=F32)
+        num = jnp.dot(jnp.concatenate([major, minor, major], axis=1), jnp.concatenate([high, high, low], axis=0), preferred_element_type=F32)
         def vertical(parts):
-            down = jnp.where(row == 0, 0.0, pltpu.roll(parts[0], 1, 1))
-            up = jnp.where(row == 7, 0.0, pltpu.roll(parts[2], 7, 1))
-            return parts[1] + down + up
-
+            p = [parts[:, a * LANES : (a + 1) * LANES].reshape(group, 8, LANES) for a in range(3)]
+            down = jnp.where(row == 0, 0.0, pltpu.roll(p[0], 1, 1))
+            up = jnp.where(row == 7, 0.0, pltpu.roll(p[2], 7, 1))
+            return p[1] + down + up
         bottom = vertical(den)
         inverse = pl.reciprocal(bottom, approx=True)
         inverse = inverse * (2.0 - bottom * inverse)
-        inverse = inverse * (2.0 - bottom * inverse)
         result = vertical(num) * inverse
-        scratch[pl.ds(pl.multiple_of(i * group * 8, group * 8), group * 8), :] = result.reshape(group * 8, LANES)
-
-    def run(left_edge, right_edge):
-        def body(i, carry):
-            one(i, left_edge, right_edge)
-            return carry
-
-        lax.fori_loop(0, count // group, body, 0, unroll=2)
-
-    @pl.when(block == 0)
-    def _():
-        run(True, False)
-
-    @pl.when(block == blocks - 1)
-    def _():
-        run(False, True)
-
-    @pl.when((block > 0) & (block < blocks - 1))
-    def _():
-        run(False, False)
-
+        scratch[pl.ds(pl.multiple_of(i * m, m), m), :] = result.reshape(m, LANES)
+        return carry
+    if count // group == 1:
+        body(0, 0)
+    else:
+        lax.fori_loop(0, count // group, body, 0)
     for r in range(8):
         out_ref[:, r * LANES : (r + 1) * LANES] = scratch[pl.ds(r, count, stride=8), :].astype(BF16)
 
-
-def filter_block(step, me, taps, phases, coherence, left, right):
+def filter_block(step, me, bands, phases, coherence, phase_edge, coh_edge):
     count, rows, _ = phases.shape
     return pl.pallas_call(
-        functools.partial(filter_kernel, step),
-        in_specs=[SMEM, SMEM, VMEM, VMEM, VMEM, VMEM],
+        functools.partial(filter_kernel, step, SIZE),
+        in_specs=[SMEM] + [VMEM] * 6,
         out_specs=VMEM,
         out_shape=jax.ShapeDtypeStruct((count, rows * LANES), BF16),
         scratch_shapes=[pltpu.VMEM((count * rows, LANES), F32)],
         compiler_params=params(),
         cost_estimate=cost(1.5e9, 1e6),
         name="filter",
-    )(me, taps, phases, coherence, left, right)
+    )(me, *bands, phases, coherence, phase_edge, coh_edge)
 
 
 def network_kernel(pairs_ref, triplets_ref, member_ref, dates_ref, first):
@@ -297,7 +284,7 @@
     return pl.pallas_call(
         functools.partial(late_kernel, steps),
         in_specs=[SMEM] + [VMEM] * (4 + len(pieces)),
-        out_specs=[ANY, ANY],
+        out_specs=[HBM, HBM],
         out_shape=[jax.ShapeDtypeStruct(shape, BF16) for shape in outs],
         scratch_shapes=[
             pltpu.VMEM(outs[0], BF16),
@@ -320,12 +307,14 @@
     to_left, to_right = pack_edges(phases, coherence)
     left = lax.ppermute(to_right, "img", [(i, i + 1) for i in range(size - 1)])
     right = lax.ppermute(to_left, "img", [(i + 1, i) for i in range(size - 1)])
+    tap_bands = bands(kernel_taps)
     member, dates_matrix = network(date_pairs, triplets, inverse.shape[0])
+    edges = expand(left, right)
     pieces = {}
     for step in ORDER:
-        block = filter_block(step, me, kernel_taps, phases, coherence, left, right)
+        block = filter_block(step, me, tap_bands, phases, coherence, *edges)
         pieces[step] = lax.ppermute(block, "ifg", [(i, i ^ step) for i in range(peers)])
-    pieces[0] = filter_block(0, me, kernel_taps, phases, coherence, left, right)
+    pieces[0] = filter_block(0, me, tap_bands, phases, coherence, *edges)
     total = early_sum(EARLY, me, inverse, member, [pieces[s] for s in EARLY])
     return tuple(late_sum(LATE, me, inverse, member, dates_matrix, total, [pieces[s] for s in LATE], rows))
 

time: 101 us -> 59.1 us (0.59)
  Pallas kernels: 56.7 us -> 21.1 us
  waiting for transfers between devices: 0.02 us -> 10.2 us
  starting transfers between devices: 35.9 us -> 25.8 us
  local copies, waits for them, and re-layouts: 6.68 us -> 0.62 us
    pallas_call x9 -> x11, Pallas kernels: 49.8 us -> 15.8 us  [the longest x8 12.7 us: filter_block(): pl.pallas_call(functools.partial(filter_kernel, step, SIZE), in_specs=[SM...]
    ppermute x7, waiting for transfers between devices: 0.02 us -> 10.2 us  [per_device(): lax.ppermute(block, 'ifg', [(i, i ^ step) for i in range(peers)])]
    ppermute x7, starting transfers between devices: 30.4 us -> 20.3 us  [per_device(): lax.ppermute(block, 'ifg', [(i, i ^ step) for i in range(peers)])]
    unnamed x18 -> x12, local copies, waits for them, and re-layouts: 6.68 us -> 0.62 us
    pallas_call x1, Pallas kernels: 3.09 us -> 1.42 us  [early_sum(): pl.pallas_call(functools.partial(early_kernel, steps), in_specs=[SMEM] +...]
  transfers between devices with their start and end apart: 9 -> 9, of which waited for: 0 -> 3; matrix products, arithmetic and copies ran while one was open for 0% -> 0% of each run, Pallas kernels for 47% -> 15%
where the time goes in v2:
time: 59.1 us; the launch traced here: 58.8 us
  starting transfers between devices  25.8 us (44%)
  Pallas kernels  21.1 us (36%)
  waiting for transfers between devices  10.2 us (17%)
  between operations  0.99 us (2%)
  local copies, waits for them, and re-layouts  0.62 us (1%)
    ppermute x7, starting transfers between devices, per_device(): lax.ppermute(block, 'ifg', [(i, i ^ step) for i in range(peers)])  20.3 us
    pallas_call x8, Pallas kernels, filter_block(): pl.pallas_call(functools.partial(filter_kernel, step, SIZE), in_specs=[SM...  12.7 us
    ppermute x7, waiting for transfers between devices, per_device(): lax.ppermute(block, 'ifg', [(i, i ^ step) for i in range(peers)])  10.2 us
    ppermute x1, starting transfers between devices, per_device(): right = lax.ppermute(to_left, 'img', [(i + 1, i) for i in range(size - 1)])  3.64 us
    pallas_call x1, Pallas kernels, late_sum(): pl.pallas_call(functools.partial(late_kernel, steps), in_specs=[SMEM] + [...  2.2 us
    pallas_call x1, Pallas kernels, pack_edges(): pl.pallas_call(pack_kernel, in_specs=[HBM, HBM], out_specs=[VMEM, VMEM],...  2.15 us
    ppermute x1, starting transfers between devices, per_device(): left = lax.ppermute(to_right, 'img', [(i, i + 1) for i in range(size - 1)])  1.92 us
    pallas_call x1, Pallas kernels, network(): pl.pallas_call(network_kernel, in_specs=[VMEM, VMEM], out_specs=[VMEM, VM...  1.65 us
  transfers between devices with their start and end apart: 9, of which 3 were waited for; matrix products, arithmetic and copies ran while one was open for 0% of the time, Pallas kernels for 15%

profile of v2, /device:TPU:10, one launch (start us, length us, event | category | flops | bytes accessed | tf_op | source)
XLA Modules:
  0.0 58.8 jit_solution(11046790921531280780)
XLA Ops:
  0.6 2.2 %pack_edges.1 = (bf16[2,4,8,128]{3,2,1,0:T(8,128)(2,1)}, bf16[2,4,8,128]{3,2,1,0:T(8,128)(2,1)}) custom-call(bf16[128,8,1024]{2,1,0:T(8,128)(2,1)} %phase_ref.15, bf16[128,8,1024]{2,1,0:T(8,128)(2,1)} %coh_ref.15), custom_call_target="tpu_custom_call" | custom-call | flops 300000000 | bytes 1000000 | tf_op jit(solution)/shard_map/pack_edges/pallas_call | solution.py:55
  2.8 1.9 %collective-permute-start = (bf16[2,4,8,128]{3,2,1,0:T(8,128)(2,1)}, bf16[2,4,8,128]{3,2,1,0:T(8,128)(2,1)S(1)}, u32[]{:S(2)}, u32[]{:S(2)}) collective-permute-start(bf16[2,4,8,128]{3,2,1,0:T(8,128)(2,1)} %get-tuple-element.14), channel_id=1, source_target_pairs={{0,8},{8,16},{16,24},{24,32},{32,40},{40,48},{48,56},{56,64},{64,7... | collective-permute-start | bytes 49160 | tf_op jit(solution)/shard_map/ppermute | solution.py:308
  4.7 3.6 %collective-permute-start.1 = (bf16[2,4,8,128]{3,2,1,0:T(8,128)(2,1)}, bf16[2,4,8,128]{3,2,1,0:T(8,128)(2,1)S(1)}, u32[]{:S(2)}, u32[]{:S(2)}) collective-permute-start(bf16[2,4,8,128]{3,2,1,0:T(8,128)(2,1)} %get-tuple-element.15), channel_id=1, source_target_pairs={{8,0},{16,8},{24,16},{32,24},{40,32},{48,40},{56,48},{64,56},{72,6... | collective-permute-start | bytes 49160 | tf_op jit(solution)/shard_map/ppermute | solution.py:309
  8.4 0.0 copy-start.5
  8.4 0.0 copy-start.1
  8.4 1.7 %network.1 = (bf16[512,1024]{1,0:T(8,128)(2,1)S(1)}, bf16[512,256]{1,0:T(8,128)(2,1)S(1)}) custom-call(s32[2,1024]{1,0:T(2,128)S(1)} %bitcast.5, s32[3,512]{1,0:T(4,128)S(1)} %bitcast.6), custom_call_target="tpu_custom_call" | custom-call | flops 2000000000 | bytes 1000000 | tf_op jit(solution)/shard_map/network/pallas_call | solution.py:188
  10.1 0.0 copy-start
  10.1 0.7 %bands.1 = (bf16[256,384]{1,0:T(8,128)(2,1)S(1)}, bf16[256,384]{1,0:T(8,128)(2,1)S(1)}) custom-call(f32[3,5]{1,0:T(4,128)S(1)} %copy-done.5), custom_call_target="tpu_custom_call" | custom-call | flops 300000000 | bytes 100000 | tf_op jit(solution)/shard_map/bands/pallas_call | solution.py:81
  10.9 0.0 collective-permute-done.1.right_ref
  10.9 0.2 expand.1
  11.1 0.6 %copy-done = bf16[128,8,1024]{2,1,0:T(8,128)(2,1)S(1)} copy-done((bf16[128,8,1024]{2,1,0:T(8,128)(2,1)S(1)}, bf16[128,8,1024]{2,1,0:T(8,128)(2,1)}, u32[]{:S(2)}) %copy-start) | copy-done | bytes 2097176
  11.7 1.6 %filter.13 = bf16[128,1024]{1,0:T(8,128)(2,1)S(1)} custom-call(s32[1]{0:T(128)} %bitcast.me_ref, bf16[256,384]{1,0:T(8,128)(2,1)S(1)} %get-tuple-element.12.high_ref, bf16[256,384]{1,0:T(8,128)(2,1)S(1)} %get-tuple-element.13.low_ref, bf16[128,8,1024]{2,1,0:T(8,128)(2,1)S(1)} %copy-done, bf16[128,8,1024]{2,1,0:T(8,128)(2,1)S(1)} %copy-done.1, ...), custom_call_target="tpu_custom_call" | custom-call | flops 1500000000 | bytes 1000000 | tf_op jit(solution)/shard_map/filter/pallas_call | solution.py:150
  13.3 1.6 %filter.12 = bf16[128,1024]{1,0:T(8,128)(2,1)S(1)} custom-call(s32[1]{0:T(128)} %bitcast.me_ref, bf16[256,384]{1,0:T(8,128)(2,1)S(1)} %get-tuple-element.12.high_ref, bf16[256,384]{1,0:T(8,128)(2,1)S(1)} %get-tuple-element.13.low_ref, bf16[128,8,1024]{2,1,0:T(8,128)(2,1)S(1)} %copy-done, bf16[128,8,1024]{2,1,0:T(8,128)(2,1)S(1)} %copy-done.1, ...), custom_call_target="tpu_custom_call" | custom-call | flops 1500000000 | bytes 1000000 | tf_op jit(solution)/shard_map/filter/pallas_call | solution.py:150
  14.9 1.6 %filter.11 = bf16[128,1024]{1,0:T(8,128)(2,1)S(1)} custom-call(s32[1]{0:T(128)} %bitcast.me_ref, bf16[256,384]{1,0:T(8,128)(2,1)S(1)} %get-tuple-element.12.high_ref, bf16[256,384]{1,0:T(8,128)(2,1)S(1)} %get-tuple-element.13.low_ref, bf16[128,8,1024]{2,1,0:T(8,128)(2,1)S(1)} %copy-done, bf16[128,8,1024]{2,1,0:T(8,128)(2,1)S(1)} %copy-done.1, ...), custom_call_target="tpu_custom_call" | custom-call | flops 1500000000 | bytes 1000000 | tf_op jit(solution)/shard_map/filter/pallas_call | solution.py:150
  16.5 1.6 %filter.10 = bf16[128,1024]{1,0:T(8,128)(2,1)S(1)} custom-call(s32[1]{0:T(128)} %bitcast.me_ref, bf16[256,384]{1,0:T(8,128)(2,1)S(1)} %get-tuple-element.12.high_ref, bf16[256,384]{1,0:T(8,128)(2,1)S(1)} %get-tuple-element.13.low_ref, bf16[128,8,1024]{2,1,0:T(8,128)(2,1)S(1)} %copy-done, bf16[128,8,1024]{2,1,0:T(8,128)(2,1)S(1)} %copy-done.1, ...), custom_call_target="tpu_custom_call" | custom-call | flops 1500000000 | bytes 1000000 | tf_op jit(solution)/shard_map/filter/pallas_call | solution.py:150
  18.1 1.6 %filter.9 = bf16[128,1024]{1,0:T(8,128)(2,1)S(1)} custom-call(s32[1]{0:T(128)} %bitcast.me_ref, bf16[256,384]{1,0:T(8,128)(2,1)S(1)} %get-tuple-element.12.high_ref, bf16[256,384]{1,0:T(8,128)(2,1)S(1)} %get-tuple-element.13.low_ref, bf16[128,8,1024]{2,1,0:T(8,128)(2,1)S(1)} %copy-done, bf16[128,8,1024]{2,1,0:T(8,128)(2,1)S(1)} %copy-done.1, ...), custom_call_target="tpu_custom_call" | custom-call | flops 1500000000 | bytes 1000000 | tf_op jit(solution)/shard_map/filter/pallas_call | solution.py:150
  19.6 2.2 %collective-permute-start.2 = (bf16[128,1024]{1,0:T(8,128)(2,1)S(1)}, bf16[128,1024]{1,0:T(8,128)(2,1)S(1)}, u32[]{:S(2)}, u32[]{:S(2)}) collective-permute-start(bf16[128,1024]{1,0:T(8,128)(2,1)S(1)} %filter.9), channel_id=1, source_target_pairs={{0,4},{1,5},{2,6},{3,7},{4,0},{5,1},{6,2},{7,3},{8,12},{9,13},{10,... | collective-permute-start | bytes 786440 | tf_op jit(solution)/shard_map/ppermute | solution.py:316
  21.9 3.9 %collective-permute-start.3 = (bf16[128,1024]{1,0:T(8,128)(2,1)S(1)}, bf16[128,1024]{1,0:T(8,128)(2,1)S(1)}, u32[]{:S(2)}, u32[]{:S(2)}) collective-permute-start(bf16[128,1024]{1,0:T(8,128)(2,1)S(1)} %filter.10), channel_id=1, source_target_pairs={{0,2},{1,3},{2,0},{3,1},{4,6},{5,7},{6,4},{7,5},{8,10},{9,11},{10,... | collective-permute-start | bytes 786440 | tf_op jit(solution)/shard_map/ppermute | solution.py:316
  25.7 1.9 %collective-permute-start.4 = (bf16[128,1024]{1,0:T(8,128)(2,1)S(1)}, bf16[128,1024]{1,0:T(8,128)(2,1)S(1)}, u32[]{:S(2)}, u32[]{:S(2)}) collective-permute-start(bf16[128,1024]{1,0:T(8,128)(2,1)S(1)} %filter.11), channel_id=1, source_target_pairs={{0,5},{1,4},{2,7},{3,6},{4,1},{5,0},{6,3},{7,2},{8,13},{9,12},{10,... | collective-permute-start | bytes 786440 | tf_op jit(solution)/shard_map/ppermute | solution.py:316
  27.6 1.1 %collective-permute-start.5 = (bf16[128,1024]{1,0:T(8,128)(2,1)S(1)}, bf16[128,1024]{1,0:T(8,128)(2,1)S(1)}, u32[]{:S(2)}, u32[]{:S(2)}) collective-permute-start(bf16[128,1024]{1,0:T(8,128)(2,1)S(1)} %filter.12), channel_id=1, source_target_pairs={{0,7},{1,6},{2,5},{3,4},{4,3},{5,2},{6,1},{7,0},{8,15},{9,14},{10,... | collective-permute-start | bytes 786440 | tf_op jit(solution)/shard_map/ppermute | solution.py:316
  28.7 1.6 %collective-permute-start.6 = (bf16[128,1024]{1,0:T(8,128)(2,1)S(1)}, bf16[128,1024]{1,0:T(8,128)(2,1)S(1)}, u32[]{:S(2)}, u32[]{:S(2)}) collective-permute-start(bf16[128,1024]{1,0:T(8,128)(2,1)S(1)} %filter.13), channel_id=1, source_target_pairs={{0,1},{1,0},{2,3},{3,2},{4,5},{5,4},{6,7},{7,6},{8,9},{9,8},{10,11... | collective-permute-start | bytes 786440 | tf_op jit(solution)/shard_map/ppermute | solution.py:316
  30.3 1.6 %filter.15 = bf16[128,1024]{1,0:T(8,128)(2,1)S(1)} custom-call(s32[1]{0:T(128)} %bitcast.me_ref, bf16[256,384]{1,0:T(8,128)(2,1)S(1)} %get-tuple-element.12.high_ref, bf16[256,384]{1,0:T(8,128)(2,1)S(1)} %get-tuple-element.13.low_ref, bf16[128,8,1024]{2,1,0:T(8,128)(2,1)S(1)} %copy-done, bf16[128,8,1024]{2,1,0:T(8,128)(2,1)S(1)} %copy-done.1, ...), custom_call_target="tpu_custom_call" | custom-call | flops 1500000000 | bytes 1000000 | tf_op jit(solution)/shard_map/filter/pallas_call | solution.py:150
  31.8 1.6 %filter.14 = bf16[128,1024]{1,0:T(8,128)(2,1)S(1)} custom-call(s32[1]{0:T(128)} %bitcast.me_ref, bf16[256,384]{1,0:T(8,128)(2,1)S(1)} %get-tuple-element.12.high_ref, bf16[256,384]{1,0:T(8,128)(2,1)S(1)} %get-tuple-element.13.low_ref, bf16[128,8,1024]{2,1,0:T(8,128)(2,1)S(1)} %copy-done, bf16[128,8,1024]{2,1,0:T(8,128)(2,1)S(1)} %copy-done.1, ...), custom_call_target="tpu_custom_call" | custom-call | flops 1500000000 | bytes 1000000 | tf_op jit(solution)/shard_map/filter/pallas_call | solution.py:150
  33.4 0.0 copy-start.2
  33.5 4.5 %collective-permute-start.7 = (bf16[128,1024]{1,0:T(8,128)(2,1)S(1)}, bf16[128,1024]{1,0:T(8,128)(2,1)S(1)}, u32[]{:S(2)}, u32[]{:S(2)}) collective-permute-start(bf16[128,1024]{1,0:T(8,128)(2,1)S(1)} %filter.14), channel_id=1, source_target_pairs={{0,6},{1,7},{2,4},{3,5},{4,2},{5,3},{6,0},{7,1},{8,14},{9,15},{10,... | collective-permute-start | bytes 786440 | tf_op jit(solution)/shard_map/ppermute | solution.py:316
  38.0 1.1 %collective-permute-done.3.refs_2_ = bf16[128,1024]{1,0:T(8,128)(2,1)S(1)} collective-permute-done((bf16[128,1024]{1,0:T(8,128)(2,1)S(1)}, bf16[128,1024]{1,0:T(8,128)(2,1)S(1)}, u32[]{:S(2)}, u32[]{:S(2)}) %collective-permute-start.3) | collective-permute-done | bytes 262176 | tf_op jit(solution)/shard_map/ppermute | solution.py:316
  39.1 5.2 %collective-permute-start.8 = (bf16[128,1024]{1,0:T(8,128)(2,1)S(1)}, bf16[128,1024]{1,0:T(8,128)(2,1)S(1)}, u32[]{:S(2)}, u32[]{:S(2)}) collective-permute-start(bf16[128,1024]{1,0:T(8,128)(2,1)S(1)} %filter.15), channel_id=1, source_target_pairs={{0,3},{1,2},{2,1},{3,0},{4,7},{5,6},{6,5},{7,4},{8,11},{9,10},{10,... | collective-permute-start | bytes 786440 | tf_op jit(solution)/shard_map/ppermute | solution.py:316
  44.3 1.6 %filter.8.refs_0_ = bf16[128,1024]{1,0:T(8,128)(2,1)S(1)} custom-call(s32[1]{0:T(128)} %bitcast.me_ref, bf16[256,384]{1,0:T(8,128)(2,1)S(1)} %get-tuple-element.12.high_ref, bf16[256,384]{1,0:T(8,128)(2,1)S(1)} %get-tuple-element.13.low_ref, bf16[128,8,1024]{2,1,0:T(8,128)(2,1)S(1)} %copy-done, bf16[128,8,1024]{2,1,0:T(8,128)(2,1)S(1)} %copy-done.1, ...), custom_call_target="tpu_custom_call" | custom-call | flops 1500000000 | bytes 1000000 | tf_op jit(solution)/shard_map/filter/pallas_call | solution.py:150
  45.9 5.7 %collective-permute-done.6.refs_5_ = bf16[128,1024]{1,0:T(8,128)(2,1)S(1)} collective-permute-done((bf16[128,1024]{1,0:T(8,128)(2,1)S(1)}, bf16[128,1024]{1,0:T(8,128)(2,1)S(1)}, u32[]{:S(2)}, u32[]{:S(2)}) %collective-permute-start.6) | collective-permute-done | bytes 262176 | tf_op jit(solution)/shard_map/ppermute | solution.py:316
  51.6 1.4 %early_sum.1.total_ref = f32[768,1024]{1,0:T(8,128)S(1)} custom-call(s32[1]{0:T(128)} %bitcast.me_ref, bf16[256,1024]{1,0:T(8,128)(2,1)S(1)} %copy-done.2, bf16[512,1024]{1,0:T(8,128)(2,1)S(1)} %get-tuple-element.10.member_ref, bf16[128,1024]{1,0:T(8,128)(2,1)S(1)} %filter.8.refs_0_, bf16[128,1024]{1,0:T(8,128)(2,1)S(1)} %collective-permute-done.2.refs_1_, ...), custom_call_target="tpu_custom_call" | custom-call | flops 2000000000 | bytes 1000000 | tf_op jit(solution)/shard_map/early_sum/pallas_call | solution.py:227
  53.0 3.4 %collective-permute-done.8.refs_1_ = bf16[128,1024]{1,0:T(8,128)(2,1)S(1)} collective-permute-done((bf16[128,1024]{1,0:T(8,128)(2,1)S(1)}, bf16[128,1024]{1,0:T(8,128)(2,1)S(1)}, u32[]{:S(2)}, u32[]{:S(2)}) %collective-permute-start.8) | collective-permute-done | bytes 262176 | tf_op jit(solution)/shard_map/ppermute | solution.py:316
  56.4 2.2 %late_sum.1 = (bf16[256,8,128]{2,1,0:T(8,128)(2,1)}, bf16[512,8,128]{2,1,0:T(8,128)(2,1)}) custom-call(s32[1]{0:T(128)} %bitcast.me_ref, bf16[256,1024]{1,0:T(8,128)(2,1)S(1)} %copy-done.2, bf16[512,1024]{1,0:T(8,128)(2,1)S(1)} %get-tuple-element.10.member_ref, bf16[512,256]{1,0:T(8,128)(2,1)S(1)} %get-tuple-element.11.dates_ref, ...), custom_call_target="tpu_custom_call" | custom-call | flops 3000000000 | bytes 2000000 | tf_op jit(solution)/shard_map/late_sum/pallas_call | solution.py:284
  (12 shorter events, 0.0 us)
Async XLA Ops:
  0.6 7.8 %copy-start.4 = (s32[512,3]{0,1:T(4,128)S(1)}, s32[512,3]{0,1:T(4,128)}, u32[]{:S(2)}) copy-start(s32[512,3]{0,1:T(4,128)} %param.11) | copy-start | bytes 18436
  0.6 7.8 %copy-start.3 = (s32[1024,2]{0,1:T(2,128)S(1)}, s32[1024,2]{0,1:T(2,128)}, u32[]{:S(2)}) copy-start(s32[1024,2]{0,1:T(2,128)} %param.10) | copy-start | bytes 24580
  2.8 8.1 %collective-permute-start = (bf16[2,4,8,128]{3,2,1,0:T(8,128)(2,1)}, bf16[2,4,8,128]{3,2,1,0:T(8,128)(2,1)S(1)}, u32[]{:S(2)}, u32[]{:S(2)}) collective-permute-start(bf16[2,4,8,128]{3,2,1,0:T(8,128)(2,1)} %get-tuple-element.14), channel_id=1, source_target_pairs={{0,8},{8,16},{16,24},{24,32},{32,40},{40,48},{48,56},{56,64},{64,7... | collective-permute-start | bytes 49160 | tf_op jit(solution)/shard_map/ppermute | solution.py:308
  4.7 6.1 %collective-permute-start.1 = (bf16[2,4,8,128]{3,2,1,0:T(8,128)(2,1)}, bf16[2,4,8,128]{3,2,1,0:T(8,128)(2,1)S(1)}, u32[]{:S(2)}, u32[]{:S(2)}) collective-permute-start(bf16[2,4,8,128]{3,2,1,0:T(8,128)(2,1)} %get-tuple-element.15), channel_id=1, source_target_pairs={{8,0},{16,8},{24,16},{32,24},{40,32},{48,40},{56,48},{64,56},{72,6... | collective-permute-start | bytes 49160 | tf_op jit(solution)/shard_map/ppermute | solution.py:309
  8.4 1.7 %copy-start.5 = (f32[3,5]{1,0:T(4,128)S(1)}, f32[3,5]{1,0:T(4,128)}, u32[]{:S(2)}) copy-start(f32[3,5]{1,0:T(4,128)} %taps_ref.1) | copy-start | bytes 184
  8.4 2.7 %copy-start.1 = (bf16[128,8,1024]{2,1,0:T(8,128)(2,1)S(1)}, bf16[128,8,1024]{2,1,0:T(8,128)(2,1)}, u32[]{:S(2)}) copy-start(bf16[128,8,1024]{2,1,0:T(8,128)(2,1)} %coh_ref.15) | copy-start | bytes 6291460
  10.1 1.6 %copy-start = (bf16[128,8,1024]{2,1,0:T(8,128)(2,1)S(1)}, bf16[128,8,1024]{2,1,0:T(8,128)(2,1)}, u32[]{:S(2)}) copy-start(bf16[128,8,1024]{2,1,0:T(8,128)(2,1)} %phase_ref.15) | copy-start | bytes 6291460
  19.6 13.8 %collective-permute-start.2 = (bf16[128,1024]{1,0:T(8,128)(2,1)S(1)}, bf16[128,1024]{1,0:T(8,128)(2,1)S(1)}, u32[]{:S(2)}, u32[]{:S(2)}) collective-permute-start(bf16[128,1024]{1,0:T(8,128)(2,1)S(1)} %filter.9), channel_id=1, source_target_pairs={{0,4},{1,5},{2,6},{3,7},{4,0},{5,1},{6,2},{7,3},{8,12},{9,13},{10,... | collective-permute-start | bytes 786440 | tf_op jit(solution)/shard_map/ppermute | solution.py:316
  21.9 17.2 %collective-permute-start.3 = (bf16[128,1024]{1,0:T(8,128)(2,1)S(1)}, bf16[128,1024]{1,0:T(8,128)(2,1)S(1)}, u32[]{:S(2)}, u32[]{:S(2)}) collective-permute-start(bf16[128,1024]{1,0:T(8,128)(2,1)S(1)} %filter.10), channel_id=1, source_target_pairs={{0,2},{1,3},{2,0},{3,1},{4,6},{5,7},{6,4},{7,5},{8,10},{9,11},{10,... | collective-permute-start | bytes 786440 | tf_op jit(solution)/shard_map/ppermute | solution.py:316
  25.7 20.1 %collective-permute-start.4 = (bf16[128,1024]{1,0:T(8,128)(2,1)S(1)}, bf16[128,1024]{1,0:T(8,128)(2,1)S(1)}, u32[]{:S(2)}, u32[]{:S(2)}) collective-permute-start(bf16[128,1024]{1,0:T(8,128)(2,1)S(1)} %filter.11), channel_id=1, source_target_pairs={{0,5},{1,4},{2,7},{3,6},{4,1},{5,0},{6,3},{7,2},{8,13},{9,12},{10,... | collective-permute-start | bytes 786440 | tf_op jit(solution)/shard_map/ppermute | solution.py:316
  27.6 18.3 %collective-permute-start.5 = (bf16[128,1024]{1,0:T(8,128)(2,1)S(1)}, bf16[128,1024]{1,0:T(8,128)(2,1)S(1)}, u32[]{:S(2)}, u32[]{:S(2)}) collective-permute-start(bf16[128,1024]{1,0:T(8,128)(2,1)S(1)} %filter.12), channel_id=1, source_target_pairs={{0,7},{1,6},{2,5},{3,4},{4,3},{5,2},{6,1},{7,0},{8,15},{9,14},{10,... | collective-permute-start | bytes 786440 | tf_op jit(solution)/shard_map/ppermute | solution.py:316
  28.7 22.9 %collective-permute-start.6 = (bf16[128,1024]{1,0:T(8,128)(2,1)S(1)}, bf16[128,1024]{1,0:T(8,128)(2,1)S(1)}, u32[]{:S(2)}, u32[]{:S(2)}) collective-permute-start(bf16[128,1024]{1,0:T(8,128)(2,1)S(1)} %filter.13), channel_id=1, source_target_pairs={{0,1},{1,0},{2,3},{3,2},{4,5},{5,4},{6,7},{7,6},{8,9},{9,8},{10,11... | collective-permute-start | bytes 786440 | tf_op jit(solution)/shard_map/ppermute | solution.py:316
  33.4 18.1 %copy-start.2 = (bf16[256,1024]{1,0:T(8,128)(2,1)S(1)}, bf16[256,1024]{1,0:T(8,128)(2,1)}, u32[]{:S(2)}) copy-start(bf16[256,1024]{1,0:T(8,128)(2,1)} %inverse_ref.3) | copy-start | bytes 1572868
  33.5 19.5 %collective-permute-start.7 = (bf16[128,1024]{1,0:T(8,128)(2,1)S(1)}, bf16[128,1024]{1,0:T(8,128)(2,1)S(1)}, u32[]{:S(2)}, u32[]{:S(2)}) collective-permute-start(bf16[128,1024]{1,0:T(8,128)(2,1)S(1)} %filter.14), channel_id=1, source_target_pairs={{0,6},{1,7},{2,4},{3,5},{4,2},{5,3},{6,0},{7,1},{8,14},{9,15},{10,... | collective-permute-start | bytes 786440 | tf_op jit(solution)/shard_map/ppermute | solution.py:316
  39.1 17.3 %collective-permute-start.8 = (bf16[128,1024]{1,0:T(8,128)(2,1)S(1)}, bf16[128,1024]{1,0:T(8,128)(2,1)S(1)}, u32[]{:S(2)}, u32[]{:S(2)}) collective-permute-start(bf16[128,1024]{1,0:T(8,128)(2,1)S(1)} %filter.15), channel_id=1, source_target_pairs={{0,3},{1,2},{2,1},{3,0},{4,7},{5,6},{6,5},{7,4},{8,11},{9,10},{10,... | collective-permute-start | bytes 786440 | tf_op jit(solution)/shard_map/ppermute | solution.py:316

commit v3 on v2

--- a/solution.py
+++ b/solution.py
@@ -13,6 +13,7 @@
 VMEM = pl.BlockSpec(memory_space=pltpu.VMEM)
 SMEM = pl.BlockSpec(memory_space=pltpu.SMEM)
 HBM = pl.BlockSpec(memory_space=pltpu.HBM)
+ANY = pl.BlockSpec(memory_space=pl.ANY)
 SIZE = 1024
 ORDER = (4, 2, 5, 7, 6, 1, 3)
 EARLY = (0, 4, 2, 5, 7, 1)
@@ -64,7 +65,7 @@
     )(phases, coherence)
 
 
-def bands_kernel(taps_ref, high_ref, low_ref):
+def bands_kernel(taps_ref, _, high_ref, low_ref):
     place = lax.broadcasted_iota(jnp.int32, (2 * LANES, LANES), 0)
     place = jnp.where(place >= LANES + 64, place - 2 * LANES, place)
     tap = place - lax.broadcasted_iota(jnp.int32, (2 * LANES, LANES), 1) + 2
@@ -76,10 +77,10 @@
         high_ref[:, a * LANES : (a + 1) * LANES] = high
         low_ref[:, a * LANES : (a + 1) * LANES] = (band - high.astype(F32)).astype(BF16)
 
-def bands(taps):
+def bands(taps, after):
     shape = jax.ShapeDtypeStruct((2 * LANES, 3 * LANES), BF16)
-    return pl.pallas_call(bands_kernel, in_specs=[SMEM], out_specs=[VMEM, VMEM], out_shape=[shape, shape],
-        compiler_params=params(), cost_estimate=cost(3e8, 1e5), name="bands")(taps)
+    return pl.pallas_call(bands_kernel, in_specs=[SMEM, ANY], out_specs=[VMEM, VMEM], out_shape=[shape, shape],
+        compiler_params=params(), cost_estimate=cost(3e8,1e5), name="bands")(taps, after)
 
 
 def expand_kernel(left_ref, right_ref, phase_out, coh_out):
@@ -93,7 +94,7 @@
 def expand(left, right):
     shape = jax.ShapeDtypeStruct((4, 32, 8, LANES), BF16)
     out = pl.pallas_call(expand_kernel, in_specs=[VMEM, VMEM], out_specs=[VMEM, VMEM], out_shape=[shape, shape],
-        compiler_params=params(), cost_estimate=cost(5e8, 1e5), name="expand")(left, right)
+        compiler_params=params(), cost_estimate=cost(5e8,1e5), name="expand")(left, right)
     return [o.reshape(128, 8, LANES) for o in out]
 
 
@@ -154,7 +155,7 @@
         out_shape=jax.ShapeDtypeStruct((count, rows * LANES), BF16),
         scratch_shapes=[pltpu.VMEM((count * rows, LANES), F32)],
         compiler_params=params(),
-        cost_estimate=cost(1.5e9, 1e6),
+        cost_estimate=cost(3e8,1e5),
         name="filter",
     )(me, *bands, phases, coherence, phase_edge, coh_edge)
 
@@ -195,7 +196,7 @@
         ],
         scratch_shapes=[pltpu.VMEM((count, dates), BF16)],
         compiler_params=params(),
-        cost_estimate=cost(2e9, 1e6),
+        cost_estimate=cost(2e9,1e6),
         name="network",
     )(date_pairs.T, triplets.T)
 
@@ -230,7 +231,7 @@
         out_specs=VMEM,
         out_shape=jax.ShapeDtypeStruct((rows, width), F32),
         compiler_params=params(),
-        cost_estimate=cost(2e9, 1e6),
+        cost_estimate=cost(5e8,1e5),
         name="early_sum",
     )(me, inverse, member, *pieces)
 
@@ -294,7 +295,7 @@
             pltpu.SemaphoreType.DMA(((dates + triplet_count) // 128,)),
         ],
         compiler_params=params(),
-        cost_estimate=cost(3e9, 2e6),
+        cost_estimate=cost(3e9,2e6),
         name="late_sum",
     )(me, inverse, member, dates_matrix, total, *pieces)
 
@@ -307,8 +308,8 @@
     to_left, to_right = pack_edges(phases, coherence)
     left = lax.ppermute(to_right, "img", [(i, i + 1) for i in range(size - 1)])
     right = lax.ppermute(to_left, "img", [(i + 1, i) for i in range(size - 1)])
-    tap_bands = bands(kernel_taps)
     member, dates_matrix = network(date_pairs, triplets, inverse.shape[0])
+    tap_bands = bands(kernel_taps, dates_matrix)
     edges = expand(left, right)
     pieces = {}
     for step in ORDER:

time: 59.1 us -> 54.9 us (0.929)
  starting transfers between devices: 25.8 us -> 21.2 us
  waiting for transfers between devices: 10.2 us -> 10.8 us
    ppermute x7, starting transfers between devices: 20.3 us -> 15.6 us  [per_device(): lax.ppermute(block, 'ifg', [(i, i ^ step) for i in range(peers)])]
  transfers between devices with their start and end apart: 9 -> 9, of which waited for: 3 -> 3; matrix products, arithmetic and copies ran while one was open for 0% -> 0% of each run, Pallas kernels for 15% -> 27%
where the time goes in v3:
time: 54.9 us; the launch traced here: 54.6 us
  starting transfers between devices  21.2 us (39%)
  Pallas kernels  21 us (38%)
  waiting for transfers between devices  10.8 us (20%)
  between operations  0.98 us (2%)
  local copies, waits for them, and re-layouts  0.61 us (1%)
    ppermute x7, starting transfers between devices, per_device(): lax.ppermute(block, 'ifg', [(i, i ^ step) for i in range(peers)])  15.6 us
    pallas_call x8, Pallas kernels, filter_block(): pl.pallas_call(functools.partial(filter_kernel, step, SIZE), in_specs=[SM...  12.7 us
    ppermute x7, waiting for transfers between devices, per_device(): lax.ppermute(block, 'ifg', [(i, i ^ step) for i in range(peers)])  10.8 us
    ppermute x1, starting transfers between devices, per_device(): right = lax.ppermute(to_left, 'img', [(i + 1, i) for i in range(size - 1)])  3.64 us
    pallas_call x1, Pallas kernels, late_sum(): pl.pallas_call(functools.partial(late_kernel, steps), in_specs=[SMEM] + [...  2.18 us
    pallas_call x1, Pallas kernels, pack_edges(): pl.pallas_call(pack_kernel, in_specs=[HBM, HBM], out_specs=[VMEM, VMEM],...  2.15 us
    ppermute x1, starting transfers between devices, per_device(): left = lax.ppermute(to_right, 'img', [(i, i + 1) for i in range(size - 1)])  1.92 us
    pallas_call x1, Pallas kernels, network(): pl.pallas_call(network_kernel, in_specs=[VMEM, VMEM], out_specs=[VMEM, VM...  1.65 us
  transfers between devices with their start and end apart: 9, of which 3 were waited for; matrix products, arithmetic and copies ran while one was open for 0% of the time, Pallas kernels for 27%

profile of v3, /device:TPU:10, one launch (start us, length us, event | category | flops | bytes accessed | tf_op | source)
XLA Modules:
  0.0 54.6 jit_solution(4459260917929922407)
XLA Ops:
  0.6 2.2 %pack_edges.1 = (bf16[2,4,8,128]{3,2,1,0:T(8,128)(2,1)}, bf16[2,4,8,128]{3,2,1,0:T(8,128)(2,1)}) custom-call(bf16[128,8,1024]{2,1,0:T(8,128)(2,1)} %phase_ref.15, bf16[128,8,1024]{2,1,0:T(8,128)(2,1)} %coh_ref.15), custom_call_target="tpu_custom_call" | custom-call | flops 300000000 | bytes 1000000 | tf_op jit(solution)/shard_map/pack_edges/pallas_call | solution.py:56
  2.8 1.9 %collective-permute-start = (bf16[2,4,8,128]{3,2,1,0:T(8,128)(2,1)}, bf16[2,4,8,128]{3,2,1,0:T(8,128)(2,1)S(1)}, u32[]{:S(2)}, u32[]{:S(2)}) collective-permute-start(bf16[2,4,8,128]{3,2,1,0:T(8,128)(2,1)} %get-tuple-element.14), channel_id=1, source_target_pairs={{0,8},{8,16},{16,24},{24,32},{32,40},{40,48},{48,56},{56,64},{64,7... | collective-permute-start | bytes 49160 | tf_op jit(solution)/shard_map/ppermute | solution.py:309
  4.7 3.6 %collective-permute-start.1 = (bf16[2,4,8,128]{3,2,1,0:T(8,128)(2,1)}, bf16[2,4,8,128]{3,2,1,0:T(8,128)(2,1)S(1)}, u32[]{:S(2)}, u32[]{:S(2)}) collective-permute-start(bf16[2,4,8,128]{3,2,1,0:T(8,128)(2,1)} %get-tuple-element.15), channel_id=1, source_target_pairs={{8,0},{16,8},{24,16},{32,24},{40,32},{48,40},{56,48},{64,56},{72,6... | collective-permute-start | bytes 49160 | tf_op jit(solution)/shard_map/ppermute | solution.py:310
  8.4 0.0 copy-start.5
  8.4 0.0 copy-start.1
  8.4 1.7 %network.1 = (bf16[512,1024]{1,0:T(8,128)(2,1)S(1)}, bf16[512,256]{1,0:T(8,128)(2,1)S(1)}) custom-call(s32[2,1024]{1,0:T(2,128)S(1)} %bitcast.21, s32[3,512]{1,0:T(4,128)S(1)} %bitcast.22), custom_call_target="tpu_custom_call" | custom-call | flops 2000000000 | bytes 1000000 | tf_op jit(solution)/shard_map/network/pallas_call | solution.py:189
  10.1 0.0 copy-start
  10.1 0.7 %bands.1 = (bf16[256,384]{1,0:T(8,128)(2,1)S(1)}, bf16[256,384]{1,0:T(8,128)(2,1)S(1)}) custom-call(f32[3,5]{1,0:T(4,128)S(1)} %copy-done.5, bf16[512,256]{1,0:T(8,128)(2,1)S(1)} %get-tuple-element.11._.dates_ref), custom_call_target="tpu_custom_call" | custom-call | flops 300000000 | bytes 100000 | tf_op jit(solution)/shard_map/bands/pallas_call | solution.py:82
  10.9 0.0 collective-permute-done.1.right_ref
  10.9 0.2 expand.1
  11.1 0.6 %copy-done = bf16[128,8,1024]{2,1,0:T(8,128)(2,1)S(1)} copy-done((bf16[128,8,1024]{2,1,0:T(8,128)(2,1)S(1)}, bf16[128,8,1024]{2,1,0:T(8,128)(2,1)}, u32[]{:S(2)}) %copy-start) | copy-done | bytes 2097176
  11.7 1.6 %filter.9 = bf16[128,1024]{1,0:T(8,128)(2,1)S(1)} custom-call(s32[1]{0:T(128)} %bitcast.me_ref, bf16[256,384]{1,0:T(8,128)(2,1)S(1)} %get-tuple-element.12.high_ref, bf16[256,384]{1,0:T(8,128)(2,1)S(1)} %get-tuple-element.13.low_ref, bf16[128,8,1024]{2,1,0:T(8,128)(2,1)S(1)} %copy-done, bf16[128,8,1024]{2,1,0:T(8,128)(2,1)S(1)} %copy-done.1, ...), custom_call_target="tpu_custom_call" | custom-call | flops 300000000 | bytes 100000 | tf_op jit(solution)/shard_map/filter/pallas_call | solution.py:151
  13.3 2.2 %collective-permute-start.2 = (bf16[128,1024]{1,0:T(8,128)(2,1)S(1)}, bf16[128,1024]{1,0:T(8,128)(2,1)S(1)}, u32[]{:S(2)}, u32[]{:S(2)}) collective-permute-start(bf16[128,1024]{1,0:T(8,128)(2,1)S(1)} %filter.9), channel_id=1, source_target_pairs={{0,4},{1,5},{2,6},{3,7},{4,0},{5,1},{6,2},{7,3},{8,12},{9,13},{10,... | collective-permute-start | bytes 786440 | tf_op jit(solution)/shard_map/ppermute | solution.py:317
  15.5 1.6 %filter.10 = bf16[128,1024]{1,0:T(8,128)(2,1)S(1)} custom-call(s32[1]{0:T(128)} %bitcast.me_ref, bf16[256,384]{1,0:T(8,128)(2,1)S(1)} %get-tuple-element.12.high_ref, bf16[256,384]{1,0:T(8,128)(2,1)S(1)} %get-tuple-element.13.low_ref, bf16[128,8,1024]{2,1,0:T(8,128)(2,1)S(1)} %copy-done, bf16[128,8,1024]{2,1,0:T(8,128)(2,1)S(1)} %copy-done.1, ...), custom_call_target="tpu_custom_call" | custom-call | flops 300000000 | bytes 100000 | tf_op jit(solution)/shard_map/filter/pallas_call | solution.py:151
  17.1 4.0 %collective-permute-start.3 = (bf16[128,1024]{1,0:T(8,128)(2,1)S(1)}, bf16[128,1024]{1,0:T(8,128)(2,1)S(1)}, u32[]{:S(2)}, u32[]{:S(2)}) collective-permute-start(bf16[128,1024]{1,0:T(8,128)(2,1)S(1)} %filter.10), channel_id=1, source_target_pairs={{0,2},{1,3},{2,0},{3,1},{4,6},{5,7},{6,4},{7,5},{8,10},{9,11},{10,... | collective-permute-start | bytes 786440 | tf_op jit(solution)/shard_map/ppermute | solution.py:317
  21.0 1.6 %filter.11 = bf16[128,1024]{1,0:T(8,128)(2,1)S(1)} custom-call(s32[1]{0:T(128)} %bitcast.me_ref, bf16[256,384]{1,0:T(8,128)(2,1)S(1)} %get-tuple-element.12.high_ref, bf16[256,384]{1,0:T(8,128)(2,1)S(1)} %get-tuple-element.13.low_ref, bf16[128,8,1024]{2,1,0:T(8,128)(2,1)S(1)} %copy-done, bf16[128,8,1024]{2,1,0:T(8,128)(2,1)S(1)} %copy-done.1, ...), custom_call_target="tpu_custom_call" | custom-call | flops 300000000 | bytes 100000 | tf_op jit(solution)/shard_map/filter/pallas_call | solution.py:151
  22.6 1.9 %collective-permute-start.4 = (bf16[128,1024]{1,0:T(8,128)(2,1)S(1)}, bf16[128,1024]{1,0:T(8,128)(2,1)S(1)}, u32[]{:S(2)}, u32[]{:S(2)}) collective-permute-start(bf16[128,1024]{1,0:T(8,128)(2,1)S(1)} %filter.11), channel_id=1, source_target_pairs={{0,5},{1,4},{2,7},{3,6},{4,1},{5,0},{6,3},{7,2},{8,13},{9,12},{10,... | collective-permute-start | bytes 786440 | tf_op jit(solution)/shard_map/ppermute | solution.py:317
  24.5 1.6 %filter.12 = bf16[128,1024]{1,0:T(8,128)(2,1)S(1)} custom-call(s32[1]{0:T(128)} %bitcast.me_ref, bf16[256,384]{1,0:T(8,128)(2,1)S(1)} %get-tuple-element.12.high_ref, bf16[256,384]{1,0:T(8,128)(2,1)S(1)} %get-tuple-element.13.low_ref, bf16[128,8,1024]{2,1,0:T(8,128)(2,1)S(1)} %copy-done, bf16[128,8,1024]{2,1,0:T(8,128)(2,1)S(1)} %copy-done.1, ...), custom_call_target="tpu_custom_call" | custom-call | flops 300000000 | bytes 100000 | tf_op jit(solution)/shard_map/filter/pallas_call | solution.py:151
  26.1 1.2 %collective-permute-start.5 = (bf16[128,1024]{1,0:T(8,128)(2,1)S(1)}, bf16[128,1024]{1,0:T(8,128)(2,1)S(1)}, u32[]{:S(2)}, u32[]{:S(2)}) collective-permute-start(bf16[128,1024]{1,0:T(8,128)(2,1)S(1)} %filter.12), channel_id=1, source_target_pairs={{0,7},{1,6},{2,5},{3,4},{4,3},{5,2},{6,1},{7,0},{8,15},{9,14},{10,... | collective-permute-start | bytes 786440 | tf_op jit(solution)/shard_map/ppermute | solution.py:317
  27.3 1.6 %filter.13 = bf16[128,1024]{1,0:T(8,128)(2,1)S(1)} custom-call(s32[1]{0:T(128)} %bitcast.me_ref, bf16[256,384]{1,0:T(8,128)(2,1)S(1)} %get-tuple-element.12.high_ref, bf16[256,384]{1,0:T(8,128)(2,1)S(1)} %get-tuple-element.13.low_ref, bf16[128,8,1024]{2,1,0:T(8,128)(2,1)S(1)} %copy-done, bf16[128,8,1024]{2,1,0:T(8,128)(2,1)S(1)} %copy-done.1, ...), custom_call_target="tpu_custom_call" | custom-call | flops 300000000 | bytes 100000 | tf_op jit(solution)/shard_map/filter/pallas_call | solution.py:151
  28.9 1.8 %collective-permute-start.6 = (bf16[128,1024]{1,0:T(8,128)(2,1)S(1)}, bf16[128,1024]{1,0:T(8,128)(2,1)S(1)}, u32[]{:S(2)}, u32[]{:S(2)}) collective-permute-start(bf16[128,1024]{1,0:T(8,128)(2,1)S(1)} %filter.13), channel_id=1, source_target_pairs={{0,1},{1,0},{2,3},{3,2},{4,5},{5,4},{6,7},{7,6},{8,9},{9,8},{10,11... | collective-permute-start | bytes 786440 | tf_op jit(solution)/shard_map/ppermute | solution.py:317
  30.7 1.6 %filter.15 = bf16[128,1024]{1,0:T(8,128)(2,1)S(1)} custom-call(s32[1]{0:T(128)} %bitcast.me_ref, bf16[256,384]{1,0:T(8,128)(2,1)S(1)} %get-tuple-element.12.high_ref, bf16[256,384]{1,0:T(8,128)(2,1)S(1)} %get-tuple-element.13.low_ref, bf16[128,8,1024]{2,1,0:T(8,128)(2,1)S(1)} %copy-done, bf16[128,8,1024]{2,1,0:T(8,128)(2,1)S(1)} %copy-done.1, ...), custom_call_target="tpu_custom_call" | custom-call | flops 300000000 | bytes 100000 | tf_op jit(solution)/shard_map/filter/pallas_call | solution.py:151
  32.3 1.6 %filter.14 = bf16[128,1024]{1,0:T(8,128)(2,1)S(1)} custom-call(s32[1]{0:T(128)} %bitcast.me_ref, bf16[256,384]{1,0:T(8,128)(2,1)S(1)} %get-tuple-element.12.high_ref, bf16[256,384]{1,0:T(8,128)(2,1)S(1)} %get-tuple-element.13.low_ref, bf16[128,8,1024]{2,1,0:T(8,128)(2,1)S(1)} %copy-done, bf16[128,8,1024]{2,1,0:T(8,128)(2,1)S(1)} %copy-done.1, ...), custom_call_target="tpu_custom_call" | custom-call | flops 300000000 | bytes 100000 | tf_op jit(solution)/shard_map/filter/pallas_call | solution.py:151
  33.9 0.0 copy-start.2
  33.9 0.0 collective-permute-done.2.refs_1_
  33.9 4.5 %collective-permute-start.7 = (bf16[128,1024]{1,0:T(8,128)(2,1)S(1)}, bf16[128,1024]{1,0:T(8,128)(2,1)S(1)}, u32[]{:S(2)}, u32[]{:S(2)}) collective-permute-start(bf16[128,1024]{1,0:T(8,128)(2,1)S(1)} %filter.14), channel_id=1, source_target_pairs={{0,6},{1,7},{2,4},{3,5},{4,2},{5,3},{6,0},{7,1},{8,14},{9,15},{10,... | collective-permute-start | bytes 786440 | tf_op jit(solution)/shard_map/ppermute | solution.py:317
  38.4 1.6 %filter.8.refs_0_ = bf16[128,1024]{1,0:T(8,128)(2,1)S(1)} custom-call(s32[1]{0:T(128)} %bitcast.me_ref, bf16[256,384]{1,0:T(8,128)(2,1)S(1)} %get-tuple-element.12.high_ref, bf16[256,384]{1,0:T(8,128)(2,1)S(1)} %get-tuple-element.13.low_ref, bf16[128,8,1024]{2,1,0:T(8,128)(2,1)S(1)} %copy-done, bf16[128,8,1024]{2,1,0:T(8,128)(2,1)S(1)} %copy-done.1, ...), custom_call_target="tpu_custom_call" | custom-call | flops 300000000 | bytes 100000 | tf_op jit(solution)/shard_map/filter/pallas_call | solution.py:151
  40.0 0.3 collective-permute-done.6.refs_5_
  40.3 1.4 %early_sum.1.total_ref = f32[768,1024]{1,0:T(8,128)S(1)} custom-call(s32[1]{0:T(128)} %bitcast.me_ref, bf16[256,1024]{1,0:T(8,128)(2,1)S(1)} %copy-done.2, bf16[512,1024]{1,0:T(8,128)(2,1)S(1)} %get-tuple-element.10.member_ref, bf16[128,1024]{1,0:T(8,128)(2,1)S(1)} %filter.8.refs_0_, bf16[128,1024]{1,0:T(8,128)(2,1)S(1)} %collective-permute-done.2.refs_1_, ...), custom_call_target="tpu_custom_call" | custom-call | flops 500000000 | bytes 100000 | tf_op jit(solution)/shard_map/early_sum/pallas_call | solution.py:228
  41.7 5.0 %collective-permute-done.7.refs_0_ = bf16[128,1024]{1,0:T(8,128)(2,1)S(1)} collective-permute-done((bf16[128,1024]{1,0:T(8,128)(2,1)S(1)}, bf16[128,1024]{1,0:T(8,128)(2,1)S(1)}, u32[]{:S(2)}, u32[]{:S(2)}) %collective-permute-start.7) | collective-permute-done | bytes 262176 | tf_op jit(solution)/shard_map/ppermute | solution.py:317
  46.7 5.5 %collective-permute-done.8.refs_1_ = bf16[128,1024]{1,0:T(8,128)(2,1)S(1)} collective-permute-done((bf16[128,1024]{1,0:T(8,128)(2,1)S(1)}, bf16[128,1024]{1,0:T(8,128)(2,1)S(1)}, u32[]{:S(2)}, u32[]{:S(2)}) %collective-permute-start.8) | collective-permute-done | bytes 262176 | tf_op jit(solution)/shard_map/ppermute | solution.py:317
  52.2 2.2 %late_sum.1 = (bf16[256,8,128]{2,1,0:T(8,128)(2,1)}, bf16[512,8,128]{2,1,0:T(8,128)(2,1)}) custom-call(s32[1]{0:T(128)} %bitcast.me_ref, bf16[256,1024]{1,0:T(8,128)(2,1)S(1)} %copy-done.2, bf16[512,1024]{1,0:T(8,128)(2,1)S(1)} %get-tuple-element.10.member_ref, bf16[512,256]{1,0:T(8,128)(2,1)S(1)} %get-tuple-element.11._.dates_ref, ...), custom_call_target="tpu_custom_call" | custom-call | flops 3000000000 | bytes 2000000 | tf_op jit(solution)/shard_map/late_sum/pallas_call | solution.py:285
  (12 shorter events, 0.0 us)
Async XLA Ops:
  0.6 7.8 %copy-start.4 = (s32[512,3]{0,1:T(4,128)S(1)}, s32[512,3]{0,1:T(4,128)}, u32[]{:S(2)}) copy-start(s32[512,3]{0,1:T(4,128)} %param.11) | copy-start | bytes 18436
  0.6 7.8 %copy-start.3 = (s32[1024,2]{0,1:T(2,128)S(1)}, s32[1024,2]{0,1:T(2,128)}, u32[]{:S(2)}) copy-start(s32[1024,2]{0,1:T(2,128)} %param.10) | copy-start | bytes 24580
  2.8 8.1 %collective-permute-start = (bf16[2,4,8,128]{3,2,1,0:T(8,128)(2,1)}, bf16[2,4,8,128]{3,2,1,0:T(8,128)(2,1)S(1)}, u32[]{:S(2)}, u32[]{:S(2)}) collective-permute-start(bf16[2,4,8,128]{3,2,1,0:T(8,128)(2,1)} %get-tuple-element.14), channel_id=1, source_target_pairs={{0,8},{8,16},{16,24},{24,32},{32,40},{40,48},{48,56},{56,64},{64,7... | collective-permute-start | bytes 49160 | tf_op jit(solution)/shard_map/ppermute | solution.py:309
  4.7 6.1 %collective-permute-start.1 = (bf16[2,4,8,128]{3,2,1,0:T(8,128)(2,1)}, bf16[2,4,8,128]{3,2,1,0:T(8,128)(2,1)S(1)}, u32[]{:S(2)}, u32[]{:S(2)}) collective-permute-start(bf16[2,4,8,128]{3,2,1,0:T(8,128)(2,1)} %get-tuple-element.15), channel_id=1, source_target_pairs={{8,0},{16,8},{24,16},{32,24},{40,32},{48,40},{56,48},{64,56},{72,6... | collective-permute-start | bytes 49160 | tf_op jit(solution)/shard_map/ppermute | solution.py:310
  8.4 1.7 %copy-start.5 = (f32[3,5]{1,0:T(4,128)S(1)}, f32[3,5]{1,0:T(4,128)}, u32[]{:S(2)}) copy-start(f32[3,5]{1,0:T(4,128)} %taps_ref.1) | copy-start | bytes 184
  8.4 2.7 %copy-start.1 = (bf16[128,8,1024]{2,1,0:T(8,128)(2,1)S(1)}, bf16[128,8,1024]{2,1,0:T(8,128)(2,1)}, u32[]{:S(2)}) copy-start(bf16[128,8,1024]{2,1,0:T(8,128)(2,1)} %coh_ref.15) | copy-start | bytes 6291460
  10.1 1.6 %copy-start = (bf16[128,8,1024]{2,1,0:T(8,128)(2,1)S(1)}, bf16[128,8,1024]{2,1,0:T(8,128)(2,1)}, u32[]{:S(2)}) copy-start(bf16[128,8,1024]{2,1,0:T(8,128)(2,1)} %phase_ref.15) | copy-start | bytes 6291460
  13.3 20.7 %collective-permute-start.2 = (bf16[128,1024]{1,0:T(8,128)(2,1)S(1)}, bf16[128,1024]{1,0:T(8,128)(2,1)S(1)}, u32[]{:S(2)}, u32[]{:S(2)}) collective-permute-start(bf16[128,1024]{1,0:T(8,128)(2,1)S(1)} %filter.9), channel_id=1, source_target_pairs={{0,4},{1,5},{2,6},{3,7},{4,0},{5,1},{6,2},{7,3},{8,12},{9,13},{10,... | collective-permute-start | bytes 786440 | tf_op jit(solution)/shard_map/ppermute | solution.py:317
  17.1 21.3 %collective-permute-start.3 = (bf16[128,1024]{1,0:T(8,128)(2,1)S(1)}, bf16[128,1024]{1,0:T(8,128)(2,1)S(1)}, u32[]{:S(2)}, u32[]{:S(2)}) collective-permute-start(bf16[128,1024]{1,0:T(8,128)(2,1)S(1)} %filter.10), channel_id=1, source_target_pairs={{0,2},{1,3},{2,0},{3,1},{4,6},{5,7},{6,4},{7,5},{8,10},{9,11},{10,... | collective-permute-start | bytes 786440 | tf_op jit(solution)/shard_map/ppermute | solution.py:317
  22.6 17.4 %collective-permute-start.4 = (bf16[128,1024]{1,0:T(8,128)(2,1)S(1)}, bf16[128,1024]{1,0:T(8,128)(2,1)S(1)}, u32[]{:S(2)}, u32[]{:S(2)}) collective-permute-start(bf16[128,1024]{1,0:T(8,128)(2,1)S(1)} %filter.11), channel_id=1, source_target_pairs={{0,5},{1,4},{2,7},{3,6},{4,1},{5,0},{6,3},{7,2},{8,13},{9,12},{10,... | collective-permute-start | bytes 786440 | tf_op jit(solution)/shard_map/ppermute | solution.py:317
  26.1 13.9 %collective-permute-start.5 = (bf16[128,1024]{1,0:T(8,128)(2,1)S(1)}, bf16[128,1024]{1,0:T(8,128)(2,1)S(1)}, u32[]{:S(2)}, u32[]{:S(2)}) collective-permute-start(bf16[128,1024]{1,0:T(8,128)(2,1)S(1)} %filter.12), channel_id=1, source_target_pairs={{0,7},{1,6},{2,5},{3,4},{4,3},{5,2},{6,1},{7,0},{8,15},{9,14},{10,... | collective-permute-start | bytes 786440 | tf_op jit(solution)/shard_map/ppermute | solution.py:317
  28.9 11.4 %collective-permute-start.6 = (bf16[128,1024]{1,0:T(8,128)(2,1)S(1)}, bf16[128,1024]{1,0:T(8,128)(2,1)S(1)}, u32[]{:S(2)}, u32[]{:S(2)}) collective-permute-start(bf16[128,1024]{1,0:T(8,128)(2,1)S(1)} %filter.13), channel_id=1, source_target_pairs={{0,1},{1,0},{2,3},{3,2},{4,5},{5,4},{6,7},{7,6},{8,9},{9,8},{10,11... | collective-permute-start | bytes 786440 | tf_op jit(solution)/shard_map/ppermute | solution.py:317
  33.9 6.4 %copy-start.2 = (bf16[256,1024]{1,0:T(8,128)(2,1)S(1)}, bf16[256,1024]{1,0:T(8,128)(2,1)}, u32[]{:S(2)}) copy-start(bf16[256,1024]{1,0:T(8,128)(2,1)} %inverse_ref.3) | copy-start | bytes 1572868
  33.9 12.8 %collective-permute-start.7 = (bf16[128,1024]{1,0:T(8,128)(2,1)S(1)}, bf16[128,1024]{1,0:T(8,128)(2,1)S(1)}, u32[]{:S(2)}, u32[]{:S(2)}) collective-permute-start(bf16[128,1024]{1,0:T(8,128)(2,1)S(1)} %filter.14), channel_id=1, source_target_pairs={{0,6},{1,7},{2,4},{3,5},{4,2},{5,3},{6,0},{7,1},{8,14},{9,15},{10,... | collective-permute-start | bytes 786440 | tf_op jit(solution)/shard_map/ppermute | solution.py:317
  38.4 13.8 %collective-permute-start.8 = (bf16[128,1024]{1,0:T(8,128)(2,1)S(1)}, bf16[128,1024]{1,0:T(8,128)(2,1)S(1)}, u32[]{:S(2)}, u32[]{:S(2)}) collective-permute-start(bf16[128,1024]{1,0:T(8,128)(2,1)S(1)} %filter.15), channel_id=1, source_target_pairs={{0,3},{1,2},{2,1},{3,0},{4,7},{5,6},{6,5},{7,4},{8,11},{9,10},{10,... | collective-permute-start | bytes 786440 | tf_op jit(solution)/shard_map/ppermute | solution.py:317

commit v4 on v3

--- a/solution.py
+++ b/solution.py
@@ -15,9 +15,9 @@
 HBM = pl.BlockSpec(memory_space=pltpu.HBM)
 ANY = pl.BlockSpec(memory_space=pl.ANY)
 SIZE = 1024
-ORDER = (4, 2, 5, 7, 6, 1, 3)
-EARLY = (0, 4, 2, 5, 7, 1)
-LATE = (6, 3)
+ORDER = (6, 5, 3, 7, 1, 4, 2)
+EARLY = (0, 6, 5, 3, 7, 1)
+LATE = (4, 2)
 
 
 def cost(flops, nbytes):

time: 54.9 us -> 49.2 us (0.90)
  waiting for transfers between devices: 10.8 us -> 4.95 us
    ppermute x7, waiting for transfers between devices: 10.8 us -> 4.94 us  [per_device(): lax.ppermute(block, 'ifg', [(i, i ^ step) for i in range(peers)])]
  transfers between devices with their start and end apart: 9 -> 9, of which waited for: 3 -> 3; matrix products, arithmetic and copies ran while one was open for 0% -> 0% of each run, Pallas kernels for 27% -> 31%
where the time goes in v4:
time: 49.2 us; the launch traced here: 48.8 us
  starting transfers between devices  21.2 us (43%)
  Pallas kernels  21 us (43%)
  waiting for transfers between devices  4.95 us (10%)
  between operations  1 us (2%)
  local copies, waits for them, and re-layouts  0.61 us (1%)
    ppermute x7, starting transfers between devices, per_device(): lax.ppermute(block, 'ifg', [(i, i ^ step) for i in range(peers)])  15.6 us
    pallas_call x8, Pallas kernels, filter_block(): pl.pallas_call(functools.partial(filter_kernel, step, SIZE), in_specs=[SM...  12.7 us
    ppermute x7, waiting for transfers between devices, per_device(): lax.ppermute(block, 'ifg', [(i, i ^ step) for i in range(peers)])  4.94 us
    ppermute x1, starting transfers between devices, per_device(): right = lax.ppermute(to_left, 'img', [(i + 1, i) for i in range(size - 1)])  3.64 us
    pallas_call x1, Pallas kernels, late_sum(): pl.pallas_call(functools.partial(late_kernel, steps), in_specs=[SMEM] + [...  2.2 us
    pallas_call x1, Pallas kernels, pack_edges(): pl.pallas_call(pack_kernel, in_specs=[HBM, HBM], out_specs=[VMEM, VMEM],...  2.15 us
    ppermute x1, starting transfers between devices, per_device(): left = lax.ppermute(to_right, 'img', [(i, i + 1) for i in range(size - 1)])  1.92 us
    pallas_call x1, Pallas kernels, network(): pl.pallas_call(network_kernel, in_specs=[VMEM, VMEM], out_specs=[VMEM, VM...  1.65 us
  transfers between devices with their start and end apart: 9, of which 3 were waited for; matrix products, arithmetic and copies ran while one was open for 0% of the time, Pallas kernels for 31%

profile of v4, /device:TPU:10, one launch (start us, length us, event | category | flops | bytes accessed | tf_op | source)
XLA Modules:
  0.0 48.8 jit_solution(5257625405214614040)
XLA Ops:
  0.6 2.2 %pack_edges.1 = (bf16[2,4,8,128]{3,2,1,0:T(8,128)(2,1)}, bf16[2,4,8,128]{3,2,1,0:T(8,128)(2,1)}) custom-call(bf16[128,8,1024]{2,1,0:T(8,128)(2,1)} %phase_ref.15, bf16[128,8,1024]{2,1,0:T(8,128)(2,1)} %coh_ref.15), custom_call_target="tpu_custom_call" | custom-call | flops 300000000 | bytes 1000000 | tf_op jit(solution)/shard_map/pack_edges/pallas_call | solution.py:56
  2.8 1.9 %collective-permute-start = (bf16[2,4,8,128]{3,2,1,0:T(8,128)(2,1)}, bf16[2,4,8,128]{3,2,1,0:T(8,128)(2,1)S(1)}, u32[]{:S(2)}, u32[]{:S(2)}) collective-permute-start(bf16[2,4,8,128]{3,2,1,0:T(8,128)(2,1)} %get-tuple-element.14), channel_id=1, source_target_pairs={{0,8},{8,16},{16,24},{24,32},{32,40},{40,48},{48,56},{56,64},{64,7... | collective-permute-start | bytes 49160 | tf_op jit(solution)/shard_map/ppermute | solution.py:309
  4.7 3.6 %collective-permute-start.1 = (bf16[2,4,8,128]{3,2,1,0:T(8,128)(2,1)}, bf16[2,4,8,128]{3,2,1,0:T(8,128)(2,1)S(1)}, u32[]{:S(2)}, u32[]{:S(2)}) collective-permute-start(bf16[2,4,8,128]{3,2,1,0:T(8,128)(2,1)} %get-tuple-element.15), channel_id=1, source_target_pairs={{8,0},{16,8},{24,16},{32,24},{40,32},{48,40},{56,48},{64,56},{72,6... | collective-permute-start | bytes 49160 | tf_op jit(solution)/shard_map/ppermute | solution.py:310
  8.4 0.0 copy-start.5
  8.4 0.0 copy-start.1
  8.4 1.7 %network.1 = (bf16[512,1024]{1,0:T(8,128)(2,1)S(1)}, bf16[512,256]{1,0:T(8,128)(2,1)S(1)}) custom-call(s32[2,1024]{1,0:T(2,128)S(1)} %bitcast.21, s32[3,512]{1,0:T(4,128)S(1)} %bitcast.22), custom_call_target="tpu_custom_call" | custom-call | flops 2000000000 | bytes 1000000 | tf_op jit(solution)/shard_map/network/pallas_call | solution.py:189
  10.1 0.0 copy-start
  10.1 0.7 %bands.1 = (bf16[256,384]{1,0:T(8,128)(2,1)S(1)}, bf16[256,384]{1,0:T(8,128)(2,1)S(1)}) custom-call(f32[3,5]{1,0:T(4,128)S(1)} %copy-done.5, bf16[512,256]{1,0:T(8,128)(2,1)S(1)} %get-tuple-element.11._.dates_ref), custom_call_target="tpu_custom_call" | custom-call | flops 300000000 | bytes 100000 | tf_op jit(solution)/shard_map/bands/pallas_call | solution.py:82
  10.9 0.0 collective-permute-done.1.right_ref
  10.9 0.2 expand.1
  11.1 0.6 %copy-done = bf16[128,8,1024]{2,1,0:T(8,128)(2,1)S(1)} copy-done((bf16[128,8,1024]{2,1,0:T(8,128)(2,1)S(1)}, bf16[128,8,1024]{2,1,0:T(8,128)(2,1)}, u32[]{:S(2)}) %copy-start) | copy-done | bytes 2097176
  11.7 1.6 %filter.9 = bf16[128,1024]{1,0:T(8,128)(2,1)S(1)} custom-call(s32[1]{0:T(128)} %bitcast.me_ref, bf16[256,384]{1,0:T(8,128)(2,1)S(1)} %get-tuple-element.12.high_ref, bf16[256,384]{1,0:T(8,128)(2,1)S(1)} %get-tuple-element.13.low_ref, bf16[128,8,1024]{2,1,0:T(8,128)(2,1)S(1)} %copy-done, bf16[128,8,1024]{2,1,0:T(8,128)(2,1)S(1)} %copy-done.1, ...), custom_call_target="tpu_custom_call" | custom-call | flops 300000000 | bytes 100000 | tf_op jit(solution)/shard_map/filter/pallas_call | solution.py:151
  13.3 5.5 %collective-permute-start.2 = (bf16[128,1024]{1,0:T(8,128)(2,1)S(1)}, bf16[128,1024]{1,0:T(8,128)(2,1)S(1)}, u32[]{:S(2)}, u32[]{:S(2)}) collective-permute-start(bf16[128,1024]{1,0:T(8,128)(2,1)S(1)} %filter.9), channel_id=1, source_target_pairs={{0,6},{1,7},{2,4},{3,5},{4,2},{5,3},{6,0},{7,1},{8,14},{9,15},{10,... | collective-permute-start | bytes 786440 | tf_op jit(solution)/shard_map/ppermute | solution.py:317
  18.8 1.6 %filter.10 = bf16[128,1024]{1,0:T(8,128)(2,1)S(1)} custom-call(s32[1]{0:T(128)} %bitcast.me_ref, bf16[256,384]{1,0:T(8,128)(2,1)S(1)} %get-tuple-element.12.high_ref, bf16[256,384]{1,0:T(8,128)(2,1)S(1)} %get-tuple-element.13.low_ref, bf16[128,8,1024]{2,1,0:T(8,128)(2,1)S(1)} %copy-done, bf16[128,8,1024]{2,1,0:T(8,128)(2,1)S(1)} %copy-done.1, ...), custom_call_target="tpu_custom_call" | custom-call | flops 300000000 | bytes 100000 | tf_op jit(solution)/shard_map/filter/pallas_call | solution.py:151
  20.4 1.9 %collective-permute-start.3 = (bf16[128,1024]{1,0:T(8,128)(2,1)S(1)}, bf16[128,1024]{1,0:T(8,128)(2,1)S(1)}, u32[]{:S(2)}, u32[]{:S(2)}) collective-permute-start(bf16[128,1024]{1,0:T(8,128)(2,1)S(1)} %filter.10), channel_id=1, source_target_pairs={{0,5},{1,4},{2,7},{3,6},{4,1},{5,0},{6,3},{7,2},{8,13},{9,12},{10,... | collective-permute-start | bytes 786440 | tf_op jit(solution)/shard_map/ppermute | solution.py:317
  22.3 1.6 %filter.11 = bf16[128,1024]{1,0:T(8,128)(2,1)S(1)} custom-call(s32[1]{0:T(128)} %bitcast.me_ref, bf16[256,384]{1,0:T(8,128)(2,1)S(1)} %get-tuple-element.12.high_ref, bf16[256,384]{1,0:T(8,128)(2,1)S(1)} %get-tuple-element.13.low_ref, bf16[128,8,1024]{2,1,0:T(8,128)(2,1)S(1)} %copy-done, bf16[128,8,1024]{2,1,0:T(8,128)(2,1)S(1)} %copy-done.1, ...), custom_call_target="tpu_custom_call" | custom-call | flops 300000000 | bytes 100000 | tf_op jit(solution)/shard_map/filter/pallas_call | solution.py:151
  23.9 0.1 collective-permute-start.4
  24.0 1.6 %filter.12 = bf16[128,1024]{1,0:T(8,128)(2,1)S(1)} custom-call(s32[1]{0:T(128)} %bitcast.me_ref, bf16[256,384]{1,0:T(8,128)(2,1)S(1)} %get-tuple-element.12.high_ref, bf16[256,384]{1,0:T(8,128)(2,1)S(1)} %get-tuple-element.13.low_ref, bf16[128,8,1024]{2,1,0:T(8,128)(2,1)S(1)} %copy-done, bf16[128,8,1024]{2,1,0:T(8,128)(2,1)S(1)} %copy-done.1, ...), custom_call_target="tpu_custom_call" | custom-call | flops 300000000 | bytes 100000 | tf_op jit(solution)/shard_map/filter/pallas_call | solution.py:151
  25.6 4.9 %collective-permute-start.5 = (bf16[128,1024]{1,0:T(8,128)(2,1)S(1)}, bf16[128,1024]{1,0:T(8,128)(2,1)S(1)}, u32[]{:S(2)}, u32[]{:S(2)}) collective-permute-start(bf16[128,1024]{1,0:T(8,128)(2,1)S(1)} %filter.12), channel_id=1, source_target_pairs={{0,7},{1,6},{2,5},{3,4},{4,3},{5,2},{6,1},{7,0},{8,15},{9,14},{10,... | collective-permute-start | bytes 786440 | tf_op jit(solution)/shard_map/ppermute | solution.py:317
  30.4 1.6 %filter.13 = bf16[128,1024]{1,0:T(8,128)(2,1)S(1)} custom-call(s32[1]{0:T(128)} %bitcast.me_ref, bf16[256,384]{1,0:T(8,128)(2,1)S(1)} %get-tuple-element.12.high_ref, bf16[256,384]{1,0:T(8,128)(2,1)S(1)} %get-tuple-element.13.low_ref, bf16[128,8,1024]{2,1,0:T(8,128)(2,1)S(1)} %copy-done, bf16[128,8,1024]{2,1,0:T(8,128)(2,1)S(1)} %copy-done.1, ...), custom_call_target="tpu_custom_call" | custom-call | flops 300000000 | bytes 100000 | tf_op jit(solution)/shard_map/filter/pallas_call | solution.py:151
  32.0 0.3 collective-permute-start.6
  32.3 1.6 %filter.15 = bf16[128,1024]{1,0:T(8,128)(2,1)S(1)} custom-call(s32[1]{0:T(128)} %bitcast.me_ref, bf16[256,384]{1,0:T(8,128)(2,1)S(1)} %get-tuple-element.12.high_ref, bf16[256,384]{1,0:T(8,128)(2,1)S(1)} %get-tuple-element.13.low_ref, bf16[128,8,1024]{2,1,0:T(8,128)(2,1)S(1)} %copy-done, bf16[128,8,1024]{2,1,0:T(8,128)(2,1)S(1)} %copy-done.1, ...), custom_call_target="tpu_custom_call" | custom-call | flops 300000000 | bytes 100000 | tf_op jit(solution)/shard_map/filter/pallas_call | solution.py:151
  33.9 1.6 %filter.14 = bf16[128,1024]{1,0:T(8,128)(2,1)S(1)} custom-call(s32[1]{0:T(128)} %bitcast.me_ref, bf16[256,384]{1,0:T(8,128)(2,1)S(1)} %get-tuple-element.12.high_ref, bf16[256,384]{1,0:T(8,128)(2,1)S(1)} %get-tuple-element.13.low_ref, bf16[128,8,1024]{2,1,0:T(8,128)(2,1)S(1)} %copy-done, bf16[128,8,1024]{2,1,0:T(8,128)(2,1)S(1)} %copy-done.1, ...), custom_call_target="tpu_custom_call" | custom-call | flops 300000000 | bytes 100000 | tf_op jit(solution)/shard_map/filter/pallas_call | solution.py:151
  35.5 0.0 copy-start.2
  35.5 1.5 %collective-permute-start.7 = (bf16[128,1024]{1,0:T(8,128)(2,1)S(1)}, bf16[128,1024]{1,0:T(8,128)(2,1)S(1)}, u32[]{:S(2)}, u32[]{:S(2)}) collective-permute-start(bf16[128,1024]{1,0:T(8,128)(2,1)S(1)} %filter.14), channel_id=1, source_target_pairs={{0,4},{1,5},{2,6},{3,7},{4,0},{5,1},{6,2},{7,3},{8,12},{9,13},{10,... | collective-permute-start | bytes 786440 | tf_op jit(solution)/shard_map/ppermute | solution.py:317
  37.0 1.5 %collective-permute-start.8 = (bf16[128,1024]{1,0:T(8,128)(2,1)S(1)}, bf16[128,1024]{1,0:T(8,128)(2,1)S(1)}, u32[]{:S(2)}, u32[]{:S(2)}) collective-permute-start(bf16[128,1024]{1,0:T(8,128)(2,1)S(1)} %filter.15), channel_id=1, source_target_pairs={{0,2},{1,3},{2,0},{3,1},{4,6},{5,7},{6,4},{7,5},{8,10},{9,11},{10,... | collective-permute-start | bytes 786440 | tf_op jit(solution)/shard_map/ppermute | solution.py:317
  38.4 1.6 %filter.8.refs_0_ = bf16[128,1024]{1,0:T(8,128)(2,1)S(1)} custom-call(s32[1]{0:T(128)} %bitcast.me_ref, bf16[256,384]{1,0:T(8,128)(2,1)S(1)} %get-tuple-element.12.high_ref, bf16[256,384]{1,0:T(8,128)(2,1)S(1)} %get-tuple-element.13.low_ref, bf16[128,8,1024]{2,1,0:T(8,128)(2,1)S(1)} %copy-done, bf16[128,8,1024]{2,1,0:T(8,128)(2,1)S(1)} %copy-done.1, ...), custom_call_target="tpu_custom_call" | custom-call | flops 300000000 | bytes 100000 | tf_op jit(solution)/shard_map/filter/pallas_call | solution.py:151
  40.0 1.4 %collective-permute-done.6.refs_5_ = bf16[128,1024]{1,0:T(8,128)(2,1)S(1)} collective-permute-done((bf16[128,1024]{1,0:T(8,128)(2,1)S(1)}, bf16[128,1024]{1,0:T(8,128)(2,1)S(1)}, u32[]{:S(2)}, u32[]{:S(2)}) %collective-permute-start.6) | collective-permute-done | bytes 262176 | tf_op jit(solution)/shard_map/ppermute | solution.py:317
  41.4 1.4 %early_sum.1.total_ref = f32[768,1024]{1,0:T(8,128)S(1)} custom-call(s32[1]{0:T(128)} %bitcast.me_ref, bf16[256,1024]{1,0:T(8,128)(2,1)S(1)} %copy-done.2, bf16[512,1024]{1,0:T(8,128)(2,1)S(1)} %get-tuple-element.10.member_ref, bf16[128,1024]{1,0:T(8,128)(2,1)S(1)} %filter.8.refs_0_, bf16[128,1024]{1,0:T(8,128)(2,1)S(1)} %collective-permute-done.2.refs_1_, ...), custom_call_target="tpu_custom_call" | custom-call | flops 500000000 | bytes 100000 | tf_op jit(solution)/shard_map/early_sum/pallas_call | solution.py:228
  42.9 2.7 %collective-permute-done.7.refs_0_ = bf16[128,1024]{1,0:T(8,128)(2,1)S(1)} collective-permute-done((bf16[128,1024]{1,0:T(8,128)(2,1)S(1)}, bf16[128,1024]{1,0:T(8,128)(2,1)S(1)}, u32[]{:S(2)}, u32[]{:S(2)}) %collective-permute-start.7) | collective-permute-done | bytes 262176 | tf_op jit(solution)/shard_map/ppermute | solution.py:317
  45.6 0.8 %collective-permute-done.8.refs_1_ = bf16[128,1024]{1,0:T(8,128)(2,1)S(1)} collective-permute-done((bf16[128,1024]{1,0:T(8,128)(2,1)S(1)}, bf16[128,1024]{1,0:T(8,128)(2,1)S(1)}, u32[]{:S(2)}, u32[]{:S(2)}) %collective-permute-start.8) | collective-permute-done | bytes 262176 | tf_op jit(solution)/shard_map/ppermute | solution.py:317
  46.4 2.2 %late_sum.1 = (bf16[256,8,128]{2,1,0:T(8,128)(2,1)}, bf16[512,8,128]{2,1,0:T(8,128)(2,1)}) custom-call(s32[1]{0:T(128)} %bitcast.me_ref, bf16[256,1024]{1,0:T(8,128)(2,1)S(1)} %copy-done.2, bf16[512,1024]{1,0:T(8,128)(2,1)S(1)} %get-tuple-element.10.member_ref, bf16[512,256]{1,0:T(8,128)(2,1)S(1)} %get-tuple-element.11._.dates_ref, ...), custom_call_target="tpu_custom_call" | custom-call | flops 3000000000 | bytes 2000000 | tf_op jit(solution)/shard_map/late_sum/pallas_call | solution.py:285
  (12 shorter events, 0.0 us)
Async XLA Ops:
  0.6 7.8 %copy-start.4 = (s32[512,3]{0,1:T(4,128)S(1)}, s32[512,3]{0,1:T(4,128)}, u32[]{:S(2)}) copy-start(s32[512,3]{0,1:T(4,128)} %param.11) | copy-start | bytes 18436
  0.6 7.8 %copy-start.3 = (s32[1024,2]{0,1:T(2,128)S(1)}, s32[1024,2]{0,1:T(2,128)}, u32[]{:S(2)}) copy-start(s32[1024,2]{0,1:T(2,128)} %param.10) | copy-start | bytes 24580
  2.8 8.1 %collective-permute-start = (bf16[2,4,8,128]{3,2,1,0:T(8,128)(2,1)}, bf16[2,4,8,128]{3,2,1,0:T(8,128)(2,1)S(1)}, u32[]{:S(2)}, u32[]{:S(2)}) collective-permute-start(bf16[2,4,8,128]{3,2,1,0:T(8,128)(2,1)} %get-tuple-element.14), channel_id=1, source_target_pairs={{0,8},{8,16},{16,24},{24,32},{32,40},{40,48},{48,56},{56,64},{64,7... | collective-permute-start | bytes 49160 | tf_op jit(solution)/shard_map/ppermute | solution.py:309
  4.7 6.1 %collective-permute-start.1 = (bf16[2,4,8,128]{3,2,1,0:T(8,128)(2,1)}, bf16[2,4,8,128]{3,2,1,0:T(8,128)(2,1)S(1)}, u32[]{:S(2)}, u32[]{:S(2)}) collective-permute-start(bf16[2,4,8,128]{3,2,1,0:T(8,128)(2,1)} %get-tuple-element.15), channel_id=1, source_target_pairs={{8,0},{16,8},{24,16},{32,24},{40,32},{48,40},{56,48},{64,56},{72,6... | collective-permute-start | bytes 49160 | tf_op jit(solution)/shard_map/ppermute | solution.py:310
  8.4 1.7 %copy-start.5 = (f32[3,5]{1,0:T(4,128)S(1)}, f32[3,5]{1,0:T(4,128)}, u32[]{:S(2)}) copy-start(f32[3,5]{1,0:T(4,128)} %taps_ref.1) | copy-start | bytes 184
  8.4 2.7 %copy-start.1 = (bf16[128,8,1024]{2,1,0:T(8,128)(2,1)S(1)}, bf16[128,8,1024]{2,1,0:T(8,128)(2,1)}, u32[]{:S(2)}) copy-start(bf16[128,8,1024]{2,1,0:T(8,128)(2,1)} %coh_ref.15) | copy-start | bytes 6291460
  10.1 1.6 %copy-start = (bf16[128,8,1024]{2,1,0:T(8,128)(2,1)S(1)}, bf16[128,8,1024]{2,1,0:T(8,128)(2,1)}, u32[]{:S(2)}) copy-start(bf16[128,8,1024]{2,1,0:T(8,128)(2,1)} %phase_ref.15) | copy-start | bytes 6291460
  13.3 22.2 %collective-permute-start.2 = (bf16[128,1024]{1,0:T(8,128)(2,1)S(1)}, bf16[128,1024]{1,0:T(8,128)(2,1)S(1)}, u32[]{:S(2)}, u32[]{:S(2)}) collective-permute-start(bf16[128,1024]{1,0:T(8,128)(2,1)S(1)} %filter.9), channel_id=1, source_target_pairs={{0,6},{1,7},{2,4},{3,5},{4,2},{5,3},{6,0},{7,1},{8,14},{9,15},{10,... | collective-permute-start | bytes 786440 | tf_op jit(solution)/shard_map/ppermute | solution.py:317
  20.4 16.6 %collective-permute-start.3 = (bf16[128,1024]{1,0:T(8,128)(2,1)S(1)}, bf16[128,1024]{1,0:T(8,128)(2,1)S(1)}, u32[]{:S(2)}, u32[]{:S(2)}) collective-permute-start(bf16[128,1024]{1,0:T(8,128)(2,1)S(1)} %filter.10), channel_id=1, source_target_pairs={{0,5},{1,4},{2,7},{3,6},{4,1},{5,0},{6,3},{7,2},{8,13},{9,12},{10,... | collective-permute-start | bytes 786440 | tf_op jit(solution)/shard_map/ppermute | solution.py:317
  23.9 16.1 %collective-permute-start.4 = (bf16[128,1024]{1,0:T(8,128)(2,1)S(1)}, bf16[128,1024]{1,0:T(8,128)(2,1)S(1)}, u32[]{:S(2)}, u32[]{:S(2)}) collective-permute-start(bf16[128,1024]{1,0:T(8,128)(2,1)S(1)} %filter.11), channel_id=1, source_target_pairs={{0,3},{1,2},{2,1},{3,0},{4,7},{5,6},{6,5},{7,4},{8,11},{9,10},{10,... | collective-permute-start | bytes 786440 | tf_op jit(solution)/shard_map/ppermute | solution.py:317
  25.6 14.5 %collective-permute-start.5 = (bf16[128,1024]{1,0:T(8,128)(2,1)S(1)}, bf16[128,1024]{1,0:T(8,128)(2,1)S(1)}, u32[]{:S(2)}, u32[]{:S(2)}) collective-permute-start(bf16[128,1024]{1,0:T(8,128)(2,1)S(1)} %filter.12), channel_id=1, source_target_pairs={{0,7},{1,6},{2,5},{3,4},{4,3},{5,2},{6,1},{7,0},{8,15},{9,14},{10,... | collective-permute-start | bytes 786440 | tf_op jit(solution)/shard_map/ppermute | solution.py:317
  32.0 9.4 %collective-permute-start.6 = (bf16[128,1024]{1,0:T(8,128)(2,1)S(1)}, bf16[128,1024]{1,0:T(8,128)(2,1)S(1)}, u32[]{:S(2)}, u32[]{:S(2)}) collective-permute-start(bf16[128,1024]{1,0:T(8,128)(2,1)S(1)} %filter.13), channel_id=1, source_target_pairs={{0,1},{1,0},{2,3},{3,2},{4,5},{5,4},{6,7},{7,6},{8,9},{9,8},{10,11... | collective-permute-start | bytes 786440 | tf_op jit(solution)/shard_map/ppermute | solution.py:317
  35.5 6.0 %copy-start.2 = (bf16[256,1024]{1,0:T(8,128)(2,1)S(1)}, bf16[256,1024]{1,0:T(8,128)(2,1)}, u32[]{:S(2)}) copy-start(bf16[256,1024]{1,0:T(8,128)(2,1)} %inverse_ref.3) | copy-start | bytes 1572868
  35.5 10.1 %collective-permute-start.7 = (bf16[128,1024]{1,0:T(8,128)(2,1)S(1)}, bf16[128,1024]{1,0:T(8,128)(2,1)S(1)}, u32[]{:S(2)}, u32[]{:S(2)}) collective-permute-start(bf16[128,1024]{1,0:T(8,128)(2,1)S(1)} %filter.14), channel_id=1, source_target_pairs={{0,4},{1,5},{2,6},{3,7},{4,0},{5,1},{6,2},{7,3},{8,12},{9,13},{10,... | collective-permute-start | bytes 786440 | tf_op jit(solution)/shard_map/ppermute | solution.py:317
  37.0 9.4 %collective-permute-start.8 = (bf16[128,1024]{1,0:T(8,128)(2,1)S(1)}, bf16[128,1024]{1,0:T(8,128)(2,1)S(1)}, u32[]{:S(2)}, u32[]{:S(2)}) collective-permute-start(bf16[128,1024]{1,0:T(8,128)(2,1)S(1)} %filter.15), channel_id=1, source_target_pairs={{0,2},{1,3},{2,0},{3,1},{4,6},{5,7},{6,4},{7,5},{8,10},{9,11},{10,... | collective-permute-start | bytes 786440 | tf_op jit(solution)/shard_map/ppermute | solution.py:317

commit v5 on v4

--- a/solution.py
+++ b/solution.py
@@ -65,7 +65,7 @@
     )(phases, coherence)
 
 
-def bands_kernel(taps_ref, _, high_ref, low_ref):
+def bands_kernel(taps_ref, high_ref, low_ref):
     place = lax.broadcasted_iota(jnp.int32, (2 * LANES, LANES), 0)
     place = jnp.where(place >= LANES + 64, place - 2 * LANES, place)
     tap = place - lax.broadcasted_iota(jnp.int32, (2 * LANES, LANES), 1) + 2
@@ -77,10 +77,10 @@
         high_ref[:, a * LANES : (a + 1) * LANES] = high
         low_ref[:, a * LANES : (a + 1) * LANES] = (band - high.astype(F32)).astype(BF16)
 
-def bands(taps, after):
+def bands(taps):
     shape = jax.ShapeDtypeStruct((2 * LANES, 3 * LANES), BF16)
-    return pl.pallas_call(bands_kernel, in_specs=[SMEM, ANY], out_specs=[VMEM, VMEM], out_shape=[shape, shape],
-        compiler_params=params(), cost_estimate=cost(3e8,1e5), name="bands")(taps, after)
+    return pl.pallas_call(bands_kernel, in_specs=[SMEM], out_specs=[VMEM, VMEM], out_shape=[shape, shape],
+        compiler_params=params(), cost_estimate=cost(2e9,1e6), name="bands")(taps)
 
 
 def expand_kernel(left_ref, right_ref, phase_out, coh_out):
@@ -94,7 +94,7 @@
 def expand(left, right):
     shape = jax.ShapeDtypeStruct((4, 32, 8, LANES), BF16)
     out = pl.pallas_call(expand_kernel, in_specs=[VMEM, VMEM], out_specs=[VMEM, VMEM], out_shape=[shape, shape],
-        compiler_params=params(), cost_estimate=cost(5e8,1e5), name="expand")(left, right)
+        compiler_params=params(), cost_estimate=cost(2e9,1e6), name="expand")(left, right)
     return [o.reshape(128, 8, LANES) for o in out]
 
 
@@ -124,10 +124,9 @@
         coh = jnp.concatenate([flat(coh_ref[at, :, here]), flat(edge(coh_ref, coh_edge_ref))], axis=1)
         product = phase.astype(F32) * coh.astype(F32)
         major = product.astype(BF16)
-        minor = (product - major.astype(F32)).astype(BF16)
         high, low = high_ref[...], low_ref[...]
         den = jnp.dot(jnp.concatenate([coh, coh], axis=1), jnp.concatenate([high, low], axis=0), preferred_element_type=F32)
-        num = jnp.dot(jnp.concatenate([major, minor, major], axis=1), jnp.concatenate([high, high, low], axis=0), preferred_element_type=F32)
+        num = jnp.dot(jnp.concatenate([major, major], axis=1), jnp.concatenate([high, low], axis=0), preferred_element_type=F32)
         def vertical(parts):
             p = [parts[:, a * LANES : (a + 1) * LANES].reshape(group, 8, LANES) for a in range(3)]
             down = jnp.where(row == 0, 0.0, pltpu.roll(p[0], 1, 1))
@@ -160,7 +159,7 @@
     )(me, *bands, phases, coherence, phase_edge, coh_edge)
 
 
-def network_kernel(pairs_ref, triplets_ref, member_ref, dates_ref, first):
+def network_kernel(pairs_ref, triplets_ref, _, member_ref, dates_ref, first):
     count = pairs_ref.shape[1]
     triplet_count = triplets_ref.shape[1]
     date_count = dates_ref.shape[1]
@@ -183,12 +182,12 @@
     dates_ref[...] = jnp.dot(member_ref[...], first[...], preferred_element_type=F32).astype(BF16)
 
 
-def network(date_pairs, triplets, dates):
+def network(date_pairs, triplets, dates, after):
     count = date_pairs.shape[0]
     triplet_count = triplets.shape[0]
     return pl.pallas_call(
         network_kernel,
-        in_specs=[VMEM, VMEM],
+        in_specs=[VMEM, VMEM, ANY],
         out_specs=[VMEM, VMEM],
         out_shape=[
             jax.ShapeDtypeStruct((triplet_count, count), BF16),
@@ -198,7 +197,7 @@
         compiler_params=params(),
         cost_estimate=cost(2e9,1e6),
         name="network",
-    )(date_pairs.T, triplets.T)
+    )(date_pairs.T, triplets.T, after)
 
 
 def piece(me, step, matrix_ref, rows, share):
@@ -308,13 +307,13 @@
     to_left, to_right = pack_edges(phases, coherence)
     left = lax.ppermute(to_right, "img", [(i, i + 1) for i in range(size - 1)])
     right = lax.ppermute(to_left, "img", [(i + 1, i) for i in range(size - 1)])
-    member, dates_matrix = network(date_pairs, triplets, inverse.shape[0])
-    tap_bands = bands(kernel_taps, dates_matrix)
+    tap_bands = bands(kernel_taps)
     edges = expand(left, right)
     pieces = {}
     for step in ORDER:
         block = filter_block(step, me, tap_bands, phases, coherence, *edges)
         pieces[step] = lax.ppermute(block, "ifg", [(i, i ^ step) for i in range(peers)])
+    member, dates_matrix = network(date_pairs, triplets, inverse.shape[0], block)
     pieces[0] = filter_block(0, me, tap_bands, phases, coherence, *edges)
     total = early_sum(EARLY, me, inverse, member, [pieces[s] for s in EARLY])
     return tuple(late_sum(LATE, me, inverse, member, dates_matrix, total, [pieces[s] for s in LATE], rows))

time: 49.2 us -> 47.1 us (0.957)
  Pallas kernels: 21 us -> 18.8 us
  local copies, waits for them, and re-layouts: 0.61 us -> 1.18 us
    pallas_call x8, Pallas kernels: 12.7 us -> 10.5 us  [filter_block(): pl.pallas_call(functools.partial(filter_kernel, step, SIZE), in_specs=[SM...]
    ppermute x7, waiting for transfers between devices: 4.94 us -> 4.07 us  [per_device(): lax.ppermute(block, 'ifg', [(i, i ^ step) for i in range(peers)])]
    ppermute x1, waiting for transfers between devices: 0.01 us -> 0.83 us  [per_device(): right = lax.ppermute(to_left, 'img', [(i + 1, i) for i in range(size - 1)])]
    unnamed x12, local copies, waits for them, and re-layouts: 0.61 us -> 1.18 us
  transfers between devices with their start and end apart: 9 -> 9, of which waited for: 3 -> 4; matrix products, arithmetic and copies ran while one was open for 0% -> 0% of each run, Pallas kernels for 31% -> 28%
where the time goes in v5:
time: 47.1 us; the launch traced here: 46.9 us
  starting transfers between devices  21 us (45%)
  Pallas kernels  18.8 us (40%)
  waiting for transfers between devices  4.9 us (10%)
  local copies, waits for them, and re-layouts  1.18 us (3%)
  between operations  0.98 us (2%)
    ppermute x7, starting transfers between devices, per_device(): lax.ppermute(block, 'ifg', [(i, i ^ step) for i in range(peers)])  15.4 us
    pallas_call x8, Pallas kernels, filter_block(): pl.pallas_call(functools.partial(filter_kernel, step, SIZE), in_specs=[SM...  10.5 us
    ppermute x7, waiting for transfers between devices, per_device(): lax.ppermute(block, 'ifg', [(i, i ^ step) for i in range(peers)])  4.07 us
    ppermute x1, starting transfers between devices, per_device(): right = lax.ppermute(to_left, 'img', [(i + 1, i) for i in range(size - 1)])  3.64 us
    pallas_call x1, Pallas kernels, late_sum(): pl.pallas_call(functools.partial(late_kernel, steps), in_specs=[SMEM] + [...  2.17 us
    pallas_call x1, Pallas kernels, pack_edges(): pl.pallas_call(pack_kernel, in_specs=[HBM, HBM], out_specs=[VMEM, VMEM],...  2.15 us
    ppermute x1, starting transfers between devices, per_device(): left = lax.ppermute(to_right, 'img', [(i, i + 1) for i in range(size - 1)])  1.92 us
    pallas_call x1, Pallas kernels, network(): pl.pallas_call(network_kernel, in_specs=[VMEM, VMEM, ANY], out_specs=[VME...  1.65 us
  transfers between devices with their start and end apart: 9, of which 4 were waited for; matrix products, arithmetic and copies ran while one was open for 0% of the time, Pallas kernels for 28%

profile of v5, /device:TPU:10, one launch (start us, length us, event | category | flops | bytes accessed | tf_op | source)
XLA Modules:
  0.0 46.9 jit_solution(720941926857423439)
XLA Ops:
  0.6 2.1 %pack_edges.1 = (bf16[2,4,8,128]{3,2,1,0:T(8,128)(2,1)}, bf16[2,4,8,128]{3,2,1,0:T(8,128)(2,1)}) custom-call(bf16[128,8,1024]{2,1,0:T(8,128)(2,1)} %phase_ref.15, bf16[128,8,1024]{2,1,0:T(8,128)(2,1)} %coh_ref.15), custom_call_target="tpu_custom_call" | custom-call | flops 300000000 | bytes 1000000 | tf_op jit(solution)/shard_map/pack_edges/pallas_call | solution.py:56
  2.8 1.9 %collective-permute-start = (bf16[2,4,8,128]{3,2,1,0:T(8,128)(2,1)}, bf16[2,4,8,128]{3,2,1,0:T(8,128)(2,1)S(1)}, u32[]{:S(2)}, u32[]{:S(2)}) collective-permute-start(bf16[2,4,8,128]{3,2,1,0:T(8,128)(2,1)} %get-tuple-element.12), channel_id=1, source_target_pairs={{0,8},{8,16},{16,24},{24,32},{32,40},{40,48},{48,56},{56,64},{64,7... | collective-permute-start | bytes 49160 | tf_op jit(solution)/shard_map/ppermute | solution.py:308
  4.7 3.6 %collective-permute-start.1 = (bf16[2,4,8,128]{3,2,1,0:T(8,128)(2,1)}, bf16[2,4,8,128]{3,2,1,0:T(8,128)(2,1)S(1)}, u32[]{:S(2)}, u32[]{:S(2)}) collective-permute-start(bf16[2,4,8,128]{3,2,1,0:T(8,128)(2,1)} %get-tuple-element.13), channel_id=1, source_target_pairs={{8,0},{16,8},{24,16},{32,24},{40,32},{48,40},{56,48},{64,56},{72,6... | collective-permute-start | bytes 49160 | tf_op jit(solution)/shard_map/ppermute | solution.py:309
  8.4 0.7 %bands.1 = (bf16[256,384]{1,0:T(8,128)(2,1)S(1)}, bf16[256,384]{1,0:T(8,128)(2,1)S(1)}) custom-call(f32[3,5]{1,0:T(4,128)S(1)} %copy-done.5), custom_call_target="tpu_custom_call" | custom-call | flops 2000000000 | bytes 1000000 | tf_op jit(solution)/shard_map/bands/pallas_call | solution.py:82
  9.1 0.0 copy-start
  9.1 0.0 copy-start.1
  9.2 0.8 %collective-permute-done.1.right_ref = bf16[2,4,8,128]{3,2,1,0:T(8,128)(2,1)S(1)} collective-permute-done((bf16[2,4,8,128]{3,2,1,0:T(8,128)(2,1)}, bf16[2,4,8,128]{3,2,1,0:T(8,128)(2,1)S(1)}, u32[]{:S(2)}, u32[]{:S(2)}) %collective-permute-start.1) | collective-permute-done | bytes 16416 | tf_op jit(solution)/shard_map/ppermute | solution.py:309
  10.0 0.2 expand.1
  10.2 0.5 %copy-done = bf16[128,8,1024]{2,1,0:T(8,128)(2,1)S(1)} copy-done((bf16[128,8,1024]{2,1,0:T(8,128)(2,1)S(1)}, bf16[128,8,1024]{2,1,0:T(8,128)(2,1)}, u32[]{:S(2)}) %copy-start) | copy-done | bytes 2097176
  10.7 0.6 %copy-done.1 = bf16[128,8,1024]{2,1,0:T(8,128)(2,1)S(1)} copy-done((bf16[128,8,1024]{2,1,0:T(8,128)(2,1)S(1)}, bf16[128,8,1024]{2,1,0:T(8,128)(2,1)}, u32[]{:S(2)}) %copy-start.1) | copy-done | bytes 2097176
  11.4 1.3 %filter.10 = bf16[128,1024]{1,0:T(8,128)(2,1)S(1)} custom-call(s32[1]{0:T(128)} %bitcast.me_ref, bf16[256,384]{1,0:T(8,128)(2,1)S(1)} %get-tuple-element.10.high_ref, bf16[256,384]{1,0:T(8,128)(2,1)S(1)} %get-tuple-element.11.low_ref, bf16[128,8,1024]{2,1,0:T(8,128)(2,1)S(1)} %copy-done, bf16[128,8,1024]{2,1,0:T(8,128)(2,1)S(1)} %copy-done.1, ...), custom_call_target="tpu_custom_call" | custom-call | flops 300000000 | bytes 100000 | tf_op jit(solution)/shard_map/filter/pallas_call | solution.py:150
  12.7 5.5 %collective-permute-start.2 = (bf16[128,1024]{1,0:T(8,128)(2,1)S(1)}, bf16[128,1024]{1,0:T(8,128)(2,1)S(1)}, u32[]{:S(2)}, u32[]{:S(2)}) collective-permute-start(bf16[128,1024]{1,0:T(8,128)(2,1)S(1)} %filter.10), channel_id=1, source_target_pairs={{0,6},{1,7},{2,4},{3,5},{4,2},{5,3},{6,0},{7,1},{8,14},{9,15},{10,... | collective-permute-start | bytes 786440 | tf_op jit(solution)/shard_map/ppermute | solution.py:315
  18.2 1.3 %filter.11 = bf16[128,1024]{1,0:T(8,128)(2,1)S(1)} custom-call(s32[1]{0:T(128)} %bitcast.me_ref, bf16[256,384]{1,0:T(8,128)(2,1)S(1)} %get-tuple-element.10.high_ref, bf16[256,384]{1,0:T(8,128)(2,1)S(1)} %get-tuple-element.11.low_ref, bf16[128,8,1024]{2,1,0:T(8,128)(2,1)S(1)} %copy-done, bf16[128,8,1024]{2,1,0:T(8,128)(2,1)S(1)} %copy-done.1, ...), custom_call_target="tpu_custom_call" | custom-call | flops 300000000 | bytes 100000 | tf_op jit(solution)/shard_map/filter/pallas_call | solution.py:150
  19.5 1.9 %collective-permute-start.3 = (bf16[128,1024]{1,0:T(8,128)(2,1)S(1)}, bf16[128,1024]{1,0:T(8,128)(2,1)S(1)}, u32[]{:S(2)}, u32[]{:S(2)}) collective-permute-start(bf16[128,1024]{1,0:T(8,128)(2,1)S(1)} %filter.11), channel_id=1, source_target_pairs={{0,5},{1,4},{2,7},{3,6},{4,1},{5,0},{6,3},{7,2},{8,13},{9,12},{10,... | collective-permute-start | bytes 786440 | tf_op jit(solution)/shard_map/ppermute | solution.py:315
  21.4 1.3 %filter.12 = bf16[128,1024]{1,0:T(8,128)(2,1)S(1)} custom-call(s32[1]{0:T(128)} %bitcast.me_ref, bf16[256,384]{1,0:T(8,128)(2,1)S(1)} %get-tuple-element.10.high_ref, bf16[256,384]{1,0:T(8,128)(2,1)S(1)} %get-tuple-element.11.low_ref, bf16[128,8,1024]{2,1,0:T(8,128)(2,1)S(1)} %copy-done, bf16[128,8,1024]{2,1,0:T(8,128)(2,1)S(1)} %copy-done.1, ...), custom_call_target="tpu_custom_call" | custom-call | flops 300000000 | bytes 100000 | tf_op jit(solution)/shard_map/filter/pallas_call | solution.py:150
  22.8 0.1 collective-permute-start.4
  22.9 1.3 %filter.13 = bf16[128,1024]{1,0:T(8,128)(2,1)S(1)} custom-call(s32[1]{0:T(128)} %bitcast.me_ref, bf16[256,384]{1,0:T(8,128)(2,1)S(1)} %get-tuple-element.10.high_ref, bf16[256,384]{1,0:T(8,128)(2,1)S(1)} %get-tuple-element.11.low_ref, bf16[128,8,1024]{2,1,0:T(8,128)(2,1)S(1)} %copy-done, bf16[128,8,1024]{2,1,0:T(8,128)(2,1)S(1)} %copy-done.1, ...), custom_call_target="tpu_custom_call" | custom-call | flops 300000000 | bytes 100000 | tf_op jit(solution)/shard_map/filter/pallas_call | solution.py:150
  24.2 4.9 %collective-permute-start.5 = (bf16[128,1024]{1,0:T(8,128)(2,1)S(1)}, bf16[128,1024]{1,0:T(8,128)(2,1)S(1)}, u32[]{:S(2)}, u32[]{:S(2)}) collective-permute-start(bf16[128,1024]{1,0:T(8,128)(2,1)S(1)} %filter.13), channel_id=1, source_target_pairs={{0,7},{1,6},{2,5},{3,4},{4,3},{5,2},{6,1},{7,0},{8,15},{9,14},{10,... | collective-permute-start | bytes 786440 | tf_op jit(solution)/shard_map/ppermute | solution.py:315
  29.0 1.3 %filter.14 = bf16[128,1024]{1,0:T(8,128)(2,1)S(1)} custom-call(s32[1]{0:T(128)} %bitcast.me_ref, bf16[256,384]{1,0:T(8,128)(2,1)S(1)} %get-tuple-element.10.high_ref, bf16[256,384]{1,0:T(8,128)(2,1)S(1)} %get-tuple-element.11.low_ref, bf16[128,8,1024]{2,1,0:T(8,128)(2,1)S(1)} %copy-done, bf16[128,8,1024]{2,1,0:T(8,128)(2,1)S(1)} %copy-done.1, ...), custom_call_target="tpu_custom_call" | custom-call | flops 300000000 | bytes 100000 | tf_op jit(solution)/shard_map/filter/pallas_call | solution.py:150
  30.4 0.1 collective-permute-start.6
  30.5 1.3 %filter.8._ = bf16[128,1024]{1,0:T(8,128)(2,1)S(1)} custom-call(s32[1]{0:T(128)} %bitcast.me_ref, bf16[256,384]{1,0:T(8,128)(2,1)S(1)} %get-tuple-element.10.high_ref, bf16[256,384]{1,0:T(8,128)(2,1)S(1)} %get-tuple-element.11.low_ref, bf16[128,8,1024]{2,1,0:T(8,128)(2,1)S(1)} %copy-done, bf16[128,8,1024]{2,1,0:T(8,128)(2,1)S(1)} %copy-done.1, ...), custom_call_target="tpu_custom_call" | custom-call | flops 300000000 | bytes 100000 | tf_op jit(solution)/shard_map/filter/pallas_call | solution.py:150
  31.8 1.3 %filter.15 = bf16[128,1024]{1,0:T(8,128)(2,1)S(1)} custom-call(s32[1]{0:T(128)} %bitcast.me_ref, bf16[256,384]{1,0:T(8,128)(2,1)S(1)} %get-tuple-element.10.high_ref, bf16[256,384]{1,0:T(8,128)(2,1)S(1)} %get-tuple-element.11.low_ref, bf16[128,8,1024]{2,1,0:T(8,128)(2,1)S(1)} %copy-done, bf16[128,8,1024]{2,1,0:T(8,128)(2,1)S(1)} %copy-done.1, ...), custom_call_target="tpu_custom_call" | custom-call | flops 300000000 | bytes 100000 | tf_op jit(solution)/shard_map/filter/pallas_call | solution.py:150
  33.1 0.0 copy-start.3
  33.1 1.5 %collective-permute-start.7 = (bf16[128,1024]{1,0:T(8,128)(2,1)S(1)}, bf16[128,1024]{1,0:T(8,128)(2,1)S(1)}, u32[]{:S(2)}, u32[]{:S(2)}) collective-permute-start(bf16[128,1024]{1,0:T(8,128)(2,1)S(1)} %filter.15), channel_id=1, source_target_pairs={{0,4},{1,5},{2,6},{3,7},{4,0},{5,1},{6,2},{7,3},{8,12},{9,13},{10,... | collective-permute-start | bytes 786440 | tf_op jit(solution)/shard_map/ppermute | solution.py:315
  34.6 1.5 %collective-permute-start.8 = (bf16[128,1024]{1,0:T(8,128)(2,1)S(1)}, bf16[128,1024]{1,0:T(8,128)(2,1)S(1)}, u32[]{:S(2)}, u32[]{:S(2)}) collective-permute-start(bf16[128,1024]{1,0:T(8,128)(2,1)S(1)} %filter.8._), channel_id=1, source_target_pairs={{0,2},{1,3},{2,0},{3,1},{4,6},{5,7},{6,4},{7,5},{8,10},{9,11},{10,... | collective-permute-start | bytes 786440 | tf_op jit(solution)/shard_map/ppermute | solution.py:315
  36.1 1.3 %filter.9.refs_0_ = bf16[128,1024]{1,0:T(8,128)(2,1)S(1)} custom-call(s32[1]{0:T(128)} %bitcast.me_ref, bf16[256,384]{1,0:T(8,128)(2,1)S(1)} %get-tuple-element.10.high_ref, bf16[256,384]{1,0:T(8,128)(2,1)S(1)} %get-tuple-element.11.low_ref, bf16[128,8,1024]{2,1,0:T(8,128)(2,1)S(1)} %copy-done, bf16[128,8,1024]{2,1,0:T(8,128)(2,1)S(1)} %copy-done.1, ...), custom_call_target="tpu_custom_call" | custom-call | flops 300000000 | bytes 100000 | tf_op jit(solution)/shard_map/filter/pallas_call | solution.py:150
  37.4 1.7 %network.1 = (bf16[512,1024]{1,0:T(8,128)(2,1)S(1)}, bf16[512,256]{1,0:T(8,128)(2,1)S(1)}) custom-call(s32[2,1024]{1,0:T(2,128)S(1)} %bitcast.21, s32[3,512]{1,0:T(4,128)S(1)} %bitcast.22, bf16[128,1024]{1,0:T(8,128)(2,1)S(1)} %filter.8._), custom_call_target="tpu_custom_call" | custom-call | flops 2000000000 | bytes 1000000 | tf_op jit(solution)/shard_map/network/pallas_call | solution.py:188
  39.1 0.4 collective-permute-done.6.refs_5_
  39.5 1.4 %early_sum.1.total_ref = f32[768,1024]{1,0:T(8,128)S(1)} custom-call(s32[1]{0:T(128)} %bitcast.me_ref, bf16[256,1024]{1,0:T(8,128)(2,1)S(1)} %copy-done.2, bf16[512,1024]{1,0:T(8,128)(2,1)S(1)} %get-tuple-element.16.member_ref, bf16[128,1024]{1,0:T(8,128)(2,1)S(1)} %filter.9.refs_0_, bf16[128,1024]{1,0:T(8,128)(2,1)S(1)} %collective-permute-done.2.refs_1_, ...), custom_call_target="tpu_custom_call" | custom-call | flops 500000000 | bytes 100000 | tf_op jit(solution)/shard_map/early_sum/pallas_call | solution.py:227
  41.0 2.7 %collective-permute-done.7.refs_0_ = bf16[128,1024]{1,0:T(8,128)(2,1)S(1)} collective-permute-done((bf16[128,1024]{1,0:T(8,128)(2,1)S(1)}, bf16[128,1024]{1,0:T(8,128)(2,1)S(1)}, u32[]{:S(2)}, u32[]{:S(2)}) %collective-permute-start.7) | collective-permute-done | bytes 262176 | tf_op jit(solution)/shard_map/ppermute | solution.py:315
  43.7 0.9 %collective-permute-done.8.refs_1_ = bf16[128,1024]{1,0:T(8,128)(2,1)S(1)} collective-permute-done((bf16[128,1024]{1,0:T(8,128)(2,1)S(1)}, bf16[128,1024]{1,0:T(8,128)(2,1)S(1)}, u32[]{:S(2)}, u32[]{:S(2)}) %collective-permute-start.8) | collective-permute-done | bytes 262176 | tf_op jit(solution)/shard_map/ppermute | solution.py:315
  44.6 2.2 %late_sum.1 = (bf16[256,8,128]{2,1,0:T(8,128)(2,1)}, bf16[512,8,128]{2,1,0:T(8,128)(2,1)}) custom-call(s32[1]{0:T(128)} %bitcast.me_ref, bf16[256,1024]{1,0:T(8,128)(2,1)S(1)} %copy-done.2, bf16[512,1024]{1,0:T(8,128)(2,1)S(1)} %get-tuple-element.16.member_ref, bf16[512,256]{1,0:T(8,128)(2,1)S(1)} %get-tuple-element.17.dates_ref, ...), custom_call_target="tpu_custom_call" | custom-call | flops 3000000000 | bytes 2000000 | tf_op jit(solution)/shard_map/late_sum/pallas_call | solution.py:284
  (12 shorter events, 0.0 us)
Async XLA Ops:
  0.6 7.7 %copy-start.5 = (f32[3,5]{1,0:T(4,128)S(1)}, f32[3,5]{1,0:T(4,128)}, u32[]{:S(2)}) copy-start(f32[3,5]{1,0:T(4,128)} %taps_ref.1) | copy-start | bytes 184
  2.8 6.4 %collective-permute-start = (bf16[2,4,8,128]{3,2,1,0:T(8,128)(2,1)}, bf16[2,4,8,128]{3,2,1,0:T(8,128)(2,1)S(1)}, u32[]{:S(2)}, u32[]{:S(2)}) collective-permute-start(bf16[2,4,8,128]{3,2,1,0:T(8,128)(2,1)} %get-tuple-element.12), channel_id=1, source_target_pairs={{0,8},{8,16},{16,24},{24,32},{32,40},{40,48},{48,56},{56,64},{64,7... | collective-permute-start | bytes 49160 | tf_op jit(solution)/shard_map/ppermute | solution.py:308
  4.7 5.3 %collective-permute-start.1 = (bf16[2,4,8,128]{3,2,1,0:T(8,128)(2,1)}, bf16[2,4,8,128]{3,2,1,0:T(8,128)(2,1)S(1)}, u32[]{:S(2)}, u32[]{:S(2)}) collective-permute-start(bf16[2,4,8,128]{3,2,1,0:T(8,128)(2,1)} %get-tuple-element.13), channel_id=1, source_target_pairs={{8,0},{16,8},{24,16},{32,24},{40,32},{48,40},{56,48},{64,56},{72,6... | collective-permute-start | bytes 49160 | tf_op jit(solution)/shard_map/ppermute | solution.py:309
  9.1 1.6 %copy-start = (bf16[128,8,1024]{2,1,0:T(8,128)(2,1)S(1)}, bf16[128,8,1024]{2,1,0:T(8,128)(2,1)}, u32[]{:S(2)}) copy-start(bf16[128,8,1024]{2,1,0:T(8,128)(2,1)} %phase_ref.15) | copy-start | bytes 6291460
  9.1 2.2 %copy-start.1 = (bf16[128,8,1024]{2,1,0:T(8,128)(2,1)S(1)}, bf16[128,8,1024]{2,1,0:T(8,128)(2,1)}, u32[]{:S(2)}) copy-start(bf16[128,8,1024]{2,1,0:T(8,128)(2,1)} %coh_ref.15) | copy-start | bytes 6291460
  12.7 20.5 %collective-permute-start.2 = (bf16[128,1024]{1,0:T(8,128)(2,1)S(1)}, bf16[128,1024]{1,0:T(8,128)(2,1)S(1)}, u32[]{:S(2)}, u32[]{:S(2)}) collective-permute-start(bf16[128,1024]{1,0:T(8,128)(2,1)S(1)} %filter.10), channel_id=1, source_target_pairs={{0,6},{1,7},{2,4},{3,5},{4,2},{5,3},{6,0},{7,1},{8,14},{9,15},{10,... | collective-permute-start | bytes 786440 | tf_op jit(solution)/shard_map/ppermute | solution.py:315
  19.5 15.1 %collective-permute-start.3 = (bf16[128,1024]{1,0:T(8,128)(2,1)S(1)}, bf16[128,1024]{1,0:T(8,128)(2,1)S(1)}, u32[]{:S(2)}, u32[]{:S(2)}) collective-permute-start(bf16[128,1024]{1,0:T(8,128)(2,1)S(1)} %filter.11), channel_id=1, source_target_pairs={{0,5},{1,4},{2,7},{3,6},{4,1},{5,0},{6,3},{7,2},{8,13},{9,12},{10,... | collective-permute-start | bytes 786440 | tf_op jit(solution)/shard_map/ppermute | solution.py:315
  22.8 16.3 %collective-permute-start.4 = (bf16[128,1024]{1,0:T(8,128)(2,1)S(1)}, bf16[128,1024]{1,0:T(8,128)(2,1)S(1)}, u32[]{:S(2)}, u32[]{:S(2)}) collective-permute-start(bf16[128,1024]{1,0:T(8,128)(2,1)S(1)} %filter.12), channel_id=1, source_target_pairs={{0,3},{1,2},{2,1},{3,0},{4,7},{5,6},{6,5},{7,4},{8,11},{9,10},{10,... | collective-permute-start | bytes 786440 | tf_op jit(solution)/shard_map/ppermute | solution.py:315
  24.2 14.9 %collective-permute-start.5 = (bf16[128,1024]{1,0:T(8,128)(2,1)S(1)}, bf16[128,1024]{1,0:T(8,128)(2,1)S(1)}, u32[]{:S(2)}, u32[]{:S(2)}) collective-permute-start(bf16[128,1024]{1,0:T(8,128)(2,1)S(1)} %filter.13), channel_id=1, source_target_pairs={{0,7},{1,6},{2,5},{3,4},{4,3},{5,2},{6,1},{7,0},{8,15},{9,14},{10,... | collective-permute-start | bytes 786440 | tf_op jit(solution)/shard_map/ppermute | solution.py:315
  30.4 9.2 %collective-permute-start.6 = (bf16[128,1024]{1,0:T(8,128)(2,1)S(1)}, bf16[128,1024]{1,0:T(8,128)(2,1)S(1)}, u32[]{:S(2)}, u32[]{:S(2)}) collective-permute-start(bf16[128,1024]{1,0:T(8,128)(2,1)S(1)} %filter.14), channel_id=1, source_target_pairs={{0,1},{1,0},{2,3},{3,2},{4,5},{5,4},{6,7},{7,6},{8,9},{9,8},{10,11... | collective-permute-start | bytes 786440 | tf_op jit(solution)/shard_map/ppermute | solution.py:315
  33.1 4.3 %copy-start.3 = (s32[1024,2]{0,1:T(2,128)S(1)}, s32[1024,2]{0,1:T(2,128)}, u32[]{:S(2)}) copy-start(s32[1024,2]{0,1:T(2,128)} %param.10) | copy-start | bytes 24580
  33.1 4.3 %copy-start.4 = (s32[512,3]{0,1:T(4,128)S(1)}, s32[512,3]{0,1:T(4,128)}, u32[]{:S(2)}) copy-start(s32[512,3]{0,1:T(4,128)} %param.11) | copy-start | bytes 18436
  33.1 10.5 %collective-permute-start.7 = (bf16[128,1024]{1,0:T(8,128)(2,1)S(1)}, bf16[128,1024]{1,0:T(8,128)(2,1)S(1)}, u32[]{:S(2)}, u32[]{:S(2)}) collective-permute-start(bf16[128,1024]{1,0:T(8,128)(2,1)S(1)} %filter.15), channel_id=1, source_target_pairs={{0,4},{1,5},{2,6},{3,7},{4,0},{5,1},{6,2},{7,3},{8,12},{9,13},{10,... | collective-permute-start | bytes 786440 | tf_op jit(solution)/shard_map/ppermute | solution.py:315
  34.6 10.0 %collective-permute-start.8 = (bf16[128,1024]{1,0:T(8,128)(2,1)S(1)}, bf16[128,1024]{1,0:T(8,128)(2,1)S(1)}, u32[]{:S(2)}, u32[]{:S(2)}) collective-permute-start(bf16[128,1024]{1,0:T(8,128)(2,1)S(1)} %filter.8._), channel_id=1, source_target_pairs={{0,2},{1,3},{2,0},{3,1},{4,6},{5,7},{6,4},{7,5},{8,10},{9,11},{10,... | collective-permute-start | bytes 786440 | tf_op jit(solution)/shard_map/ppermute | solution.py:315
  37.4 2.1 %copy-start.2 = (bf16[256,1024]{1,0:T(8,128)(2,1)S(1)}, bf16[256,1024]{1,0:T(8,128)(2,1)}, u32[]{:S(2)}) copy-start(bf16[256,1024]{1,0:T(8,128)(2,1)} %inverse_ref.3) | copy-start | bytes 1572868

commit v6 on v5

--- a/solution.py
+++ b/solution.py
@@ -65,7 +65,7 @@
     )(phases, coherence)
 
 
-def bands_kernel(taps_ref, high_ref, low_ref):
+def bands_kernel(taps_ref, band_ref):
     place = lax.broadcasted_iota(jnp.int32, (2 * LANES, LANES), 0)
     place = jnp.where(place >= LANES + 64, place - 2 * LANES, place)
     tap = place - lax.broadcasted_iota(jnp.int32, (2 * LANES, LANES), 1) + 2
@@ -73,13 +73,11 @@
         band = jnp.zeros((2 * LANES, LANES), F32)
         for b in range(5):
             band = jnp.where(tap == b, taps_ref[a, b], band)
-        high = band.astype(BF16)
-        high_ref[:, a * LANES : (a + 1) * LANES] = high
-        low_ref[:, a * LANES : (a + 1) * LANES] = (band - high.astype(F32)).astype(BF16)
+        band_ref[:, a * LANES : (a + 1) * LANES] = band.astype(BF16)
 
 def bands(taps):
     shape = jax.ShapeDtypeStruct((2 * LANES, 3 * LANES), BF16)
-    return pl.pallas_call(bands_kernel, in_specs=[SMEM], out_specs=[VMEM, VMEM], out_shape=[shape, shape],
+    return pl.pallas_call(bands_kernel, in_specs=[SMEM], out_specs=VMEM, out_shape=shape,
         compiler_params=params(), cost_estimate=cost(2e9,1e6), name="bands")(taps)
 
 
@@ -98,7 +96,7 @@
     return [o.reshape(128, 8, LANES) for o in out]
 
 
-def filter_kernel(step, m, me_ref, high_ref, low_ref, phase_ref, coh_ref, phase_edge_ref, coh_edge_ref, out_ref, scratch):
+def filter_kernel(step, m, me_ref, band_ref, phase_ref, coh_ref, phase_edge_ref, coh_edge_ref, out_ref, scratch):
     block = me_ref[0] ^ step
     count = phase_ref.shape[0]
     blocks = phase_ref.shape[2] // LANES
@@ -124,9 +122,10 @@
         coh = jnp.concatenate([flat(coh_ref[at, :, here]), flat(edge(coh_ref, coh_edge_ref))], axis=1)
         product = phase.astype(F32) * coh.astype(F32)
         major = product.astype(BF16)
-        high, low = high_ref[...], low_ref[...]
-        den = jnp.dot(jnp.concatenate([coh, coh], axis=1), jnp.concatenate([high, low], axis=0), preferred_element_type=F32)
-        num = jnp.dot(jnp.concatenate([major, major], axis=1), jnp.concatenate([high, low], axis=0), preferred_element_type=F32)
+        minor = (product - major.astype(F32)).astype(BF16)
+        high = band_ref[...]
+        den = jnp.dot(coh, high, preferred_element_type=F32)
+        num = jnp.dot(jnp.concatenate([major, minor], axis=1), jnp.concatenate([high, high], axis=0), preferred_element_type=F32)
         def vertical(parts):
             p = [parts[:, a * LANES : (a + 1) * LANES].reshape(group, 8, LANES) for a in range(3)]
             down = jnp.where(row == 0, 0.0, pltpu.roll(p[0], 1, 1))
@@ -149,14 +148,14 @@
     count, rows, _ = phases.shape
     return pl.pallas_call(
         functools.partial(filter_kernel, step, SIZE),
-        in_specs=[SMEM] + [VMEM] * 6,
+        in_specs=[SMEM] + [VMEM] * 5,
         out_specs=VMEM,
         out_shape=jax.ShapeDtypeStruct((count, rows * LANES), BF16),
         scratch_shapes=[pltpu.VMEM((count * rows, LANES), F32)],
         compiler_params=params(),
         cost_estimate=cost(3e8,1e5),
         name="filter",
-    )(me, *bands, phases, coherence, phase_edge, coh_edge)
+    )(me, bands, phases, coherence, phase_edge, coh_edge)
 
 
 def network_kernel(pairs_ref, triplets_ref, _, member_ref, dates_ref, first):

time: 47.1 us -> 47.6 us (1.011)
  waiting for transfers between devices: 4.9 us -> 7.47 us
  Pallas kernels: 18.8 us -> 16.8 us
    ppermute x7, waiting for transfers between devices: 4.07 us -> 6.6 us  [per_device(): lax.ppermute(block, 'ifg', [(i, i ^ step) for i in range(peers)])]
    pallas_call x8, Pallas kernels: 10.5 us -> 8.49 us  [filter_block(): pl.pallas_call(functools.partial(filter_kernel, step, SIZE), in_specs=[SM...]
  transfers between devices with their start and end apart: 9 -> 9, of which waited for: 4 -> 2; matrix products, arithmetic and copies ran while one was open for 0% -> 0% of each run, Pallas kernels for 28% -> 24%
where the time goes in v6:
time: 47.6 us; the launch traced here: 47.4 us
  starting transfers between devices  21 us (44%)
  Pallas kernels  16.8 us (35%)
  waiting for transfers between devices  7.47 us (16%)
  local copies, waits for them, and re-layouts  1.15 us (2%)
  between operations  0.99 us (2%)
    ppermute x7, starting transfers between devices, per_device(): lax.ppermute(block, 'ifg', [(i, i ^ step) for i in range(peers)])  15.4 us
    pallas_call x8, Pallas kernels, filter_block(): pl.pallas_call(functools.partial(filter_kernel, step, SIZE), in_specs=[SM...  8.49 us
    ppermute x7, waiting for transfers between devices, per_device(): lax.ppermute(block, 'ifg', [(i, i ^ step) for i in range(peers)])  6.6 us
    ppermute x1, starting transfers between devices, per_device(): right = lax.ppermute(to_left, 'img', [(i + 1, i) for i in range(size - 1)])  3.64 us
    pallas_call x1, Pallas kernels, late_sum(): pl.pallas_call(functools.partial(late_kernel, steps), in_specs=[SMEM] + [...  2.19 us
    pallas_call x1, Pallas kernels, pack_edges(): pl.pallas_call(pack_kernel, in_specs=[HBM, HBM], out_specs=[VMEM, VMEM],...  2.15 us
    ppermute x1, starting transfers between devices, per_device(): left = lax.ppermute(to_right, 'img', [(i, i + 1) for i in range(size - 1)])  1.92 us
    pallas_call x1, Pallas kernels, network(): pl.pallas_call(network_kernel, in_specs=[VMEM, VMEM, ANY], out_specs=[VME...  1.65 us
  transfers between devices with their start and end apart: 9, of which 2 were waited for; matrix products, arithmetic and copies ran while one was open for 0% of the time, Pallas kernels for 24%

profile of v6, /device:TPU:10, one launch (start us, length us, event | category | flops | bytes accessed | tf_op | source)
XLA Modules:
  0.0 47.4 jit_solution(9371690389023354330)
XLA Ops:
  0.6 2.1 %pack_edges.1 = (bf16[2,4,8,128]{3,2,1,0:T(8,128)(2,1)}, bf16[2,4,8,128]{3,2,1,0:T(8,128)(2,1)}) custom-call(bf16[128,8,1024]{2,1,0:T(8,128)(2,1)} %phase_ref.15, bf16[128,8,1024]{2,1,0:T(8,128)(2,1)} %coh_ref.15), custom_call_target="tpu_custom_call" | custom-call | flops 300000000 | bytes 1000000 | tf_op jit(solution)/shard_map/pack_edges/pallas_call | solution.py:56
  2.8 1.9 %collective-permute-start = (bf16[2,4,8,128]{3,2,1,0:T(8,128)(2,1)}, bf16[2,4,8,128]{3,2,1,0:T(8,128)(2,1)S(1)}, u32[]{:S(2)}, u32[]{:S(2)}) collective-permute-start(bf16[2,4,8,128]{3,2,1,0:T(8,128)(2,1)} %get-tuple-element.8), channel_id=1, source_target_pairs={{0,8},{8,16},{16,24},{24,32},{32,40},{40,48},{48,56},{56,64},{64,7... | collective-permute-start | bytes 49160 | tf_op jit(solution)/shard_map/ppermute | solution.py:307
  4.7 3.6 %collective-permute-start.1 = (bf16[2,4,8,128]{3,2,1,0:T(8,128)(2,1)}, bf16[2,4,8,128]{3,2,1,0:T(8,128)(2,1)S(1)}, u32[]{:S(2)}, u32[]{:S(2)}) collective-permute-start(bf16[2,4,8,128]{3,2,1,0:T(8,128)(2,1)} %get-tuple-element.9), channel_id=1, source_target_pairs={{8,0},{16,8},{24,16},{32,24},{40,32},{48,40},{56,48},{64,56},{72,6... | collective-permute-start | bytes 49160 | tf_op jit(solution)/shard_map/ppermute | solution.py:308
  8.4 0.7 %bands.1.band_ref = bf16[256,384]{1,0:T(8,128)(2,1)S(1)} custom-call(f32[3,5]{1,0:T(4,128)S(1)} %copy-done.5), custom_call_target="tpu_custom_call" | custom-call | flops 2000000000 | bytes 1000000 | tf_op jit(solution)/shard_map/bands/pallas_call | solution.py:80
  9.1 0.0 copy-start
  9.1 0.0 copy-start.1
  9.1 0.9 %collective-permute-done.1.right_ref = bf16[2,4,8,128]{3,2,1,0:T(8,128)(2,1)S(1)} collective-permute-done((bf16[2,4,8,128]{3,2,1,0:T(8,128)(2,1)}, bf16[2,4,8,128]{3,2,1,0:T(8,128)(2,1)S(1)}, u32[]{:S(2)}, u32[]{:S(2)}) %collective-permute-start.1) | collective-permute-done | bytes 16416 | tf_op jit(solution)/shard_map/ppermute | solution.py:308
  10.0 0.2 expand.1
  10.2 0.5 %copy-done = bf16[128,8,1024]{2,1,0:T(8,128)(2,1)S(1)} copy-done((bf16[128,8,1024]{2,1,0:T(8,128)(2,1)S(1)}, bf16[128,8,1024]{2,1,0:T(8,128)(2,1)}, u32[]{:S(2)}) %copy-start) | copy-done | bytes 2097176
  10.7 0.6 %copy-done.1 = bf16[128,8,1024]{2,1,0:T(8,128)(2,1)S(1)} copy-done((bf16[128,8,1024]{2,1,0:T(8,128)(2,1)S(1)}, bf16[128,8,1024]{2,1,0:T(8,128)(2,1)}, u32[]{:S(2)}) %copy-start.1) | copy-done | bytes 2097176
  11.3 1.1 %filter.10 = bf16[128,1024]{1,0:T(8,128)(2,1)S(1)} custom-call(s32[1]{0:T(128)} %bitcast.me_ref, bf16[256,384]{1,0:T(8,128)(2,1)S(1)} %bands.1.band_ref, bf16[128,8,1024]{2,1,0:T(8,128)(2,1)S(1)} %copy-done, bf16[128,8,1024]{2,1,0:T(8,128)(2,1)S(1)} %copy-done.1, bf16[128,8,128]{2,1,0:T(8,128)(2,1)S(1)} %bitcast.5, bf16[128,8,128]{2,1,0:T(8,128)(2,1)S(1)} %bitcast.13), custom_call_target="tpu_custom_call" | custom-call | flops 300000000 | bytes 100000 | tf_op jit(solution)/shard_map/filter/pallas_call | solution.py:149
  12.4 5.5 %collective-permute-start.2 = (bf16[128,1024]{1,0:T(8,128)(2,1)S(1)}, bf16[128,1024]{1,0:T(8,128)(2,1)S(1)}, u32[]{:S(2)}, u32[]{:S(2)}) collective-permute-start(bf16[128,1024]{1,0:T(8,128)(2,1)S(1)} %filter.10), channel_id=1, source_target_pairs={{0,6},{1,7},{2,4},{3,5},{4,2},{5,3},{6,0},{7,1},{8,14},{9,15},{10,... | collective-permute-start | bytes 786440 | tf_op jit(solution)/shard_map/ppermute | solution.py:314
  17.9 1.1 %filter.11 = bf16[128,1024]{1,0:T(8,128)(2,1)S(1)} custom-call(s32[1]{0:T(128)} %bitcast.me_ref, bf16[256,384]{1,0:T(8,128)(2,1)S(1)} %bands.1.band_ref, bf16[128,8,1024]{2,1,0:T(8,128)(2,1)S(1)} %copy-done, bf16[128,8,1024]{2,1,0:T(8,128)(2,1)S(1)} %copy-done.1, bf16[128,8,128]{2,1,0:T(8,128)(2,1)S(1)} %bitcast.6, bf16[128,8,128]{2,1,0:T(8,128)(2,1)S(1)} %bitcast.14), custom_call_target="tpu_custom_call" | custom-call | flops 300000000 | bytes 100000 | tf_op jit(solution)/shard_map/filter/pallas_call | solution.py:149
  19.0 1.9 %collective-permute-start.3 = (bf16[128,1024]{1,0:T(8,128)(2,1)S(1)}, bf16[128,1024]{1,0:T(8,128)(2,1)S(1)}, u32[]{:S(2)}, u32[]{:S(2)}) collective-permute-start(bf16[128,1024]{1,0:T(8,128)(2,1)S(1)} %filter.11), channel_id=1, source_target_pairs={{0,5},{1,4},{2,7},{3,6},{4,1},{5,0},{6,3},{7,2},{8,13},{9,12},{10,... | collective-permute-start | bytes 786440 | tf_op jit(solution)/shard_map/ppermute | solution.py:314
  20.9 1.1 %filter.12 = bf16[128,1024]{1,0:T(8,128)(2,1)S(1)} custom-call(s32[1]{0:T(128)} %bitcast.me_ref, bf16[256,384]{1,0:T(8,128)(2,1)S(1)} %bands.1.band_ref, bf16[128,8,1024]{2,1,0:T(8,128)(2,1)S(1)} %copy-done, bf16[128,8,1024]{2,1,0:T(8,128)(2,1)S(1)} %copy-done.1, bf16[128,8,128]{2,1,0:T(8,128)(2,1)S(1)} %bitcast.7, bf16[128,8,128]{2,1,0:T(8,128)(2,1)S(1)} %bitcast.15), custom_call_target="tpu_custom_call" | custom-call | flops 300000000 | bytes 100000 | tf_op jit(solution)/shard_map/filter/pallas_call | solution.py:149
  22.0 0.1 collective-permute-start.4
  22.1 1.1 %filter.13 = bf16[128,1024]{1,0:T(8,128)(2,1)S(1)} custom-call(s32[1]{0:T(128)} %bitcast.me_ref, bf16[256,384]{1,0:T(8,128)(2,1)S(1)} %bands.1.band_ref, bf16[128,8,1024]{2,1,0:T(8,128)(2,1)S(1)} %copy-done, bf16[128,8,1024]{2,1,0:T(8,128)(2,1)S(1)} %copy-done.1, bf16[128,8,128]{2,1,0:T(8,128)(2,1)S(1)} %bitcast.8, bf16[128,8,128]{2,1,0:T(8,128)(2,1)S(1)} %bitcast.16), custom_call_target="tpu_custom_call" | custom-call | flops 300000000 | bytes 100000 | tf_op jit(solution)/shard_map/filter/pallas_call | solution.py:149
  23.1 4.9 %collective-permute-start.5 = (bf16[128,1024]{1,0:T(8,128)(2,1)S(1)}, bf16[128,1024]{1,0:T(8,128)(2,1)S(1)}, u32[]{:S(2)}, u32[]{:S(2)}) collective-permute-start(bf16[128,1024]{1,0:T(8,128)(2,1)S(1)} %filter.13), channel_id=1, source_target_pairs={{0,7},{1,6},{2,5},{3,4},{4,3},{5,2},{6,1},{7,0},{8,15},{9,14},{10,... | collective-permute-start | bytes 786440 | tf_op jit(solution)/shard_map/ppermute | solution.py:314
  28.0 1.1 %filter.14 = bf16[128,1024]{1,0:T(8,128)(2,1)S(1)} custom-call(s32[1]{0:T(128)} %bitcast.me_ref, bf16[256,384]{1,0:T(8,128)(2,1)S(1)} %bands.1.band_ref, bf16[128,8,1024]{2,1,0:T(8,128)(2,1)S(1)} %copy-done, bf16[128,8,1024]{2,1,0:T(8,128)(2,1)S(1)} %copy-done.1, bf16[128,8,128]{2,1,0:T(8,128)(2,1)S(1)} %bitcast.9, bf16[128,8,128]{2,1,0:T(8,128)(2,1)S(1)} %bitcast.17), custom_call_target="tpu_custom_call" | custom-call | flops 300000000 | bytes 100000 | tf_op jit(solution)/shard_map/filter/pallas_call | solution.py:149
  29.1 0.1 collective-permute-start.6
  29.2 1.1 %filter.8._ = bf16[128,1024]{1,0:T(8,128)(2,1)S(1)} custom-call(s32[1]{0:T(128)} %bitcast.me_ref, bf16[256,384]{1,0:T(8,128)(2,1)S(1)} %bands.1.band_ref, bf16[128,8,1024]{2,1,0:T(8,128)(2,1)S(1)} %copy-done, bf16[128,8,1024]{2,1,0:T(8,128)(2,1)S(1)} %copy-done.1, bf16[128,8,128]{2,1,0:T(8,128)(2,1)S(1)} %bitcast.10, bf16[128,8,128]{2,1,0:T(8,128)(2,1)S(1)} %bitcast.18), custom_call_target="tpu_custom_call" | custom-call | flops 300000000 | bytes 100000 | tf_op jit(solution)/shard_map/filter/pallas_call | solution.py:149
  30.2 1.1 %filter.15 = bf16[128,1024]{1,0:T(8,128)(2,1)S(1)} custom-call(s32[1]{0:T(128)} %bitcast.me_ref, bf16[256,384]{1,0:T(8,128)(2,1)S(1)} %bands.1.band_ref, bf16[128,8,1024]{2,1,0:T(8,128)(2,1)S(1)} %copy-done, bf16[128,8,1024]{2,1,0:T(8,128)(2,1)S(1)} %copy-done.1, bf16[128,8,128]{2,1,0:T(8,128)(2,1)S(1)} %bitcast.11, bf16[128,8,128]{2,1,0:T(8,128)(2,1)S(1)} %bitcast.19), custom_call_target="tpu_custom_call" | custom-call | flops 300000000 | bytes 100000 | tf_op jit(solution)/shard_map/filter/pallas_call | solution.py:149
  31.3 0.0 copy-start.3
  31.3 0.0 copy-start.4
  31.3 1.5 %collective-permute-start.7 = (bf16[128,1024]{1,0:T(8,128)(2,1)S(1)}, bf16[128,1024]{1,0:T(8,128)(2,1)S(1)}, u32[]{:S(2)}, u32[]{:S(2)}) collective-permute-start(bf16[128,1024]{1,0:T(8,128)(2,1)S(1)} %filter.15), channel_id=1, source_target_pairs={{0,4},{1,5},{2,6},{3,7},{4,0},{5,1},{6,2},{7,3},{8,12},{9,13},{10,... | collective-permute-start | bytes 786440 | tf_op jit(solution)/shard_map/ppermute | solution.py:314
  32.8 1.5 %collective-permute-start.8 = (bf16[128,1024]{1,0:T(8,128)(2,1)S(1)}, bf16[128,1024]{1,0:T(8,128)(2,1)S(1)}, u32[]{:S(2)}, u32[]{:S(2)}) collective-permute-start(bf16[128,1024]{1,0:T(8,128)(2,1)S(1)} %filter.8._), channel_id=1, source_target_pairs={{0,2},{1,3},{2,0},{3,1},{4,6},{5,7},{6,4},{7,5},{8,10},{9,11},{10,... | collective-permute-start | bytes 786440 | tf_op jit(solution)/shard_map/ppermute | solution.py:314
  34.3 1.1 %filter.9.refs_0_ = bf16[128,1024]{1,0:T(8,128)(2,1)S(1)} custom-call(s32[1]{0:T(128)} %bitcast.me_ref, bf16[256,384]{1,0:T(8,128)(2,1)S(1)} %bands.1.band_ref, bf16[128,8,1024]{2,1,0:T(8,128)(2,1)S(1)} %copy-done, bf16[128,8,1024]{2,1,0:T(8,128)(2,1)S(1)} %copy-done.1, bf16[128,8,128]{2,1,0:T(8,128)(2,1)S(1)} %bitcast.12, bf16[128,8,128]{2,1,0:T(8,128)(2,1)S(1)} %bitcast.20), custom_call_target="tpu_custom_call" | custom-call | flops 300000000 | bytes 100000 | tf_op jit(solution)/shard_map/filter/pallas_call | solution.py:149
  35.4 0.0 copy-start.2
  35.4 1.7 %network.1 = (bf16[512,1024]{1,0:T(8,128)(2,1)S(1)}, bf16[512,256]{1,0:T(8,128)(2,1)S(1)}) custom-call(s32[2,1024]{1,0:T(2,128)S(1)} %bitcast.21, s32[3,512]{1,0:T(4,128)S(1)} %bitcast.22, bf16[128,1024]{1,0:T(8,128)(2,1)S(1)} %filter.8._), custom_call_target="tpu_custom_call" | custom-call | flops 2000000000 | bytes 1000000 | tf_op jit(solution)/shard_map/network/pallas_call | solution.py:187
  37.0 6.6 %collective-permute-done.4.refs_3_ = bf16[128,1024]{1,0:T(8,128)(2,1)S(1)} collective-permute-done((bf16[128,1024]{1,0:T(8,128)(2,1)S(1)}, bf16[128,1024]{1,0:T(8,128)(2,1)S(1)}, u32[]{:S(2)}, u32[]{:S(2)}) %collective-permute-start.4) | collective-permute-done | bytes 262176 | tf_op jit(solution)/shard_map/ppermute | solution.py:314
  43.6 1.4 %early_sum.1.total_ref = f32[768,1024]{1,0:T(8,128)S(1)} custom-call(s32[1]{0:T(128)} %bitcast.me_ref, bf16[256,1024]{1,0:T(8,128)(2,1)S(1)} %copy-done.2, bf16[512,1024]{1,0:T(8,128)(2,1)S(1)} %get-tuple-element.12.member_ref, bf16[128,1024]{1,0:T(8,128)(2,1)S(1)} %filter.9.refs_0_, bf16[128,1024]{1,0:T(8,128)(2,1)S(1)} %collective-permute-done.2.refs_1_, ...), custom_call_target="tpu_custom_call" | custom-call | flops 500000000 | bytes 100000 | tf_op jit(solution)/shard_map/early_sum/pallas_call | solution.py:226
  45.1 2.2 %late_sum.1 = (bf16[256,8,128]{2,1,0:T(8,128)(2,1)}, bf16[512,8,128]{2,1,0:T(8,128)(2,1)}) custom-call(s32[1]{0:T(128)} %bitcast.me_ref, bf16[256,1024]{1,0:T(8,128)(2,1)S(1)} %copy-done.2, bf16[512,1024]{1,0:T(8,128)(2,1)S(1)} %get-tuple-element.12.member_ref, bf16[512,256]{1,0:T(8,128)(2,1)S(1)} %get-tuple-element.13.dates_ref, ...), custom_call_target="tpu_custom_call" | custom-call | flops 3000000000 | bytes 2000000 | tf_op jit(solution)/shard_map/late_sum/pallas_call | solution.py:283
  (12 shorter events, 0.0 us)
Async XLA Ops:
  0.6 7.7 %copy-start.5 = (f32[3,5]{1,0:T(4,128)S(1)}, f32[3,5]{1,0:T(4,128)}, u32[]{:S(2)}) copy-start(f32[3,5]{1,0:T(4,128)} %taps_ref.1) | copy-start | bytes 184
  2.8 6.3 %collective-permute-start = (bf16[2,4,8,128]{3,2,1,0:T(8,128)(2,1)}, bf16[2,4,8,128]{3,2,1,0:T(8,128)(2,1)S(1)}, u32[]{:S(2)}, u32[]{:S(2)}) collective-permute-start(bf16[2,4,8,128]{3,2,1,0:T(8,128)(2,1)} %get-tuple-element.8), channel_id=1, source_target_pairs={{0,8},{8,16},{16,24},{24,32},{32,40},{40,48},{48,56},{56,64},{64,7... | collective-permute-start | bytes 49160 | tf_op jit(solution)/shard_map/ppermute | solution.py:307
  4.7 5.3 %collective-permute-start.1 = (bf16[2,4,8,128]{3,2,1,0:T(8,128)(2,1)}, bf16[2,4,8,128]{3,2,1,0:T(8,128)(2,1)S(1)}, u32[]{:S(2)}, u32[]{:S(2)}) collective-permute-start(bf16[2,4,8,128]{3,2,1,0:T(8,128)(2,1)} %get-tuple-element.9), channel_id=1, source_target_pairs={{8,0},{16,8},{24,16},{32,24},{40,32},{48,40},{56,48},{64,56},{72,6... | collective-permute-start | bytes 49160 | tf_op jit(solution)/shard_map/ppermute | solution.py:308
  9.1 1.6 %copy-start = (bf16[128,8,1024]{2,1,0:T(8,128)(2,1)S(1)}, bf16[128,8,1024]{2,1,0:T(8,128)(2,1)}, u32[]{:S(2)}) copy-start(bf16[128,8,1024]{2,1,0:T(8,128)(2,1)} %phase_ref.15) | copy-start | bytes 6291460
  9.1 2.2 %copy-start.1 = (bf16[128,8,1024]{2,1,0:T(8,128)(2,1)S(1)}, bf16[128,8,1024]{2,1,0:T(8,128)(2,1)}, u32[]{:S(2)}) copy-start(bf16[128,8,1024]{2,1,0:T(8,128)(2,1)} %coh_ref.15) | copy-start | bytes 6291460
  12.4 18.9 %collective-permute-start.2 = (bf16[128,1024]{1,0:T(8,128)(2,1)S(1)}, bf16[128,1024]{1,0:T(8,128)(2,1)S(1)}, u32[]{:S(2)}, u32[]{:S(2)}) collective-permute-start(bf16[128,1024]{1,0:T(8,128)(2,1)S(1)} %filter.10), channel_id=1, source_target_pairs={{0,6},{1,7},{2,4},{3,5},{4,2},{5,3},{6,0},{7,1},{8,14},{9,15},{10,... | collective-permute-start | bytes 786440 | tf_op jit(solution)/shard_map/ppermute | solution.py:314
  19.0 13.8 %collective-permute-start.3 = (bf16[128,1024]{1,0:T(8,128)(2,1)S(1)}, bf16[128,1024]{1,0:T(8,128)(2,1)S(1)}, u32[]{:S(2)}, u32[]{:S(2)}) collective-permute-start(bf16[128,1024]{1,0:T(8,128)(2,1)S(1)} %filter.11), channel_id=1, source_target_pairs={{0,5},{1,4},{2,7},{3,6},{4,1},{5,0},{6,3},{7,2},{8,13},{9,12},{10,... | collective-permute-start | bytes 786440 | tf_op jit(solution)/shard_map/ppermute | solution.py:314
  22.0 21.6 %collective-permute-start.4 = (bf16[128,1024]{1,0:T(8,128)(2,1)S(1)}, bf16[128,1024]{1,0:T(8,128)(2,1)S(1)}, u32[]{:S(2)}, u32[]{:S(2)}) collective-permute-start(bf16[128,1024]{1,0:T(8,128)(2,1)S(1)} %filter.12), channel_id=1, source_target_pairs={{0,3},{1,2},{2,1},{3,0},{4,7},{5,6},{6,5},{7,4},{8,11},{9,10},{10,... | collective-permute-start | bytes 786440 | tf_op jit(solution)/shard_map/ppermute | solution.py:314
  23.1 20.5 %collective-permute-start.5 = (bf16[128,1024]{1,0:T(8,128)(2,1)S(1)}, bf16[128,1024]{1,0:T(8,128)(2,1)S(1)}, u32[]{:S(2)}, u32[]{:S(2)}) collective-permute-start(bf16[128,1024]{1,0:T(8,128)(2,1)S(1)} %filter.13), channel_id=1, source_target_pairs={{0,7},{1,6},{2,5},{3,4},{4,3},{5,2},{6,1},{7,0},{8,15},{9,14},{10,... | collective-permute-start | bytes 786440 | tf_op jit(solution)/shard_map/ppermute | solution.py:314
  29.1 14.5 %collective-permute-start.6 = (bf16[128,1024]{1,0:T(8,128)(2,1)S(1)}, bf16[128,1024]{1,0:T(8,128)(2,1)S(1)}, u32[]{:S(2)}, u32[]{:S(2)}) collective-permute-start(bf16[128,1024]{1,0:T(8,128)(2,1)S(1)} %filter.14), channel_id=1, source_target_pairs={{0,1},{1,0},{2,3},{3,2},{4,5},{5,4},{6,7},{7,6},{8,9},{9,8},{10,11... | collective-permute-start | bytes 786440 | tf_op jit(solution)/shard_map/ppermute | solution.py:314
  31.3 4.0 %copy-start.3 = (s32[1024,2]{0,1:T(2,128)S(1)}, s32[1024,2]{0,1:T(2,128)}, u32[]{:S(2)}) copy-start(s32[1024,2]{0,1:T(2,128)} %param.10) | copy-start | bytes 24580
  31.3 4.0 %copy-start.4 = (s32[512,3]{0,1:T(4,128)S(1)}, s32[512,3]{0,1:T(4,128)}, u32[]{:S(2)}) copy-start(s32[512,3]{0,1:T(4,128)} %param.11) | copy-start | bytes 18436
  31.3 13.7 %collective-permute-start.7 = (bf16[128,1024]{1,0:T(8,128)(2,1)S(1)}, bf16[128,1024]{1,0:T(8,128)(2,1)S(1)}, u32[]{:S(2)}, u32[]{:S(2)}) collective-permute-start(bf16[128,1024]{1,0:T(8,128)(2,1)S(1)} %filter.15), channel_id=1, source_target_pairs={{0,4},{1,5},{2,6},{3,7},{4,0},{5,1},{6,2},{7,3},{8,12},{9,13},{10,... | collective-permute-start | bytes 786440 | tf_op jit(solution)/shard_map/ppermute | solution.py:314
  32.8 12.2 %collective-permute-start.8 = (bf16[128,1024]{1,0:T(8,128)(2,1)S(1)}, bf16[128,1024]{1,0:T(8,128)(2,1)S(1)}, u32[]{:S(2)}, u32[]{:S(2)}) collective-permute-start(bf16[128,1024]{1,0:T(8,128)(2,1)S(1)} %filter.8._), channel_id=1, source_target_pairs={{0,2},{1,3},{2,0},{3,1},{4,6},{5,7},{6,4},{7,5},{8,10},{9,11},{10,... | collective-permute-start | bytes 786440 | tf_op jit(solution)/shard_map/ppermute | solution.py:314
  35.4 8.3 %copy-start.2 = (bf16[256,1024]{1,0:T(8,128)(2,1)S(1)}, bf16[256,1024]{1,0:T(8,128)(2,1)}, u32[]{:S(2)}) copy-start(bf16[256,1024]{1,0:T(8,128)(2,1)} %inverse_ref.3) | copy-start | bytes 1572868
